TPU v7x, 32 devices: a whole 2x2x4 slice. The times are simulated.
32 devices in a mesh: ctx: 8 (over z, y), fsdp: 4 (over x, core).
Axes of the slice: x: 2, y: 2, z: 4, core: 2. Of those that a mesh axis runs over, the one named last changes fastest.
Arguments:
- tokens: bfloat16 [4, 4096, 2048], P('fsdp', 'ctx'), may hold values from -6 to 6
- cotangent: bfloat16 [4, 4096, 2048], P('fsdp', 'ctx'), may hold values from -6 to 6
- cont_lengths: int32 [4, 3], P('fsdp'), may hold values from 1 to 1024, 2048 in all within a row
- routes: int32 [4, 4096, 8], P('fsdp', 'ctx'), may hold values from 0 to 15, all different within a row; in each aligned block of 512 rows (0 to 511, 512 to 1023, ..., all dimensions but the last counted through in order) at most 320 rows name the same one
- gates: float32 [4, 4096, 8], P('fsdp', 'ctx'), may hold values from 0.12 to 0.5
- attn_gain: bfloat16 [2048], P(('ctx', 'fsdp')), may hold values from 0.5 to 1.5
- query_gain: bfloat16 [2048], P(('ctx', 'fsdp')), may hold values from 0.5 to 1.5
- key_gain: bfloat16 [2048], P(('ctx', 'fsdp')), may hold values from 0.5 to 1.5
- ffn_gain: bfloat16 [2048], P(('ctx', 'fsdp')), may hold values from 0.5 to 1.5
- w_query: bfloat16 [2048, 2048], P(('ctx', 'fsdp')), may hold values from -0.125 to 0.125
- w_key: bfloat16 [2048, 2048], P(('ctx', 'fsdp')), may hold values from -0.125 to 0.125
- w_value: bfloat16 [2048, 2048], P(('ctx', 'fsdp')), may hold values from -0.125 to 0.125
- w_out: bfloat16 [2048, 2048], P(('ctx', 'fsdp')), may hold values from -1 to 1
- w_gate: bfloat16 [16, 2048, 1024], P('ctx', 'fsdp'), may hold values from -0.125 to 0.125
- w_up: bfloat16 [16, 2048, 1024], P('ctx', 'fsdp'), may hold values from -0.125 to 0.125
- w_down: bfloat16 [16, 1024, 2048], P('ctx', 'fsdp'), may hold values from -0.5 to 0.5
Outputs:
- output: float32 [4, 4096, 2048], P('fsdp', 'ctx')
- input_grad: float32 [4, 4096, 2048], P('fsdp', 'ctx')
- attn_gain_grad: float32 [2048], P(('ctx', 'fsdp'))
- query_gain_grad: float32 [2048], P(('ctx', 'fsdp'))
- key_gain_grad: float32 [2048], P(('ctx', 'fsdp'))
- ffn_gain_grad: float32 [2048], P(('ctx', 'fsdp'))
- w_query_grad: float32 [2048, 2048], P(('ctx', 'fsdp'))
- w_key_grad: float32 [2048, 2048], P(('ctx', 'fsdp'))
- w_value_grad: float32 [2048, 2048], P(('ctx', 'fsdp'))
- w_out_grad: float32 [2048, 2048], P(('ctx', 'fsdp'))
- w_gate_grad: float32 [16, 2048, 1024], P('ctx', 'fsdp')
- w_up_grad: float32 [16, 2048, 1024], P('ctx', 'fsdp')
- w_down_grad: float32 [16, 1024, 2048], P('ctx', 'fsdp')
Inputs may be any that keep to these rules, and one draw needn't show every extreme that they name: In each aligned block of 512 rows (the rows of one device) no expert is named by more than 320 routes, a bound that some block reaches; a token names 8 different experts. `cont_lengths`: the lengths of a group sum to 2048 and the largest is exactly 1024.
All inputs are finite; a program needn't handle non-finite values.
Results may differ from a plain program's by a relative error of at most 0.03.
Values may be sent and summed in bfloat16 or wider, within the bound.
No kernel may reach another device: no remote copies, remote signals or barrier semaphores. Data moves between devices by JAX's collectives and lax.ppermute only.
A program may use at most 512 MiB of HBM per device.

v0:
```python
from functools import partial

import jax
import jax.numpy as jnp
from jax import lax
from jax.sharding import PartitionSpec as P

HEAD = 128


EPSILON = 1e-05
ROPE_BASE = 10000.0
MASKED = -1e30


def norm_rows(values_in, gain_in):
    return (
        values_in
        * lax.rsqrt(jnp.mean(values_in * values_in, axis=-1, keepdims=True) + EPSILON)
        * gain_in
    )


def places(token_index, lengths_in, prompt_rows):
    ends = prompt_rows + jnp.cumsum(lengths_in)
    passed = (token_index[:, None] >= ends[None, :]).astype(jnp.int32)
    before = jnp.sum(passed * lengths_in[None, :], axis=1)
    inside = token_index >= prompt_rows
    segment = jnp.where(inside, 1 + jnp.sum(passed, axis=1), 0)
    position = jnp.where(inside, token_index - before, token_index)
    return (segment, position)


def rotate(values_in, positions):
    full_shape = values_in.shape
    per_head = values_in.reshape(full_shape[:-1] + (full_shape[-1] // HEAD, HEAD))
    half_dim = HEAD // 2
    frequency = ROPE_BASE ** (-jnp.arange(half_dim).astype(values_in.dtype) / half_dim)
    angles = positions.astype(values_in.dtype)[..., None] * frequency
    cosine = jnp.cos(angles)[..., None, :]
    sine = jnp.sin(angles)[..., None, :]
    former = per_head[..., :half_dim]
    latter = per_head[..., half_dim:]
    turned = jnp.concatenate(
        [former * cosine - latter * sine, latter * cosine + former * sine], axis=-1
    )
    return turned.reshape(full_shape)


def allowed_pairs(query_index, query_seg, key_index, key_seg):
    return (key_index[None, :] <= query_index[:, None]) & (
        (key_seg[None, :] == 0) | (key_seg[None, :] == query_seg[:, None])
    )


def attend_fold(
    state_in,
    shard_piece,
    first_row,
    query_heads,
    own_index,
    own_seg,
    lengths_in,
    prompt_rows,
    score_scale,
):
    highest, denominator, weighted = state_in
    key_rows, value_rows = shard_piece
    piece_count = key_rows.shape[0]
    key_index = jnp.arange(piece_count, dtype=jnp.int32)
    key_seg, _ = places(key_index, lengths_in, prompt_rows)
    key_heads = key_rows.reshape(piece_count, -1, HEAD)
    value_heads = value_rows.reshape(piece_count, -1, HEAD)
    scores = (
        jnp.einsum("qhd,khd->hqk", query_heads, key_heads, preferred_element_type=jnp.float32)
        * score_scale
    )
    allowed = allowed_pairs(own_index, own_seg, key_index, key_seg)
    masked = jnp.where(allowed[None], scores, MASKED)
    new_high = jnp.maximum(highest, jnp.max(masked, axis=-1))
    shrink = jnp.exp(highest - new_high)
    unnormed = jnp.where(allowed[None], jnp.exp(masked - new_high[..., None]), 0.0)
    denominator = jnp.sum(unnormed, axis=-1)
    weighted = jnp.einsum(
        "hqk,khd->hqd",
        unnormed.astype(jnp.bfloat16),
        value_heads,
        preferred_element_type=jnp.float32,
    )
    return (new_high, denominator, weighted)


def pair_terms(
    query_heads,
    grad_heads,
    log_rows,
    dot_rows,
    query_index,
    query_seg,
    key_heads,
    value_heads,
    key_index,
    key_seg,
    score_scale,
):
    scores = (
        jnp.einsum("qhd,khd->hqk", query_heads, key_heads, preferred_element_type=jnp.float32)
        * score_scale
    )
    allowed = allowed_pairs(query_index, query_seg, key_index, key_seg)
    prob = jnp.where(
        allowed[None], jnp.exp(jnp.where(allowed[None], scores, MASKED) - log_rows[..., None]), 0.0
    )
    prob_grad = jnp.einsum(
        "qhd,khd->hqk", grad_heads, value_heads, preferred_element_type=jnp.float32
    )
    score_grad = (prob * (prob_grad - dot_rows[..., None])).astype(jnp.bfloat16)
    return (prob, score_grad)


def slot_targets(route_list, expert_total, capacity):
    onehot = (route_list[:, None] == jnp.arange(expert_total, dtype=jnp.int32)[None, :]).astype(
        jnp.int32
    )
    slot_rank = jnp.sum((jnp.cumsum(onehot, axis=0) - 1) * onehot, axis=1)
    return route_list * capacity + slot_rank


def shards(
    tokens,
    cotangent,
    cont_lengths,
    routes,
    gates,
    attn_gain,
    query_gain,
    key_gain,
    ffn_gain,
    w_query,
    w_key,
    w_value,
    w_out,
    w_gate,
    w_up,
    w_down,
):
    row_count = tokens.shape[1]
    model_width = tokens.shape[2]
    route_count = routes.shape[2]
    context_size = lax.axis_size("ctx")
    all_rows = row_count * context_size
    prompt_rows = all_rows // 2
    local_experts = w_gate.shape[0]
    expert_total = local_experts * context_size
    capacity = max(2, row_count * route_count * 5 // (4 * expert_total))
    head_count = model_width // HEAD
    score_scale = HEAD ** (-0.5)
    lengths_in = cont_lengths[0]
    own_index = lax.axis_index("ctx") * row_count + jnp.arange(row_count, dtype=jnp.int32)
    own_seg, own_pos = places(own_index, lengths_in, prompt_rows)
    attention_set = (
        lax.all_gather(w_query, ("ctx", "fsdp"), axis=0, tiled=True),
        lax.all_gather(w_key, ("ctx", "fsdp"), axis=0, tiled=True),
        lax.all_gather(w_value, ("ctx", "fsdp"), axis=0, tiled=True),
        lax.all_gather(w_out, ("ctx", "fsdp"), axis=0, tiled=True),
        lax.all_gather(attn_gain, ("ctx", "fsdp"), axis=0, tiled=True),
        lax.all_gather(query_gain, ("ctx", "fsdp"), axis=0, tiled=True),
        lax.all_gather(key_gain, ("ctx", "fsdp"), axis=0, tiled=True),
        lax.all_gather(ffn_gain, ("ctx", "fsdp"), axis=0, tiled=True),
    )
    query_all, key_all, value_all, out_all = (
        attention_set[0],
        attention_set[1],
        attention_set[2],
        attention_set[3],
    )
    gain_attn = attention_set[4].astype(jnp.float32)
    gain_query = attention_set[5].astype(jnp.float32)
    gain_key = attention_set[6].astype(jnp.float32)
    gain_ffn = attention_set[7].astype(jnp.float32)
    expert_set = (
        lax.all_gather(w_gate, "fsdp", axis=1, tiled=True),
        lax.all_gather(w_up, "fsdp", axis=1, tiled=True),
        lax.all_gather(w_down, "fsdp", axis=1, tiled=True),
    )
    gate_all, up_all, down_all = expert_set
    inputs = tokens[0].astype(jnp.float32)
    normed, attn_pull = jax.vjp(norm_rows, inputs, gain_attn)
    hidden = normed.astype(jnp.bfloat16)
    query_pre = jnp.dot(hidden, query_all, preferred_element_type=jnp.float32)
    key_pre = jnp.dot(hidden, key_all, preferred_element_type=jnp.float32)
    values = jnp.dot(hidden, value_all, preferred_element_type=jnp.float32).astype(jnp.bfloat16)
    query_rot, query_pull = jax.vjp(
        lambda pre_in, gain_in: rotate(norm_rows(pre_in, gain_in), own_pos), query_pre, gain_query
    )
    key_rot, key_pull = jax.vjp(
        lambda pre_in, gain_in: rotate(norm_rows(pre_in, gain_in), own_pos), key_pre, gain_key
    )
    query_low = query_rot.astype(jnp.bfloat16)
    key_low = key_rot.astype(jnp.bfloat16)
    query_heads = query_low.reshape(row_count, head_count, HEAD)
    folder = partial(
        attend_fold,
        query_heads=query_heads,
        own_index=own_index,
        own_seg=own_seg,
        lengths_in=lengths_in,
        prompt_rows=prompt_rows,
        score_scale=score_scale,
    )
    start_state = (
        jnp.full((head_count, row_count), MASKED, jnp.float32),
        jnp.zeros((head_count, row_count), jnp.float32),
        jnp.zeros((head_count, row_count, HEAD), jnp.float32),
    )
    final_state = folder(
        start_state,
        (
            lax.all_gather(key_low, "ctx", axis=0, tiled=True),
            lax.all_gather(values, "ctx", axis=0, tiled=True),
        ),
        jnp.int32(0),
    )
    highest, denominator, weighted = final_state
    log_total = highest + jnp.log(denominator)
    attn_heads = jnp.transpose(weighted / denominator[..., None], (1, 0, 2))
    attended = attn_heads.reshape(row_count, model_width).astype(jnp.bfloat16)
    mixed = inputs + jnp.dot(attended, out_all, preferred_element_type=jnp.float32)
    normed_second, ffn_pull = jax.vjp(norm_rows, mixed, gain_ffn)
    second = normed_second.astype(jnp.bfloat16)
    route_list = routes[0].reshape(-1)
    targets = slot_targets(route_list, expert_total, capacity)

    def dispatch_rows(route_rows):
        buffer = (
            jnp.zeros((expert_total * capacity, model_width), jnp.bfloat16)
            .at[targets]
            .set(route_rows)
        )
        return buffer.reshape(context_size, local_experts * capacity, model_width)

    sent_rows = dispatch_rows(jnp.repeat(second, route_count, axis=0))
    arrived = lax.all_to_all(sent_rows, "ctx", split_axis=0, concat_axis=0, tiled=True).reshape(
        context_size, local_experts, capacity, model_width
    )
    gate_pre = jnp.einsum("sekd,edf->sekf", arrived, gate_all, preferred_element_type=jnp.float32)
    up_pre = jnp.einsum("sekd,edf->sekf", arrived, up_all, preferred_element_type=jnp.float32)
    active = (jax.nn.silu(gate_pre) * up_pre).astype(jnp.bfloat16)
    expert_out = jnp.einsum(
        "sekf,efd->sekd", active, down_all, preferred_element_type=jnp.float32
    ).astype(jnp.bfloat16)
    returned = lax.all_to_all(
        expert_out.reshape(context_size, local_experts * capacity, model_width),
        "ctx",
        split_axis=0,
        concat_axis=0,
        tiled=True,
    )
    per_route = (
        returned.reshape(expert_total * capacity, model_width)[targets]
        .astype(jnp.float32)
        .reshape(row_count, route_count, model_width)
    )
    gate_values = gates[0]
    result = mixed + jnp.sum(gate_values[..., None] * per_route, axis=1)
    output = result[None]
    upstream = cotangent[0].astype(jnp.float32)
    route_grad = (
        (gate_values[..., None] * upstream[:, None, :])
        .astype(jnp.bfloat16)
        .reshape(row_count * route_count, model_width)
    )
    grad_arrived = lax.all_to_all(
        dispatch_rows(route_grad), "ctx", split_axis=0, concat_axis=0, tiled=True
    ).reshape(context_size, local_experts, capacity, model_width)
    active_grad = jnp.einsum(
        "sekd,efd->sekf", grad_arrived, down_all, preferred_element_type=jnp.float32
    )
    down_w_grad = jnp.einsum(
        "sekf,sekd->efd", active, grad_arrived, preferred_element_type=jnp.float32
    )
    sigmoid_gate = jax.nn.sigmoid(gate_pre)
    gate_grad = (
        active_grad * up_pre * sigmoid_gate * (1.0 + gate_pre * (1.0 - sigmoid_gate))
    ).astype(jnp.bfloat16)
    up_grad = (active_grad * gate_pre * sigmoid_gate).astype(jnp.bfloat16)
    gate_w_grad = jnp.einsum(
        "sekd,sekf->edf", arrived, gate_grad, preferred_element_type=jnp.float32
    )
    up_w_grad = jnp.einsum("sekd,sekf->edf", arrived, up_grad, preferred_element_type=jnp.float32)
    arrived_grad = jnp.einsum(
        "sekf,edf->sekd", gate_grad, gate_all, preferred_element_type=jnp.float32
    )
    arrived_grad = (
        arrived_grad
        + jnp.einsum("sekf,edf->sekd", up_grad, up_all, preferred_element_type=jnp.float32)
    ).astype(jnp.bfloat16)
    grad_back = lax.all_to_all(
        arrived_grad.reshape(context_size, local_experts * capacity, model_width),
        "ctx",
        split_axis=0,
        concat_axis=0,
        tiled=True,
    )
    second_grad = jnp.sum(
        grad_back.reshape(expert_total * capacity, model_width)[targets]
        .astype(jnp.float32)
        .reshape(row_count, route_count, model_width),
        axis=1,
    )
    expert_grads = (
        lax.psum_scatter(
            gate_w_grad.astype(jnp.bfloat16), "fsdp", scatter_dimension=1, tiled=True
        ).astype(jnp.float32),
        lax.psum_scatter(
            up_w_grad.astype(jnp.bfloat16), "fsdp", scatter_dimension=1, tiled=True
        ).astype(jnp.float32),
        lax.psum_scatter(
            down_w_grad.astype(jnp.bfloat16), "fsdp", scatter_dimension=1, tiled=True
        ).astype(jnp.float32),
    )
    mixed_norm_grad, ffn_gain_grad = ffn_pull(second_grad)
    mixed_grad = upstream + mixed_norm_grad
    branch_grad = mixed_grad.astype(jnp.bfloat16)
    out_w_grad = jnp.dot(attended.T, branch_grad, preferred_element_type=jnp.float32)
    attended_grad = jnp.dot(branch_grad, out_all.T, preferred_element_type=jnp.float32).astype(
        jnp.bfloat16
    )
    grad_heads = attended_grad.reshape(row_count, head_count, HEAD)
    row_dot = jnp.transpose(jnp.sum(grad_heads.astype(jnp.float32) * attn_heads, axis=-1))
    keys_whole, values_whole = (
        lax.all_gather(key_low, "ctx", axis=0, tiled=True),
        lax.all_gather(values, "ctx", axis=0, tiled=True),
    )
    block_rows = min(1024, all_rows)
    block_count = all_rows // block_rows
    block_index = jnp.arange(all_rows, dtype=jnp.int32).reshape(block_count, block_rows)
    key_blocks = keys_whole.reshape(block_count, block_rows, model_width)
    value_blocks = values_whole.reshape(block_count, block_rows, model_width)

    def query_side(key_rows, value_rows, key_index):
        key_seg, _ = places(key_index, lengths_in, prompt_rows)
        key_heads = key_rows.reshape(block_rows, head_count, HEAD)
        value_heads = value_rows.reshape(block_rows, head_count, HEAD)
        prob, score_grad = pair_terms(
            query_heads,
            grad_heads,
            log_total,
            row_dot,
            own_index,
            own_seg,
            key_heads,
            value_heads,
            key_index,
            key_seg,
            score_scale,
        )
        query_term = (
            jnp.einsum("hqk,khd->qhd", score_grad, key_heads, preferred_element_type=jnp.float32)
            * score_scale
        )
        return (prob, score_grad, query_term)

    def back_block(query_grad, block_args):
        key_rows, value_rows, key_index = block_args
        prob, score_grad, query_term = query_side(key_rows, value_rows, key_index)
        key_term = (
            jnp.einsum("hqk,qhd->khd", score_grad, query_heads, preferred_element_type=jnp.float32)
            * score_scale
        )
        value_term = jnp.einsum(
            "hqk,qhd->khd",
            prob.astype(jnp.bfloat16),
            grad_heads,
            preferred_element_type=jnp.float32,
        )
        return (
            query_grad + query_term,
            (
                key_term.reshape(block_rows, model_width),
                value_term.reshape(block_rows, model_width),
            ),
        )

    query_grad, (key_terms, value_terms) = lax.scan(
        back_block,
        jnp.zeros((row_count, head_count, HEAD), jnp.float32),
        (key_blocks, value_blocks, block_index),
    )
    key_grad, value_grad = (
        lax.psum_scatter(
            key_terms.reshape(all_rows, model_width).astype(jnp.bfloat16),
            "ctx",
            scatter_dimension=0,
            tiled=True,
        ).astype(jnp.float32),
        lax.psum_scatter(
            value_terms.reshape(all_rows, model_width).astype(jnp.bfloat16),
            "ctx",
            scatter_dimension=0,
            tiled=True,
        ).astype(jnp.float32),
    )
    query_pre_grad, query_gain_grad = query_pull(query_grad.reshape(row_count, model_width))
    key_pre_grad, key_gain_grad = key_pull(key_grad)
    query_low_grad = query_pre_grad.astype(jnp.bfloat16)
    key_low_grad = key_pre_grad.astype(jnp.bfloat16)
    value_low_grad = value_grad.astype(jnp.bfloat16)
    query_w_grad = jnp.dot(hidden.T, query_low_grad, preferred_element_type=jnp.float32)
    key_w_grad = jnp.dot(hidden.T, key_low_grad, preferred_element_type=jnp.float32)
    value_w_grad = jnp.dot(hidden.T, value_low_grad, preferred_element_type=jnp.float32)
    hidden_grad = jnp.dot(query_low_grad, query_all.T, preferred_element_type=jnp.float32)
    hidden_grad = hidden_grad + jnp.dot(key_low_grad, key_all.T, preferred_element_type=jnp.float32)
    hidden_grad = hidden_grad + jnp.dot(
        value_low_grad, value_all.T, preferred_element_type=jnp.float32
    )
    input_norm_grad, attn_gain_grad = attn_pull(hidden_grad)
    input_grad = (mixed_grad + input_norm_grad)[None]
    summed_grads = (
        lax.psum_scatter(query_w_grad, ("ctx", "fsdp"), scatter_dimension=0, tiled=True),
        lax.psum_scatter(key_w_grad, ("ctx", "fsdp"), scatter_dimension=0, tiled=True),
        lax.psum_scatter(value_w_grad, ("ctx", "fsdp"), scatter_dimension=0, tiled=True),
        lax.psum_scatter(out_w_grad, ("ctx", "fsdp"), scatter_dimension=0, tiled=True),
        lax.psum_scatter(attn_gain_grad, ("ctx", "fsdp"), scatter_dimension=0, tiled=True),
        lax.psum_scatter(query_gain_grad, ("ctx", "fsdp"), scatter_dimension=0, tiled=True),
        lax.psum_scatter(key_gain_grad, ("ctx", "fsdp"), scatter_dimension=0, tiled=True),
        lax.psum_scatter(ffn_gain_grad, ("ctx", "fsdp"), scatter_dimension=0, tiled=True),
    )
    return (
        output,
        input_grad,
        summed_grads[4],
        summed_grads[5],
        summed_grads[6],
        summed_grads[7],
        summed_grads[0],
        summed_grads[1],
        summed_grads[2],
        summed_grads[3],
        expert_grads[0],
        expert_grads[1],
        expert_grads[2],
    )


def solution(mesh):
    placed = (
        P("fsdp", "ctx", None),
        P("fsdp", "ctx", None),
        P("fsdp", None),
        P("fsdp", "ctx", None),
        P("fsdp", "ctx", None),
        P(("ctx", "fsdp")),
        P(("ctx", "fsdp")),
        P(("ctx", "fsdp")),
        P(("ctx", "fsdp")),
        P(("ctx", "fsdp"), None),
        P(("ctx", "fsdp"), None),
        P(("ctx", "fsdp"), None),
        P(("ctx", "fsdp"), None),
        P("ctx", "fsdp", None),
        P("ctx", "fsdp", None),
        P("ctx", "fsdp", None),
    )
    return jax.shard_map(
        shards,
        mesh=mesh,
        in_specs=placed,
        out_specs=(
            P("fsdp", "ctx", None),
            P("fsdp", "ctx", None),
            P(("ctx", "fsdp")),
            P(("ctx", "fsdp")),
            P(("ctx", "fsdp")),
            P(("ctx", "fsdp")),
            P(("ctx", "fsdp"), None),
            P(("ctx", "fsdp"), None),
            P(("ctx", "fsdp"), None),
            P(("ctx", "fsdp"), None),
            P("ctx", "fsdp", None),
            P("ctx", "fsdp", None),
            P("ctx", "fsdp", None),
        ),
        check_vma=False,
    )
```

profile of v0, /device:TPU:14, one launch (start us, length us, event | category | flops | bytes accessed | tf_op | source)
XLA Modules:
  0.0 4924.8 jit_solution(5665496464390297024)
XLA Ops:
  13.7 40.7 all-reduce.13
  59.2 30.5 all-gather.12.cloned.1.call-done
  102.9 65.8 %all-gather.10.cloned.1.call-done = bf16[2048,2048]{1,0:T(8,128)(2,1)} async-done(((bf16[64,2048]{1,0:T(8,128)(2,1)}), bf16[2048,2048]{1,0:T(8,128)(2,1)}) %all-gather.10.cloned.1.call-update) | async-done | bytes 8388624 | tf_op jit(solution)/shard_map/all_gather | solution.py:162
  196.5 51.1 %all-gather.16.cloned.1.call-done = bf16[2048,2048]{1,0:T(8,128)(2,1)} async-done(((bf16[64,2048]{1,0:T(8,128)(2,1)}), bf16[2048,2048]{1,0:T(8,128)(2,1)}) %all-gather.16.cloned.1.call-update) | async-done | bytes 8388624 | tf_op jit(solution)/shard_map/all_gather | solution.py:164
  273.5 201.1 %all-gather.14.cloned.1.call-done = bf16[4096,2048]{0,1:T(8,128)(2,1)} async-done(((bf16[512,2048]{0,1:T(8,128)(2,1)}), bf16[4096,2048]{0,1:T(8,128)(2,1)}) %all-gather.14.cloned.1.call-update) | async-done | bytes 16777232 | tf_op jit(solution)/shard_map/all_gather | solution.py:219
  474.6 57.6 %fusion.13 = (f32[16,512]{1,0:T(8,128)S(1)}, f32[16,512,4096]{2,1,0:T(8,128)}) fusion(pred[512,4096]{1,0:T(8,128)(4,1)S(1)} %fusion.57, bf16[512,16,128]{2,0,1:T(8,128)(2,1)} %pad_maximum_fusion, bf16[4096,16,128]{0,2,1:T(8,128)(2,1)} %bitcast.314), kind=kOutput, calls=%fused_computation.33 | convolution fusion | flops 8690589696 | bytes 155222016 | tf_op jit(solution)/shard_map/qhd,khd->hqk/dot_general | solution.py:75
  532.2 170.8 %all-gather.18.cloned.1.call-done = bf16[4096,2048]{1,0:T(8,128)(2,1)} async-done(((bf16[512,2048]{1,0:T(8,128)(2,1)}), bf16[4096,2048]{1,0:T(8,128)(2,1)}) %all-gather.18.cloned.1.call-update) | async-done | bytes 16777232 | tf_op jit(solution)/shard_map/all_gather | solution.py:220
  703.0 20.8 copy.179
  723.7 46.2 fusion.14
  769.9 54.5 %fusion.109 = (bf16[512,16,128]{0,2,1:T(8,128)(2,1)}, f32[512,16,128]{0,2,1:T(8,128)}) fusion(f32[512,16]{0,1:T(8,128)S(1)} %bitcast.329, bf16[4096,16,128]{0,2,1:T(8,128)(2,1)} %bitcast.320, f32[16,512,4096]{2,1,0:T(8,128)} %get-tuple-element.362, f32[16,512]{1,0:T(8,128)S(1)} %broadcast_maximum_fusion, pred[512,4096]{1,0:T(8,128)(4,1)S(1)} %fusion.57), kind=kOutput, calls=%fused_computation.205 | convolution fusion | flops 8759803904 | bytes 159449088 | tf_op jit(solution)/shard_map/hqk,khd->hqd/dot_general | solution.py:84
  836.7 35.2 scatter_custom_fusion
  890.5 36.3 scatter_custom_fusion.1
  926.8 403.7 %all-to-all-done = bf16[8,640,2048]{2,1,0:T(8,128)(2,1)} async-done(((bf16[8,640,2048]{2,1,0:T(8,128)(2,1)}), bf16[8,640,2048]{2,1,0:T(8,128)(2,1)}, u32[]{:S(2)}, u32[]{:S(2)}) %all-to-all-start) | async-done | bytes 20971552 | tf_op jit(solution)/shard_map/all_to_all | solution.py:243
  1341.1 29.2 fusion.38
  1370.3 29.7 all-gather.24.cloned.1.call-done
  1400.0 29.2 fusion.36
  1429.2 30.4 all-gather.26.cloned.1.call-done
  1459.6 328.8 %all-to-all-done.2 = bf16[8,640,2048]{2,1,0:T(8,128)(2,1)} async-done(((bf16[8,640,2048]{2,1,0:T(8,128)(2,1)}), bf16[8,640,2048]{2,1,0:T(8,128)(2,1)}, u32[]{:S(2)}, u32[]{:S(2)}) %all-to-all-start.2) | async-done | bytes 20971552 | tf_op jit(solution)/shard_map/all_to_all | solution.py:273
  1788.4 43.5 fusion.26
  1831.9 30.8 fusion.51
  1862.8 35.4 fusion.21
  1898.2 17.6 copy.150
  1925.2 28.9 convert_bitcast_fusion
  1954.1 17.7 copy.147
  1971.8 401.0 %all-to-all-done.3 = bf16[8,640,2048]{2,1,0:T(8,128)(2,1)} async-done(((bf16[8,640,2048]{2,1,0:T(8,128)(2,1)}), bf16[8,640,2048]{2,1,0:T(8,128)(2,1)}, u32[]{:S(2)}, u32[]{:S(2)}) %all-to-all-start.3) | async-done | bytes 20971552 | tf_op jit(solution)/shard_map/all_to_all | solution.py:298
  2399.7 41.0 gather_fusion.1
  2456.4 374.2 %all-to-all-done.1 = bf16[8,640,2048]{2,1,0:T(8,128)(2,1)} async-done(((bf16[8,640,2048]{2,1,0:T(8,128)(2,1)}), bf16[8,640,2048]{2,1,0:T(8,128)(2,1)}, u32[]{:S(2)}, u32[]{:S(2)}) %all-to-all-start.1) | async-done | bytes 20971552 | tf_op jit(solution)/shard_map/all_to_all | solution.py:252
  2830.6 41.0 gather_fusion
  2906.6 465.0 %while.17 = (s32[]{:T(128)}, f32[512,16,128]{0,2,1:T(8,128)}, bf16[4,1024,2048]{2,1,0:T(8,128)(2,1)}, bf16[4,1024,2048]{2,1,0:T(8,128)(2,1)}, bf16[4,1024,2048]{...) while((s32[]{:T(128)}, f32[512,16,128]{0,2,1:T(8,128)}, ...), condition=%wide.region_22.23_spmd.clone, body=%wide.region_20.22_spmd.clone.sunk | while | flops 10847531008 | bytes 257577232 | solution.py:385
  2939.3 22.5 fusion.172
  3054.6 22.5 fusion.172
  3090.1 16.8 fusion.173
  3171.0 22.5 fusion.172
  3206.5 16.8 fusion.173
  3287.4 22.5 fusion.172
  3372.5 29.4 bitcast_convert_fusion.2
  3401.9 29.5 bitcast_convert_fusion.1
  3431.5 28.3 bitcast_convert_fusion
  3477.5 178.6 %reduce-scatter.10.cloned.1.call-done = bf16[512,2048]{1,0:T(8,128)(2,1)} async-done(((bf16[4096,2048]{1,0:T(8,128)(2,1)}), bf16[512,2048]{1,0:T(8,128)(2,1)}) %reduce-scatter.10.cloned.1.call-update) | async-done | bytes 2097168 | tf_op jit(solution)/shard_map/reduce_scatter | solution.py:391
  3715.8 226.4 %reduce-scatter.12.cloned.1.call-done = bf16[512,2048]{1,0:T(8,128)(2,1)} async-done(((bf16[4096,2048]{1,0:T(8,128)(2,1)}), bf16[512,2048]{1,0:T(8,128)(2,1)}) %reduce-scatter.12.cloned.1.call-update) | async-done | bytes 2097168 | tf_op jit(solution)/shard_map/reduce_scatter | solution.py:397
  3952.5 63.7 %reduce-scatter.22.cloned.1.call-done = bf16[2,512,1024]{2,1,0:T(8,128)(2,1)} async-done(((bf16[2,2048,1024]{2,1,0:T(8,128)(2,1)}), bf16[2,512,1024]{2,1,0:T(8,128)(2,1)}) %reduce-scatter.22.cloned.1.call-update) | async-done | bytes 2097168 | tf_op jit(solution)/shard_map/reduce_scatter | solution.py:312
  4020.2 70.3 %reduce-scatter.24.cloned.1.call-done = bf16[2,512,1024]{2,1,0:T(8,128)(2,1)} async-done(((bf16[2,2048,1024]{2,1,0:T(8,128)(2,1)}), bf16[2,512,1024]{2,1,0:T(8,128)(2,1)}) %reduce-scatter.24.cloned.1.call-update) | async-done | bytes 2097168 | tf_op jit(solution)/shard_map/reduce_scatter | solution.py:315
  4094.6 70.3 %reduce-scatter.26.cloned.1.call-done = bf16[2,256,2048]{2,1,0:T(8,128)(2,1)} async-done(((bf16[2,1024,2048]{2,1,0:T(8,128)(2,1)}), bf16[2,256,2048]{2,1,0:T(8,128)(2,1)}) %reduce-scatter.26.cloned.1.call-update) | async-done | bytes 2097168 | tf_op jit(solution)/shard_map/reduce_scatter | solution.py:318
  4193.8 45.5 all-reduce.12
  4248.3 106.7 %reduce-scatter.20.cloned.1.call-done = f32[64,2048]{1,0:T(8,128)} async-done(((f32[2048,2048]{1,0:T(8,128)}), f32[64,2048]{1,0:T(8,128)}) %reduce-scatter.20.cloned.1.call-update) | async-done | bytes 524304 | tf_op jit(solution)/shard_map/reduce_scatter | solution.py:423
  4355.0 187.5 %reduce-scatter.14.cloned.1.call-done = f32[64,2048]{1,0:T(8,128)} async-done(((f32[2048,2048]{1,0:T(8,128)}), f32[64,2048]{1,0:T(8,128)}) %reduce-scatter.14.cloned.1.call-update) | async-done | bytes 524304 | tf_op jit(solution)/shard_map/reduce_scatter | solution.py:420
  4542.5 187.4 %reduce-scatter.16.cloned.1.call-done = f32[64,2048]{1,0:T(8,128)} async-done(((f32[2048,2048]{1,0:T(8,128)}), f32[64,2048]{1,0:T(8,128)}) %reduce-scatter.16.cloned.1.call-update) | async-done | bytes 524304 | tf_op jit(solution)/shard_map/reduce_scatter | solution.py:421
  4729.9 187.3 %reduce-scatter.18.cloned.1.call-done = f32[64,2048]{1,0:T(8,128)} async-done(((f32[2048,2048]{1,0:T(8,128)}), f32[64,2048]{1,0:T(8,128)}) %reduce-scatter.18.cloned.1.call-update) | async-done | bytes 524304 | tf_op jit(solution)/shard_map/reduce_scatter | solution.py:422
  (359 shorter events, 679.9 us)
Async XLA Ops:
  8.0 81.7 %all-gather.12.cloned.1.call-start = ((), (), s32[]{:S(2)}) async-start(), calls=%async_computation.14 | async-start | bytes 8650752 | tf_op jit(solution)/shard_map/all_gather | solution.py:163
  8.7 159.9 %all-gather.10.cloned.1.call-start = ((), (), s32[]{:S(2)}) async-start(), calls=%async_computation.13 | async-start | bytes 8650752 | tf_op jit(solution)/shard_map/all_gather | solution.py:162
  9.5 238.1 %all-gather.16.cloned.1.call-start = ((), (), s32[]{:S(2)}) async-start(), calls=%async_computation.16 | async-start | bytes 8650752 | tf_op jit(solution)/shard_map/all_gather | solution.py:164
  10.2 464.4 %all-gather.14.cloned.1.call-start = ((), (), s32[]{:S(2)}) async-start(), calls=%async_computation.15 | async-start | bytes 18874368 | tf_op jit(solution)/shard_map/all_gather | solution.py:219
  54.4 193.2 %copy-start.42 = (f32[2048]{0:T(1024)}, f32[2048]{0:T(1024)S(1)}, u32[]{:S(2)}) copy-start(f32[2048]{0:T(1024)S(1)} %convert_element_type.185) | copy-start | bytes 24580
  54.4 43.2 copy-start.30
  54.5 121.9 %copy-start.32 = (f32[2048]{0:T(1024)}, f32[2048]{0:T(1024)S(1)}, u32[]{:S(2)}) copy-start(f32[2048]{0:T(1024)S(1)} %convert_element_type.187) | copy-start | bytes 24580
  58.1 39.4 copy-start.51
  58.2 189.5 %copy-start.59 = (f32[512]{0:T(512)}, f32[512]{0:T(512)S(1)}, u32[]{:S(2)}) copy-start(f32[512]{0:T(512)S(1)} %fusion.88) | copy-start | bytes 6148
  59.2 125.0 %copy-start.18 = (f32[512,64]{1,0:T(8,128)}, f32[512,64]{1,0:T(8,128)S(1)}, u32[]{:S(2)}) copy-start(f32[512,64]{1,0:T(8,128)S(1)} %get-tuple-element.355) | copy-start | bytes 393220
  59.2 125.0 %copy-start.20 = (f32[512,64]{1,0:T(8,128)}, f32[512,64]{1,0:T(8,128)S(1)}, u32[]{:S(2)}) copy-start(f32[512,64]{1,0:T(8,128)S(1)} %get-tuple-element.356) | copy-start | bytes 393220
  99.9 68.8 %copy-start.16 = (bf16[1,512,2048]{2,1,0:T(8,128)(2,1)S(1)}, bf16[1,512,2048]{2,1,0:T(8,128)(2,1)}, u32[]{:S(2)}) copy-start(bf16[1,512,2048]{2,1,0:T(8,128)(2,1)} %param.18) | copy-start | bytes 6291460
  196.5 61.8 %copy-start.40 = (s32[1,512,8]{1,2,0:T(8,128)S(1)}, s32[1,512,8]{1,2,0:T(8,128)}, u32[]{:S(2)}) copy-start(s32[1,512,8]{1,2,0:T(8,128)} %param.21) | copy-start | bytes 49156
  196.5 506.5 %all-gather.18.cloned.1.call-start = ((), (), s32[]{:S(2)}) async-start(), calls=%async_computation.17 | async-start | bytes 18874368 | tf_op jit(solution)/shard_map/all_gather | solution.py:220
  257.5 566.9 %all-gather.20.cloned.1.call-start = ((), (), s32[]{:S(2)}) async-start(), calls=%async_computation.18 | async-start | bytes 8650752 | tf_op jit(solution)/shard_map/all_gather | solution.py:165
  258.7 14.8 copy-start.36
  532.2 191.6 %copy-start.26 = (f32[16,512]{1,0:T(8,128)}, f32[16,512]{1,0:T(8,128)S(1)}, u32[]{:S(2)}) copy-start(f32[16,512]{1,0:T(8,128)S(1)} %get-tuple-element.361) | copy-start | bytes 98308
  769.9 54.5 %copy-start.34 = (f32[16,512]{1,0:T(8,128)}, f32[16,512]{1,0:T(8,128)S(1)}, u32[]{:S(2)}) copy-start(f32[16,512]{1,0:T(8,128)S(1)} %fusion.14) | copy-start | bytes 98308
  824.5 11.8 copy-start.28
  871.9 458.6 %all-to-all-start = ((bf16[8,640,2048]{2,1,0:T(8,128)(2,1)}), bf16[8,640,2048]{2,1,0:T(8,128)(2,1)}, u32[]{:S(2)}, u32[]{:S(2)}) async-start(bf16[8,640,2048]{2,1,0:T(8,128)(2,1)} %bitcast.312), calls=%async_computation | async-start | bytes 41943040 | tf_op jit(solution)/shard_map/all_to_all | solution.py:243
  881.1 459.9 %all-gather.22.cloned.1.call-start = ((), (), s32[]{:S(2)}) async-start(), calls=%async_computation.19 | async-start | bytes 10485760 | tf_op jit(solution)/shard_map/all_gather | solution.py:182
  1330.5 457.9 %all-to-all-start.2 = ((bf16[8,640,2048]{2,1,0:T(8,128)(2,1)}), bf16[8,640,2048]{2,1,0:T(8,128)(2,1)}, u32[]{:S(2)}, u32[]{:S(2)}) async-start(bf16[8,640,2048]{2,1,0:T(8,128)(2,1)} %bitcast.310), calls=%async_computation.2 | async-start | bytes 41943040 | tf_op jit(solution)/shard_map/all_to_all | solution.py:273
  1339.9 60.2 %all-gather.24.cloned.1.call-start = ((), (), s32[]{:S(2)}) async-start(), calls=%async_computation.20 | async-start | bytes 10485760 | tf_op jit(solution)/shard_map/all_gather | solution.py:183
  1340.5 119.2 %all-gather.26.cloned.1.call-start = ((), (), s32[]{:S(2)}) async-start(), calls=%async_computation.21 | async-start | bytes 10485760 | tf_op jit(solution)/shard_map/all_gather | solution.py:184
  1915.8 457.0 %all-to-all-start.3 = ((bf16[8,640,2048]{2,1,0:T(8,128)(2,1)}), bf16[8,640,2048]{2,1,0:T(8,128)(2,1)}, u32[]{:S(2)}, u32[]{:S(2)}) async-start(bf16[8,640,2048]{2,1,0:T(8,128)(2,1)} %bitcast.313), calls=%async_computation.3 | async-start | bytes 41943040 | tf_op jit(solution)/shard_map/all_to_all | solution.py:298
  2372.9 457.7 %all-to-all-start.1 = ((bf16[8,640,2048]{2,1,0:T(8,128)(2,1)}), bf16[8,640,2048]{2,1,0:T(8,128)(2,1)}, u32[]{:S(2)}, u32[]{:S(2)}) async-start(bf16[8,640,2048]{2,1,0:T(8,128)(2,1)} %bitcast.311), calls=%async_computation.1 | async-start | bytes 41943040 | tf_op jit(solution)/shard_map/all_to_all | solution.py:252
  2382.4 1273.7 %reduce-scatter.10.cloned.1.call-start = ((), (), s32[]{:S(2)}) async-start(), calls=%async_computation.22 | async-start | bytes 18874368 | tf_op jit(solution)/shard_map/reduce_scatter | solution.py:391
  2385.8 13.9 copy-start.27
  2385.8 13.9 copy-start.35
  2440.7 13.6 copy-start.5
  2440.7 13.6 copy-start.29
  2440.7 13.6 copy-start.46
  2871.6 16.7 copy-start.6
  2871.6 16.7 copy-start.8
  2871.6 16.7 copy-start.14
  2871.6 21.7 slice-start.2
  3077.1 13.0 copy-start.15
  3193.5 13.0 copy-start.15
  3309.9 13.0 copy-start.15
  3371.7 570.4 %reduce-scatter.12.cloned.1.call-start = ((), (), s32[]{:S(2)}) async-start(), calls=%async_computation.23 | async-start | bytes 18874368 | tf_op jit(solution)/shard_map/reduce_scatter | solution.py:397
  3372.4 643.7 %reduce-scatter.22.cloned.1.call-start = ((), (), s32[]{:S(2)}) async-start(), calls=%async_computation.28 | async-start | bytes 10485760 | tf_op jit(solution)/shard_map/reduce_scatter | solution.py:312
  3401.9 688.6 %reduce-scatter.24.cloned.1.call-start = ((), (), s32[]{:S(2)}) async-start(), calls=%async_computation.29 | async-start | bytes 10485760 | tf_op jit(solution)/shard_map/reduce_scatter | solution.py:315
  3431.5 733.4 %reduce-scatter.26.cloned.1.call-start = ((), (), s32[]{:S(2)}) async-start(), calls=%async_computation.30 | async-start | bytes 10485760 | tf_op jit(solution)/shard_map/reduce_scatter | solution.py:318
  3459.8 895.2 %reduce-scatter.20.cloned.1.call-start = ((), (), s32[]{:S(2)}) async-start(), calls=%async_computation.27 | async-start | bytes 17301504 | tf_op jit(solution)/shard_map/reduce_scatter | solution.py:423
  3471.8 1070.7 %reduce-scatter.14.cloned.1.call-start = ((), (), s32[]{:S(2)}) async-start(), calls=%async_computation.24 | async-start | bytes 17301504 | tf_op jit(solution)/shard_map/reduce_scatter | solution.py:420
  3694.6 1035.3 %reduce-scatter.16.cloned.1.call-start = ((), (), s32[]{:S(2)}) async-start(), calls=%async_computation.25 | async-start | bytes 17301504 | tf_op jit(solution)/shard_map/reduce_scatter | solution.py:421
  3715.7 1201.5 %reduce-scatter.18.cloned.1.call-start = ((), (), s32[]{:S(2)}) async-start(), calls=%async_computation.26 | async-start | bytes 17301504 | tf_op jit(solution)/shard_map/reduce_scatter | solution.py:422
  4182.5 59.2 %copy-start.52 = (f32[512]{0:T(512)S(1)}, f32[512]{0:T(512)}, u32[]{:S(2)}) copy-start(f32[512]{0:T(512)} %copy-done.51) | copy-start | bytes 6148
  (45 other events, 222.7 us)
Sparse Core Ops, SparseCore 0:
  11.7 77.9 all-gather.11
  92.6 76.0 all-gather.9
  171.5 76.0 all-gather.15
  250.1 224.4 all-gather.13
  477.1 225.7 all-gather.17
  705.7 77.5 all-gather.19
  3371.8 284.2 reduce-scatter.9
  3660.3 281.7 reduce-scatter.11
  3944.7 71.4 reduce-scatter.21
  4018.8 71.7 reduce-scatter.23
  4093.1 71.7 reduce-scatter.25
  4167.7 187.2 reduce-scatter.19
  4358.0 184.4 reduce-scatter.13
  4545.3 184.4 reduce-scatter.15
  4732.7 184.4 reduce-scatter.17
Sparse Core Ops, SparseCore 1:
  883.1 58.1 all-gather.21
  1341.9 58.1 all-gather.23
  1401.5 58.1 all-gather.25
where the time goes:
time: 4940 us; the launch traced here: 4920 us
  waiting for transfers between devices  3370 us (68%)
  matrix products  810 us (16%)
  local copies, waits for them, and re-layouts  434 us (9%)
  other arithmetic  168 us (3%)
  blocking collectives  86.2 us (2%)
    all_to_all x1, waiting for transfers between devices, shards(): lax.all_to_all(sent_rows, 'ctx', split_axis=0, concat_axis=0, tiled=True)  404 us
    all_to_all x1, waiting for transfers between devices, shards(): lax.all_to_all(arrived_grad.reshape(context_size, local_experts * capacit...  401 us
    all_to_all x1, waiting for transfers between devices, shards(): lax.all_to_all(expert_out.reshape(context_size, local_experts * capacity,...  374 us
    all_to_all x1, waiting for transfers between devices, shards(): lax.all_to_all(dispatch_rows(route_grad), 'ctx', split_axis=0, concat_axi...  329 us
    reduce_scatter x1, waiting for transfers between devices, shards(): lax.psum_scatter(value_terms.reshape(all_rows, model_width).astype(jnp.bf...  226 us
    all_gather x1, waiting for transfers between devices, shards(): lax.all_gather(key_low, 'ctx', axis=0, tiled=True)  201 us
    reduce_scatter x1, waiting for transfers between devices, shards(): lax.psum_scatter(query_w_grad, ('ctx', 'fsdp'), scatter_dimension=0, tile...  187 us
    reduce_scatter x1, waiting for transfers between devices, shards(): lax.psum_scatter(key_w_grad, ('ctx', 'fsdp'), scatter_dimension=0, tiled=...  187 us
  transfers between devices with their start and end apart: 22, of which 20 were waited for; matrix products, arithmetic and copies ran while one was open for 14% of the time, Pallas kernels for 0%

commit v1 on v0

--- a/solution.py
+++ b/solution.py
@@ -3,6 +3,8 @@
 import jax
 import jax.numpy as jnp
 from jax import lax
+from jax.experimental import pallas as pl
+from jax.experimental.pallas import tpu as pltpu
 from jax.sharding import PartitionSpec as P
 
 HEAD = 128
@@ -126,7 +128,7 @@
     return route_list * capacity + slot_rank
 
 
-def shards(
+def shards_wide(
     tokens,
     cotangent,
     cont_lengths,
@@ -443,7 +445,1267 @@
     )
 
 
+HEADS = 16
+LOG2E = 1.4426950408889634
+VMEM_BYTES = 60 * 2**20
+
+
+def dot_nn(left, right):
+    return lax.dot_general(
+        left, right, (((1,), (0,)), ((), ())), preferred_element_type=jnp.float32
+    )
+
+
+def dot_nt(left, right):
+    return lax.dot_general(
+        left, right, (((1,), (1,)), ((), ())), preferred_element_type=jnp.float32
+    )
+
+
+def dot_tn(left, right):
+    return lax.dot_general(
+        left, right, (((0,), (0,)), ((), ())), preferred_element_type=jnp.float32
+    )
+
+
+def segment_start(starts, index):
+    first = starts[0]
+    for c in range(1, starts.shape[0]):
+        first = jnp.where(index >= starts[c], starts[c], first)
+    return first
+
+
+def segment_end(starts, index, total):
+    last = jnp.int32(total)
+    for c in range(starts.shape[0] - 1, 0, -1):
+        last = jnp.where(index < starts[c], starts[c], last)
+    return last
+
+
+def allowed_tile(starts, key_first, query_first, size, prompt_rows):
+    key_index = key_first + lax.broadcasted_iota(jnp.int32, (size, size), 0)
+    query_index = query_first + lax.broadcasted_iota(jnp.int32, (1, size), 1)
+    own_start = jnp.full((1, size), prompt_rows, jnp.int32)
+    for c in range(1, starts.shape[0]):
+        own_start = jnp.where(query_index >= starts[c], starts[c], own_start)
+    return (key_index <= query_index) & ((key_index < prompt_rows) | (key_index >= own_start))
+
+
+def attend_forward_kernel(
+    starts,
+    query_pre,
+    key_pre,
+    value_t,
+    query_inv,
+    key_inv,
+    query_gain,
+    key_gain,
+    cosine,
+    sine,
+    out,
+    query,
+    key,
+    key_t,
+    log_rows,
+    *,
+    size,
+    prompt_rows,
+    score_scale,
+):
+    i = pl.program_id(0)
+    half = HEAD // 2
+    total, columns = key.shape
+    spans = [slice(h * HEAD, (h + 1) * HEAD) for h in range(columns // HEAD)]
+    prompt_blocks = prompt_rows // size
+
+    @pl.when(i == 0)
+    def _():
+        @pl.loop(0, total // size)
+        def _(b):
+            at = pl.ds(pl.multiple_of(b * size, size), size)
+            cos, sin = cosine[:, at], sine[:, at]
+            for span in spans:
+                for pre, inv, gain, is_key in (
+                    (query_pre, query_inv, query_gain, False),
+                    (key_pre, key_inv, key_gain, True),
+                ):
+                    normed = pre[span, at] * inv[:, at] * gain[span, :]
+                    former, latter = normed[:half], normed[half:]
+                    turned = jnp.concatenate(
+                        [former * cos - latter * sin, latter * cos + former * sin], axis=0
+                    )
+                    if is_key:
+                        key_t[span, at] = turned.astype(jnp.bfloat16)
+                        key[at, span] = turned.T.astype(jnp.bfloat16)
+                    else:
+                        turned = turned * (score_scale * LOG2E)
+                        query[at, span] = turned.T.astype(jnp.bfloat16)
+
+    query_first = i * size
+    here = pl.ds(pl.multiple_of(query_first, size), size)
+    chunk = size // 2
+    parts = [slice(c * chunk, (c + 1) * chunk) for c in range(2)]
+    work = [(span, part) for span in spans for part in parts]
+    query_all = [query[here, span] for span in spans]
+    query_rows = [rows[part] for rows in query_all for part in parts]
+
+    def fold(j, states, masked):
+        at = pl.ds(pl.multiple_of(j * size, size), size)
+        scores = [dot_nt(key[at, span], rows) for (span, _), rows in zip(work, query_rows)]
+        if masked:
+            allowed = allowed_tile(starts, j * size, query_first, size, prompt_rows)
+        made = []
+        for (span, part), score, (highest, denominator, weighted) in zip(work, scores, states):
+            if masked:
+                score = jnp.where(allowed[:, part], score, MASKED)
+            new_high = jnp.maximum(highest, jnp.max(score, axis=0, keepdims=True))
+            shrink = jnp.exp2(highest - new_high)
+            unnormed = jnp.exp2(score - new_high)
+            denominator = denominator * shrink + jnp.sum(unnormed, axis=0, keepdims=True)
+            weighted = weighted * shrink + dot_nn(value_t[span, at], unnormed.astype(jnp.bfloat16))
+            made.append((new_high, denominator, weighted))
+        return tuple(made)
+
+    states = tuple(
+        (
+            jnp.full((1, chunk), MASKED, jnp.float32),
+            jnp.zeros((1, chunk), jnp.float32),
+            jnp.zeros((HEAD, chunk), jnp.float32),
+        )
+        for _ in work
+    )
+    in_prompt = i < prompt_blocks
+    whole = jnp.where(in_prompt, i, prompt_blocks)
+    states = lax.fori_loop(0, whole, lambda j, s: fold(j, s, False), states)
+    own_first = jnp.where(in_prompt, i, segment_start(starts, query_first) // size)
+    states = lax.fori_loop(own_first, i + 1, lambda j, s: fold(j, s, True), states)
+    for k, ((span, part), (highest, denominator, weighted)) in enumerate(zip(work, states)):
+        out[part, span] = (weighted / denominator).T.astype(jnp.bfloat16)
+        log_rows[k // 2 : k // 2 + 1, part] = highest + jnp.log2(denominator)
+
+
+def attend_forward(starts, query_pre, key_pre, value_t, query_inv, key_inv, query_gain, key_gain, cosine, sine, size, prompt_rows, score_scale):
+    columns, total = query_pre.shape
+    heads = columns // HEAD
+    pairs = total * total // 2
+
+    def once(shape):
+        return pl.BlockSpec(shape, lambda i, s: (0, 0), pipeline_mode=pl.Buffered(1))
+
+    wide, tall, row = (columns, total), (total, columns), (1, total)
+    gain, table = (columns, 1), (HEAD // 2, total)
+    return pl.pallas_call(
+        partial(attend_forward_kernel, size=size, prompt_rows=prompt_rows, score_scale=score_scale),
+        grid_spec=pltpu.PrefetchScalarGridSpec(
+            num_scalar_prefetch=1,
+            grid=(total // size,),
+            in_specs=[once(k) for k in (wide, wide, wide, row, row, gain, gain, table, table)],
+            out_specs=[
+                pl.BlockSpec((size, columns), lambda i, s: (i, 0)),
+                pl.BlockSpec(tall, lambda i, s: (0, 0)),
+                pl.BlockSpec(tall, lambda i, s: (0, 0)),
+                pl.BlockSpec(wide, lambda i, s: (0, 0)),
+                pl.BlockSpec((heads, size), lambda i, s: (0, i)),
+            ],
+        ),
+        out_shape=[
+            jax.ShapeDtypeStruct(tall, jnp.bfloat16),
+            jax.ShapeDtypeStruct(tall, jnp.bfloat16),
+            jax.ShapeDtypeStruct(tall, jnp.bfloat16),
+            jax.ShapeDtypeStruct(wide, jnp.bfloat16),
+            jax.ShapeDtypeStruct((heads, total), jnp.float32),
+        ],
+        compiler_params=pltpu.CompilerParams(vmem_limit_bytes=VMEM_BYTES),
+        cost_estimate=pl.CostEstimate(
+            flops=12 * pairs * columns, bytes_accessed=20 * total * columns, transcendentals=pairs * heads
+        ),
+        name="attend_forward",
+    )(starts, query_pre, key_pre, value_t, query_inv, key_inv, query_gain, key_gain, cosine, sine)
+
+
+def attend_backward_kernel(
+    starts,
+    query,
+    key,
+    key_t,
+    value_t,
+    out_grad,
+    out,
+    log_rows,
+    query_pre,
+    key_pre,
+    query_inv,
+    key_inv,
+    query_gain,
+    key_gain,
+    cosine,
+    sine,
+    query_scaled,
+    key_scaled,
+    value_grad,
+    dots,
+    query_gain_grad,
+    key_gain_grad,
+    query_sum,
+    key_sum,
+    row_dot,
+    *,
+    size,
+    prompt_rows,
+    score_scale,
+):
+    j = pl.program_id(0)
+    half = HEAD // 2
+    total, columns = key.shape
+    spans = [slice(h * HEAD, (h + 1) * HEAD) for h in range(columns // HEAD)]
+    blocks = total // size
+    prompt_blocks = prompt_rows // size
+
+    @pl.when(j == 0)
+    def _():
+        query_sum[...] = jnp.zeros_like(query_sum)
+
+        @pl.loop(0, blocks)
+        def _(b):
+            at = pl.ds(pl.multiple_of(b * size, size), size)
+            for h, span in enumerate(spans):
+                product = out_grad[at, span].astype(jnp.float32) * out[at, span].astype(jnp.float32)
+                row_dot[h : h + 1, at] = jnp.sum(product.T, axis=0, keepdims=True)
+
+    chunk = size // 2
+    here = pl.ds(pl.multiple_of(j * size, size), size)
+    key_rows = [key[here, span] for span in spans]
+    key_cols = [key_t[span, here] for span in spans]
+    value_rows = [value_t[span, here].T for span in spans]
+
+    def fold(i, states, masked):
+        if masked:
+            allowed = allowed_tile(starts, j * size, i * size, size, prompt_rows)
+        made = list(states)
+        for c in range(2):
+            at = pl.ds(pl.multiple_of(i * size + c * chunk, chunk), chunk)
+            query_rows = [query[at, span] for span in spans]
+            grad_rows = [out_grad[at, span] for span in spans]
+            scores = [dot_nt(k, q) for k, q in zip(key_rows, query_rows)]
+            prob_grads = [dot_nt(v, g) for v, g in zip(value_rows, grad_rows)]
+            for h, span in enumerate(spans):
+                key_part, value_part = made[h]
+                prob = jnp.exp2(scores[h] - log_rows[h : h + 1, at])
+                if masked:
+                    prob = jnp.where(allowed[:, c * chunk : (c + 1) * chunk], prob, 0.0)
+                score_grad = (prob * (prob_grads[h] - row_dot[h : h + 1, at])).astype(jnp.bfloat16)
+                value_part = value_part + dot_nn(prob.astype(jnp.bfloat16), grad_rows[h])
+                key_part = key_part + dot_nn(score_grad, query_rows[h])
+                query_sum[span, at] += dot_nn(key_cols[h], score_grad)
+                made[h] = (key_part, value_part)
+        return tuple(made)
+
+    states = tuple(
+        (jnp.zeros((size, HEAD), jnp.float32), jnp.zeros((size, HEAD), jnp.float32)) for _ in spans
+    )
+    in_prompt = j < prompt_blocks
+    last_own = (segment_end(starts, (j + 1) * size - 1, total) - 1) // size + 1
+    masked_end = jnp.where(in_prompt, j + 1, last_own)
+    states = lax.fori_loop(j, masked_end, lambda i, s: fold(i, s, True), states)
+    whole_end = jnp.where(in_prompt, blocks, masked_end)
+    states = lax.fori_loop(masked_end, whole_end, lambda i, s: fold(i, s, False), states)
+    for span, (key_part, value_part) in zip(spans, states):
+        key_sum[span, here] = key_part.T
+        value_grad[span, here] = value_part.T.astype(jnp.bfloat16)
+
+    @pl.when(j == blocks - 1)
+    def _():
+        query_gain_grad[...] = jnp.zeros_like(query_gain_grad)
+        key_gain_grad[...] = jnp.zeros_like(key_gain_grad)
+
+        @pl.loop(0, blocks)
+        def _(b):
+            at = pl.ds(pl.multiple_of(b * size, size), size)
+            cos, sin = cosine[:, at], sine[:, at]
+            for place, (grad, factor, pre, inv, gain, scaled, gain_grad) in enumerate(
+                (
+                    (query_sum, score_scale, query_pre, query_inv, query_gain, query_scaled, query_gain_grad),
+                    (key_sum, 1.0 / LOG2E, key_pre, key_inv, key_gain, key_scaled, key_gain_grad),
+                )
+            ):
+                summed = None
+                for span in spans:
+                    turned = grad[span, at] * factor
+                    former, latter = turned[:half], turned[half:]
+                    back = jnp.concatenate(
+                        [former * cos + latter * sin, latter * cos - former * sin], axis=0
+                    )
+                    before = pre[span, at]
+                    gain_grad[span, :] += jnp.sum(
+                        back * (before * inv[:, at]), axis=1, keepdims=True
+                    )
+                    back = back * gain[span, :]
+                    scaled[span, at] = back
+                    dot = jnp.sum(back * before, axis=0, keepdims=True)
+                    summed = dot if summed is None else summed + dot
+                dots[place : place + 1, at] = summed
+
+
+def attend_backward(starts, query, key, key_t, value_t, out_grad, out, log_rows, query_pre, key_pre, query_inv, key_inv, query_gain, key_gain, cosine, sine, size, prompt_rows, score_scale):
+    columns, total = query_pre.shape
+    heads = columns // HEAD
+    pairs = total * total // 2
+
+    def once(shape):
+        return pl.BlockSpec(shape, lambda j, s: (0, 0), pipeline_mode=pl.Buffered(1))
+
+    wide, tall, row = (columns, total), (total, columns), (1, total)
+    gain, table, per_head = (columns, 1), (HEAD // 2, total), (heads, total)
+    return pl.pallas_call(
+        partial(attend_backward_kernel, size=size, prompt_rows=prompt_rows, score_scale=score_scale),
+        grid_spec=pltpu.PrefetchScalarGridSpec(
+            num_scalar_prefetch=1,
+            grid=(total // size,),
+            in_specs=[
+                once(k)
+                for k in (tall, tall, wide, wide, tall, tall, per_head, wide, wide, row, row, gain, gain, table, table)
+            ],
+            out_specs=[once(k) for k in (wide, wide, wide, (2, total), gain, gain)],
+            scratch_shapes=[
+                pltpu.VMEM(wide, jnp.float32),
+                pltpu.VMEM(wide, jnp.float32),
+                pltpu.VMEM(per_head, jnp.float32),
+            ],
+        ),
+        out_shape=[
+            jax.ShapeDtypeStruct(wide, jnp.float32),
+            jax.ShapeDtypeStruct(wide, jnp.float32),
+            jax.ShapeDtypeStruct(wide, jnp.bfloat16),
+            jax.ShapeDtypeStruct((2, total), jnp.float32),
+            jax.ShapeDtypeStruct(gain, jnp.float32),
+            jax.ShapeDtypeStruct(gain, jnp.float32),
+        ],
+        compiler_params=pltpu.CompilerParams(vmem_limit_bytes=VMEM_BYTES),
+        cost_estimate=pl.CostEstimate(
+            flops=24 * pairs * columns, bytes_accessed=40 * total * columns, transcendentals=pairs * heads
+        ),
+        name="attend_backward",
+    )(starts, query, key, key_t, value_t, out_grad, out, log_rows, query_pre, key_pre, query_inv, key_inv, query_gain, key_gain, cosine, sine)
+
+
+def project_kernel(places, *refs, count):
+    blocks = refs[:count]
+    w_t, gain = refs[count : count + 2]
+    hidden, query_pre, key_pre, value_t, squares = refs[-5:]
+    columns = query_pre.shape[0]
+    for b, block in enumerate(blocks):
+
+        @pl.when(pl.program_id(0) // 2 == b)
+        def _(block=block):
+            rows = block[...].astype(jnp.float32)
+            inverse = lax.rsqrt(jnp.mean(rows * rows, axis=-1, keepdims=True) + EPSILON)
+            hidden[...] = (rows * inverse * gain[...]).astype(jnp.bfloat16)
+
+    for k, out in enumerate((query_pre, key_pre)):
+        made = dot_nt(w_t[k * columns : (k + 1) * columns, :], hidden[...])
+        out[...] = made
+        squares[k : k + 1, :] = jnp.sum(made * made, axis=0, keepdims=True)
+    value_t[...] = dot_nt(w_t[2 * columns :, :], hidden[...]).astype(jnp.bfloat16)
+
+
+def project(places, blocks, rows, w_t, gain, held, total):
+    count, width = len(blocks), blocks[0].shape[1]
+    columns = w_t.shape[0] // 3
+    tile = rows // 2
+    held = () if held is None else tuple(held)
+
+    def block_spec(b):
+        return pl.BlockSpec((tile, width), lambda i, p: (jnp.clip(i - 2 * b, 0, 1), 0))
+
+    def there(shape, along):
+        if along == 0:
+            return pl.BlockSpec(shape, lambda i, p: (2 * p[i // 2] + i % 2, 0))
+        return pl.BlockSpec(shape, lambda i, p: (0, 2 * p[i // 2] + i % 2))
+
+    return pl.pallas_call(
+        partial(project_kernel, count=count),
+        grid_spec=pltpu.PrefetchScalarGridSpec(
+            num_scalar_prefetch=1,
+            grid=(2 * count,),
+            in_specs=[block_spec(b) for b in range(count)]
+            + [
+                pl.BlockSpec(w_t.shape, lambda i, p: (0, 0)),
+                pl.BlockSpec((1, width), lambda i, p: (0, 0)),
+            ]
+            + [pl.BlockSpec(memory_space=pl.ANY)] * len(held),
+            out_specs=[
+                there((tile, width), 0),
+                there((columns, tile), 1),
+                there((columns, tile), 1),
+                there((columns, tile), 1),
+                there((2, tile), 1),
+            ],
+        ),
+        out_shape=[
+            jax.ShapeDtypeStruct((total, width), jnp.bfloat16),
+            jax.ShapeDtypeStruct((columns, total), jnp.float32),
+            jax.ShapeDtypeStruct((columns, total), jnp.float32),
+            jax.ShapeDtypeStruct((columns, total), jnp.bfloat16),
+            jax.ShapeDtypeStruct((2, total), jnp.float32),
+        ],
+        input_output_aliases={3 + count + k: k for k in range(len(held))},
+        compiler_params=pltpu.CompilerParams(vmem_limit_bytes=VMEM_BYTES),
+        cost_estimate=pl.CostEstimate(
+            flops=6 * count * rows * width * columns,
+            bytes_accessed=count * (4 * rows * width + 10 * rows * columns) + 6 * width * columns,
+            transcendentals=count * rows,
+        ),
+        name="project",
+    )(places, *blocks, w_t, gain, *held)
+
+
+def place_rows_kernel(places, *refs):
+    *pieces, out = refs
+    for k, piece in enumerate(pieces):
+        out[places[k]] = piece[...]
+
+
+def place_rows(places, blocks, first, rows):
+    width = blocks[0].shape[1]
+    return pl.pallas_call(
+        place_rows_kernel,
+        grid_spec=pltpu.PrefetchScalarGridSpec(
+            num_scalar_prefetch=1,
+            grid=(1,),
+            in_specs=[pl.BlockSpec((rows, width), lambda i, p: (first // rows, 0))] * len(blocks),
+            out_specs=pl.BlockSpec((len(blocks), rows, width), lambda i, p: (0, 0, 0)),
+        ),
+        out_shape=jax.ShapeDtypeStruct((len(blocks), rows, width), blocks[0].dtype),
+        compiler_params=pltpu.CompilerParams(vmem_limit_bytes=VMEM_BYTES),
+        name="place_rows",
+    )(places, *blocks)
+
+
+def hidden_term_kernel(place, heads_grad, w_t, out_rows, *refs, start, halves):
+    outs = refs[-2:] if halves else refs[-1:]
+    rows = heads_grad.shape[1]
+    term = dot_tn(heads_grad[...], w_t[...])
+    below = out_rows[0]
+    if halves:
+        cut = outs[0].shape[0]
+        outs[0][...] = term[:cut].astype(jnp.bfloat16)
+        outs[1][: rows - cut, :] = term[cut:].astype(jnp.bfloat16)
+        outs[1][rows - cut :, :] = below
+        return
+    (out,) = outs
+    got = refs[0]
+    stop = start + got.shape[0]
+    upper = min(stop, rows)
+    if start:
+        out[:start, :] = term[:start].astype(jnp.bfloat16)
+    if upper < rows:
+        out[upper:rows, :] = term[upper:].astype(jnp.bfloat16)
+    out[start:upper, :] = (
+        term[start:upper] + got[: upper - start, :].astype(jnp.float32)
+    ).astype(jnp.bfloat16)
+    if stop > rows:
+        below = below.astype(jnp.float32) + got[rows - start :, :].astype(jnp.float32)
+    out[rows:, :] = below.astype(jnp.bfloat16)
+
+
+def hidden_term(place, heads_grad, w_t, out_rows, rows, got=None, start=0):
+    columns, width = w_t.shape
+    whole = rows + out_rows.shape[1]
+    tile = min(512, width)
+    halves = got is None
+    gots, outs = ([], [whole // 2] * 2) if halves else ([got], [whole])
+    made = pl.pallas_call(
+        partial(hidden_term_kernel, start=start, halves=halves),
+        grid_spec=pltpu.PrefetchScalarGridSpec(
+            num_scalar_prefetch=1,
+            grid=(width // tile,),
+            in_specs=[
+                pl.BlockSpec((columns, rows), lambda i, p: (0, p[0])),
+                pl.BlockSpec((columns, tile), lambda i, p: (0, i)),
+                pl.BlockSpec((1, whole - rows, tile), lambda i, p: (p[0], 0, i)),
+            ]
+            + [pl.BlockSpec((g.shape[0], tile), lambda i, p: (0, i)) for g in gots],
+            out_specs=[pl.BlockSpec((count, tile), lambda i, p: (0, i)) for count in outs],
+        ),
+        out_shape=[jax.ShapeDtypeStruct((count, width), jnp.bfloat16) for count in outs],
+        compiler_params=pltpu.CompilerParams(vmem_limit_bytes=VMEM_BYTES),
+        cost_estimate=pl.CostEstimate(
+            flops=2 * rows * width * columns,
+            bytes_accessed=2 * columns * (rows + width) + 4 * whole * width,
+            transcendentals=0,
+        ),
+        name="hidden_term",
+    )(place, heads_grad, w_t, out_rows, *gots)
+    return made if halves else made[0]
+
+
+def own_term_kernel(place, heads_grad, w_t, out_rows, before, past, hidden_grad, out_grad):
+    rows = heads_grad.shape[1]
+    term = dot_tn(heads_grad[...], w_t[...])
+    got = before[...].astype(jnp.float32) + past[...].astype(jnp.float32)
+    hidden_grad[...] = term + got[:rows]
+    out_grad[...] = out_rows[0].astype(jnp.float32) + got[rows:]
+
+
+def own_term(place, heads_grad, w_t, out_rows, rows, before, past):
+    columns, width = w_t.shape
+    extra = out_rows.shape[1]
+    tile = min(512, width)
+    return pl.pallas_call(
+        own_term_kernel,
+        grid_spec=pltpu.PrefetchScalarGridSpec(
+            num_scalar_prefetch=1,
+            grid=(width // tile,),
+            in_specs=[
+                pl.BlockSpec((columns, rows), lambda i, p: (0, p[0])),
+                pl.BlockSpec((columns, tile), lambda i, p: (0, i)),
+                pl.BlockSpec((1, extra, tile), lambda i, p: (p[0], 0, i)),
+                pl.BlockSpec((rows + extra, tile), lambda i, p: (0, i)),
+                pl.BlockSpec((rows + extra, tile), lambda i, p: (0, i)),
+            ],
+            out_specs=[
+                pl.BlockSpec((rows, tile), lambda i, p: (0, i)),
+                pl.BlockSpec((extra, tile), lambda i, p: (0, i)),
+            ],
+        ),
+        out_shape=[
+            jax.ShapeDtypeStruct((rows, width), jnp.float32),
+            jax.ShapeDtypeStruct((extra, width), jnp.float32),
+        ],
+        compiler_params=pltpu.CompilerParams(vmem_limit_bytes=VMEM_BYTES),
+        cost_estimate=pl.CostEstimate(
+            flops=2 * rows * width * columns,
+            bytes_accessed=2 * columns * (rows + width) + 8 * (rows + extra) * width,
+            transcendentals=0,
+        ),
+        name="own_term",
+    )(place, heads_grad, w_t, out_rows, before, past)
+
+
+def out_grad_kernel(branch, w_out, out):
+    out[0] = dot_nt(branch[...], w_out[...]).astype(jnp.bfloat16)
+
+
+def out_grad_of(branch, w_out, contexts):
+    rows, width = branch.shape
+    columns = w_out.shape[0] // contexts
+    return pl.pallas_call(
+        out_grad_kernel,
+        grid=(contexts,),
+        in_specs=[
+            pl.BlockSpec((rows, width), lambda i: (0, 0)),
+            pl.BlockSpec((columns, width), lambda i: (i, 0)),
+        ],
+        out_specs=pl.BlockSpec((1, rows, columns), lambda i: (i, 0, 0)),
+        out_shape=jax.ShapeDtypeStruct((contexts, rows, columns), jnp.bfloat16),
+        compiler_params=pltpu.CompilerParams(vmem_limit_bytes=VMEM_BYTES),
+        cost_estimate=pl.CostEstimate(
+            flops=2 * rows * width * width, bytes_accessed=2 * width * width, transcendentals=0
+        ),
+        name="out_grad",
+    )(branch, w_out)
+
+
+def heads_grad_kernel(query_scaled, key_scaled, value_grad, query_pre, key_pre, inverse, dots, out):
+    columns = query_scaled.shape[0]
+    for k, (scaled, pre) in enumerate(((query_scaled, query_pre), (key_scaled, key_pre))):
+        inv = inverse[k : k + 1, :]
+        factor = inv * inv * dots[k : k + 1, :]
+        out[k * columns : (k + 1) * columns, :] = (inv * (scaled[...] - pre[...] * factor)).astype(
+            jnp.bfloat16
+        )
+    out[2 * columns :, :] = value_grad[...]
+
+
+def heads_grad_of(query_scaled, key_scaled, value_grad, query_pre, key_pre, inverse, dots):
+    columns, total = query_scaled.shape
+    tile = total // 4
+    wide = pl.BlockSpec((columns, tile), lambda i: (0, i))
+    row = pl.BlockSpec((2, tile), lambda i: (0, i))
+    return pl.pallas_call(
+        heads_grad_kernel,
+        grid=(4,),
+        in_specs=[wide] * 5 + [row] * 2,
+        out_specs=pl.BlockSpec((3 * columns, tile), lambda i: (0, i)),
+        out_shape=jax.ShapeDtypeStruct((3 * columns, total), jnp.bfloat16),
+        compiler_params=pltpu.CompilerParams(vmem_limit_bytes=VMEM_BYTES),
+        cost_estimate=pl.CostEstimate(
+            flops=8 * columns * total, bytes_accessed=24 * columns * total, transcendentals=0
+        ),
+        name="heads_grad",
+    )(query_scaled, key_scaled, value_grad, query_pre, key_pre, inverse, dots)
+
+
+def heads_product_kernel(heads_grad, hidden, others, out):
+    columns = heads_grad.shape[0]
+    out[0, :, :columns] = dot_nn(heads_grad[...], hidden[...]).T.astype(jnp.bfloat16)
+    out[0, :, columns:] = others[...].astype(jnp.bfloat16)
+
+
+def heads_product_of(heads_grad, hidden_all, others, contexts):
+    columns, total = heads_grad.shape
+    width = hidden_all.shape[1]
+    tile, extra = width // contexts, others.shape[1]
+    return pl.pallas_call(
+        heads_product_kernel,
+        grid=(contexts,),
+        in_specs=[
+            pl.BlockSpec((columns, total), lambda i: (0, 0), pipeline_mode=pl.Buffered(1)),
+            pl.BlockSpec((total, tile), lambda i: (0, i)),
+            pl.BlockSpec((tile, extra), lambda i: (i, 0)),
+        ],
+        out_specs=pl.BlockSpec((1, tile, columns + extra), lambda i: (i, 0, 0)),
+        out_shape=jax.ShapeDtypeStruct((contexts, tile, columns + extra), jnp.bfloat16),
+        compiler_params=pltpu.CompilerParams(vmem_limit_bytes=VMEM_BYTES),
+        cost_estimate=pl.CostEstimate(
+            flops=2 * columns * total * width,
+            bytes_accessed=2 * total * (columns + width),
+            transcendentals=0,
+        ),
+        name="heads_product",
+    )(heads_grad, hidden_all, others)
+
+
+def gather_pieces_kernel(me, *refs):
+    *pieces, out = refs
+    for step, piece in enumerate(pieces):
+        out[lax.rem(me[0] + step, len(pieces))] = piece[...]
+
+
+def gather_pieces(me, pieces):
+    return pl.pallas_call(
+        gather_pieces_kernel,
+        grid_spec=pltpu.PrefetchScalarGridSpec(
+            num_scalar_prefetch=1,
+            grid=(1,),
+            in_specs=[pl.BlockSpec(piece.shape, lambda i, m: (0, 0)) for piece in pieces],
+            out_specs=pl.BlockSpec((len(pieces),) + pieces[0].shape, lambda i, m: (0, 0, 0)),
+        ),
+        out_shape=jax.ShapeDtypeStruct((len(pieces),) + pieces[0].shape, pieces[0].dtype),
+        compiler_params=pltpu.CompilerParams(vmem_limit_bytes=VMEM_BYTES),
+        name="gather_pieces",
+    )(me[None], *pieces)
+
+
+def slot_match(rank_row, slots):
+    return lax.broadcasted_iota(jnp.int32, (slots, rank_row.shape[1]), 0) == rank_row
+
+
+def slot_gates(match, gate_row):
+    return jnp.sum(jnp.where(match, gate_row, 0.0), axis=1, keepdims=True)
+
+
+def experts_forward_kernel(*refs, count, slots, aliased, tiles):
+    ranks, gates = refs[:2]
+    blocks = refs[2 : 2 + count]
+    w_gate, w_up, w_down = refs[2 + count : 5 + count]
+    refs = refs[5 + count + aliased :]
+    taken, active, gate_slope, up_slope = refs[:4]
+    outs = refs[4 : 4 + count]
+    made, weights = refs[4 + count :]
+    e, f = pl.program_id(0), pl.program_id(1)
+    tile, wide_tile = w_gate.shape[2], w_down.shape[2]
+
+    @pl.when(f == 0)
+    def _():
+        for b in range(count):
+            here = slice(b * slots, (b + 1) * slots)
+            match = slot_match(ranks[b, e], slots)
+            weights[here, :] = slot_gates(match, gates[b, e])
+            taken[0, here, :] = dot_nn(match.astype(jnp.bfloat16), blocks[b][...]).astype(
+                jnp.bfloat16
+            )
+
+    @pl.when(f < tiles)
+    def _():
+        at = pl.ds(pl.multiple_of(f * tile, tile), tile)
+        rows = taken[0]
+        gate_pre = dot_nn(rows, w_gate[0])
+        up_pre = dot_nn(rows, w_up[0])
+        sigmoid_gate = 1.0 / (1.0 + jnp.exp(-gate_pre))
+        silu = gate_pre * sigmoid_gate
+        active[0, :, at] = (silu * up_pre).astype(jnp.bfloat16)
+        up_slope[0, :, at] = silu.astype(jnp.bfloat16)
+        gate_slope[0, :, at] = (up_pre * (sigmoid_gate + silu * (1.0 - sigmoid_gate))).astype(
+            jnp.bfloat16
+        )
+
+    @pl.when(f >= tiles)
+    def _():
+        at = pl.ds(pl.multiple_of((f - tiles) * wide_tile, wide_tile), wide_tile)
+        made[e, :, at] = (dot_nn(active[0], w_down[0]) * weights[...]).astype(jnp.bfloat16)
+
+    @pl.when((f == pl.num_programs(1) - 1) & (e == pl.num_programs(0) - 1))
+    def _():
+        combine(ranks, made, outs, count, slots)
+
+
+def combine(ranks, made, outs, count, slots):
+    for b in range(count):
+        summed = None
+        for k in range(made.shape[0]):
+            match = slot_match(ranks[b, k], slots).astype(jnp.float32).astype(jnp.bfloat16)
+            term = dot_tn(match, made[k, b * slots : (b + 1) * slots, :])
+            summed = term if summed is None else summed + term
+        outs[b][...] = summed.astype(jnp.bfloat16)
+
+
+def experts_backward_kernel(*refs, count, slots, aliased, tiles):
+    ranks, gates = refs[:2]
+    blocks = refs[2 : 2 + count]
+    w_gate, w_up, w_down, gate_slope, up_slope = refs[2 + count : 7 + count]
+    refs = refs[7 + count + aliased :]
+    taken, gate_grad, up_grad = refs[:3]
+    outs = refs[3 : 3 + count]
+    (made,) = refs[3 + count :]
+    e, f = pl.program_id(0), pl.program_id(1)
+    tile, wide_tile = w_down.shape[1], w_gate.shape[1]
+
+    @pl.when(f == 0)
+    def _():
+        for b in range(count):
+            match = slot_match(ranks[b, e], slots)
+            weight = slot_gates(match, gates[b, e])
+            taken[0, b * slots : (b + 1) * slots, :] = (
+                dot_nn(match.astype(jnp.bfloat16), blocks[b][...]) * weight
+            ).astype(jnp.bfloat16)
+
+    @pl.when(f < tiles)
+    def _():
+        at = pl.ds(pl.multiple_of(f * tile, tile), tile)
+        active_grad = dot_nt(taken[0], w_down[0])
+        gate_grad[0, :, at] = (active_grad * gate_slope[0].astype(jnp.float32)).astype(jnp.bfloat16)
+        up_grad[0, :, at] = (active_grad * up_slope[0].astype(jnp.float32)).astype(jnp.bfloat16)
+
+    @pl.when(f >= tiles)
+    def _():
+        at = pl.ds(pl.multiple_of((f - tiles) * wide_tile, wide_tile), wide_tile)
+        made[e, :, at] = (dot_nt(gate_grad[0], w_gate[0]) + dot_nt(up_grad[0], w_up[0])).astype(
+            jnp.bfloat16
+        )
+
+    @pl.when((f == pl.num_programs(1) - 1) & (e == pl.num_programs(0) - 1))
+    def _():
+        combine(ranks, made, outs, count, slots)
+
+
+def experts_stage(
+    forward, ranks, gates, blocks, weights, slopes, held, place, slots, all_slots, light=False
+):
+    count = len(blocks)
+    rows, width = blocks[0].shape
+    experts, _, hidden_units = weights[0].shape
+    tile, wide_tile = min(512, hidden_units), min(1024, width)
+    tiles, wide_tiles = hidden_units // tile, width // wide_tile
+    part = count * slots
+
+    def first(f):
+        return jnp.minimum(f, tiles - 1)
+
+    def later(f):
+        return jnp.maximum(f - tiles, 0)
+
+    info = pl.BlockSpec((count, experts, 1, rows), lambda e, f: (0, 0, 0, 0))
+    block = pl.BlockSpec((rows, width), lambda e, f: (0, 0))
+    wide = pl.BlockSpec((1, part, width), lambda e, f: (e, place, 0))
+    narrow = pl.BlockSpec((1, part, hidden_units), lambda e, f: (e, place, 0))
+    slope = pl.BlockSpec((1, part, tile), lambda e, f: (e, 0, first(f)))
+    own = pl.BlockSpec((1, part, hidden_units), lambda e, f: (e, 0, 0))
+    if forward:
+        kernel, name = experts_forward_kernel, "experts_forward"
+        into = pl.BlockSpec((1, width, tile), lambda e, f: (e, 0, first(f)))
+        back = pl.BlockSpec((1, hidden_units, wide_tile), lambda e, f: (e, 0, later(f)))
+        narrow_outs, own_outs, scratch = 1, 2, [pltpu.VMEM((part, 1), jnp.float32)]
+    else:
+        kernel, name = experts_backward_kernel, "experts_backward"
+        into = pl.BlockSpec((1, wide_tile, hidden_units), lambda e, f: (e, later(f), 0))
+        back = pl.BlockSpec((1, tile, width), lambda e, f: (e, first(f), 0))
+        narrow_outs, own_outs, scratch = 2, 0, []
+    held = () if held is None else tuple(held)
+    before = 2 + count + 3 + len(slopes)
+    scale = 0 if light else 1
+    flops = 2 * experts * part * width * (3 * hidden_units + 2 * rows)
+    return pl.pallas_call(
+        partial(kernel, count=count, slots=slots, aliased=len(held), tiles=tiles),
+        grid=(experts, tiles + wide_tiles),
+        in_specs=[info, info]
+        + [block] * count
+        + [into, into, back]
+        + [slope] * len(slopes)
+        + [pl.BlockSpec(memory_space=pl.ANY)] * len(held),
+        out_specs=[wide] + [narrow] * narrow_outs + [own] * own_outs + [block] * count,
+        out_shape=[jax.ShapeDtypeStruct((experts, all_slots, width), jnp.bfloat16)]
+        + [jax.ShapeDtypeStruct((experts, all_slots, hidden_units), jnp.bfloat16)] * narrow_outs
+        + [jax.ShapeDtypeStruct((experts, part, hidden_units), jnp.bfloat16)] * own_outs
+        + [jax.ShapeDtypeStruct((rows, width), jnp.bfloat16)] * count,
+        scratch_shapes=[pltpu.VMEM((experts, part, width), jnp.bfloat16)] + scratch,
+        input_output_aliases={before + k: k for k in range(len(held))},
+        compiler_params=pltpu.CompilerParams(vmem_limit_bytes=VMEM_BYTES),
+        cost_estimate=pl.CostEstimate(
+            flops=scale * flops,
+            bytes_accessed=scale
+            * 2
+            * (3 * experts * width * hidden_units + 4 * count * rows * width),
+            transcendentals=scale * experts * part * hidden_units,
+        ),
+        name=name,
+    )(ranks, gates, *blocks, *weights, *slopes, *held)
+
+
+def ring_of(contexts):
+    order = list(range(0, contexts, 2)) + list(range(contexts - 1, 0, -2))
+    place_of = [order.index(c) for c in range(contexts)]
+    up = [(order[p], order[(p + 1) % contexts]) for p in range(contexts)]
+    down = [(b, a) for a, b in up]
+    return order, place_of, up, down
+
+
+class RingGather:
+    def __init__(self, own, ring):
+        _, _, self.up, self.down = ring
+        self.half = len(self.up) // 2
+        self.step = 0
+        self.blocks = {0: own}
+        self.from_before = self.from_after = own
+
+    def advance(self, *earlier):
+        self.step += 1
+        before, past = self.from_before, self.from_after
+        if earlier:
+            before, past = lax.optimization_barrier((before, past) + earlier)[:2]
+        if self.step < self.half:
+            self.from_before = lax.ppermute(before, "ctx", self.up)
+            self.from_after = lax.ppermute(past, "ctx", self.down)
+            self.blocks[-self.step] = self.from_before
+            self.blocks[self.step] = self.from_after
+            return (-self.step, self.step)
+        cut = before.shape[0] // 2
+        first = lax.ppermute(before[:cut], "ctx", self.up)
+        second = lax.ppermute(past[cut:], "ctx", self.down)
+        self.blocks[self.half] = jnp.concatenate([first, second], axis=0)
+        return (self.half,)
+
+
+def add_low(left, right):
+    return (left.astype(jnp.float32) + right.astype(jnp.float32)).astype(jnp.bfloat16)
+
+
+class RingScatter:
+    def __init__(self, ring):
+        _, _, self.up, self.down = ring
+        self.half = len(self.up) // 2
+        self.step = self.half
+
+    def prepare(self, terms, *earlier):
+        if self.step == self.half:
+            far = after(terms[self.half], *earlier)
+            cut = far.shape[0] // 2
+            before, past = far[:cut], far[cut:]
+        else:
+            before, past = terms[-self.step], terms[self.step]
+            got_before, got_past = self.to_before, self.to_after
+            if earlier:
+                before, past = lax.optimization_barrier((before, past) + earlier)[:2]
+            cut = got_before.shape[0]
+            if cut < before.shape[0]:
+                before = jnp.concatenate([add_low(got_before, before[:cut]), before[cut:]], axis=0)
+                past = jnp.concatenate([past[:cut], add_low(got_past, past[cut:])], axis=0)
+            else:
+                before, past = add_low(got_before, before), add_low(got_past, past)
+        self.payload = (before, past)
+        return self.payload
+
+    def send(self, *earlier):
+        before, past = self.payload
+        if earlier:
+            before, past = lax.optimization_barrier((before, past) + earlier)[:2]
+        self.to_before = lax.ppermute(before, "ctx", self.down)
+        self.to_after = lax.ppermute(past, "ctx", self.up)
+        self.step -= 1
+        return self.payload
+
+    def advance(self, terms, *earlier):
+        self.prepare(terms, *earlier)
+        return self.send()
+
+    def finish(self, own):
+        return (
+            own.astype(jnp.float32)
+            + self.to_before.astype(jnp.float32)
+            + self.to_after.astype(jnp.float32)
+        )
+
+
+def sum_over_ctx(values, contexts):
+    bit = 1
+    while bit < contexts:
+        values = values + lax.ppermute(values, "ctx", [(c, c ^ bit) for c in range(contexts)])
+        bit *= 2
+    return values
+
+
+def after(value, *earlier):
+    return lax.optimization_barrier((value,) + earlier)[0]
+
+
+def shards_by_heads(
+    tokens,
+    cotangent,
+    cont_lengths,
+    routes,
+    gates,
+    attn_gain,
+    query_gain,
+    key_gain,
+    ffn_gain,
+    w_query,
+    w_key,
+    w_value,
+    w_out,
+    w_gate,
+    w_up,
+    w_down,
+):
+    both = ("ctx", "fsdp")
+    contexts, splits = lax.axis_size("ctx"), lax.axis_size("fsdp")
+    rows, width = tokens.shape[1:]
+    route_count = routes.shape[2]
+    total = rows * contexts
+    prompt_rows = total // 2
+    columns = width // contexts
+    size = min(512, prompt_rows)
+    local_experts = w_gate.shape[0]
+    expert_total = local_experts * contexts
+    slots = max(2, rows * route_count * 5 // (4 * expert_total))
+    all_slots = contexts * slots
+    score_scale = HEAD ** (-0.5)
+    me = lax.axis_index("ctx")
+    ring = ring_of(contexts)
+    half = contexts // 2
+    place = jnp.where(me % 2 == 0, me // 2, contexts - 1 - me // 2)
+
+    def owner(offset):
+        at = (place + offset) % contexts
+        return jnp.where(at < half, 2 * at, 2 * (contexts - 1 - at) + 1)
+
+    others = [k for step in range(1, half) for k in (-step, step)] + [half]
+
+    own_rows = w_out.shape[0]
+    token_ring = RingGather(jnp.concatenate([tokens[0], w_out], axis=0), ring)
+
+    chosen = routes[0].T[None] == jnp.arange(expert_total, dtype=jnp.int32)[:, None, None]
+    member = jnp.any(chosen, axis=1)
+    gate_rows = jnp.sum(jnp.where(chosen, gates[0].T[None], 0.0), axis=1)
+    earlier = jnp.tril(jnp.ones((rows, rows), jnp.bfloat16), -1)
+    rank = jnp.einsum(
+        "et,ut->eu", member.astype(jnp.bfloat16), earlier, preferred_element_type=jnp.float32
+    )
+    rank = jnp.where(member, rank, -1.0)
+    rank_high = jnp.floor(rank / 16.0)
+    gate_high = gate_rows.astype(jnp.bfloat16).astype(jnp.float32)
+    routing = jnp.stack([rank_high, rank - 16.0 * rank_high, gate_high, gate_rows - gate_high])
+    routing = routing.astype(jnp.bfloat16).reshape(4, contexts, local_experts * rows)
+    routing = jnp.transpose(routing, (1, 0, 2)).reshape(contexts, own_rows, -1)
+    routing_columns = routing.shape[2]
+
+    cut = jnp.stack([w_query, w_key, w_value]).reshape(3, own_rows, contexts, columns)
+    cut = jnp.transpose(cut, (2, 1, 0, 3)).reshape(contexts, own_rows, 3 * columns)
+    own_gains = jnp.stack([attn_gain, query_gain, key_gain, ffn_gain], axis=1)
+    cut = jnp.concatenate(
+        [cut, jnp.broadcast_to(own_gains, (contexts,) + own_gains.shape), routing], axis=2
+    )
+    spare = -cut.shape[2] % 128
+    cut = jnp.pad(cut, ((0, 0), (0, 0), (0, spare)))
+    pieces = []
+    for step in range(contexts):
+        piece = lax.dynamic_index_in_dim(cut, (me - step) % contexts, 0, keepdims=False)
+        if step:
+            pairs = [(c, (c - step) % contexts) for c in range(contexts)]
+            piece = lax.ppermute(piece, "ctx", pairs)
+        pieces.append(piece)
+    first_piece = pieces[1]
+    pieces = gather_pieces(me, pieces)
+    token_ring.advance(first_piece)
+    gate_all = lax.all_gather(after(w_gate, pieces), "fsdp", axis=1, tiled=True)
+    w_all = lax.all_gather(pieces, "fsdp", axis=1, tiled=True).reshape(width, -1)
+    up_all = lax.all_gather(w_up, "fsdp", axis=1, tiled=True)
+    for _ in range(2, half):
+        token_ring.advance()
+    w_t = w_all[:, : 3 * columns].T
+    all_gains = w_all[:, 3 * columns : 3 * columns + 4].astype(jnp.float32).T
+    gain_attn, gain_ffn = all_gains[0], all_gains[3]
+    gain_query = lax.dynamic_slice_in_dim(all_gains[1], me * columns, columns)[:, None]
+    gain_key = lax.dynamic_slice_in_dim(all_gains[2], me * columns, columns)[:, None]
+
+    owners = owner(jnp.arange(contexts, dtype=jnp.int32))
+    routing = pieces[:, :, 3 * columns + 4 : 3 * columns + 4 + routing_columns]
+    routing = routing.reshape(contexts, 4, local_experts, 1, rows)[owners].astype(jnp.float32)
+    all_ranks = (16.0 * routing[:, 0] + routing[:, 1]).astype(jnp.int32)
+    all_gates = routing[:, 2] + routing[:, 3]
+
+    lengths_in = cont_lengths[0]
+    token_index = jnp.arange(total, dtype=jnp.int32)
+    _, position = places(token_index, lengths_in, prompt_rows)
+    starts = prompt_rows + jnp.cumsum(lengths_in) - lengths_in
+    frequency = ROPE_BASE ** (-jnp.arange(HEAD // 2).astype(jnp.float32) / (HEAD // 2))
+    angles = frequency[:, None] * position.astype(jnp.float32)[None, :]
+    cosine, sine = jnp.cos(angles), jnp.sin(angles)
+
+    def project_all(offsets, made):
+        blocks = [token_ring.blocks[offset] for offset in offsets]
+        places_of = owner(jnp.asarray(offsets, jnp.int32))
+        return project(places_of, blocks, rows, w_t, gain_attn[None], made, total)
+
+    made = project_all([0] + others[: 2 * (half - 2)], None)
+    token_ring.advance(made[-1], up_all)
+    made = project_all(others[2 * (half - 2) : -1], made)
+    made = project_all(others[-1:], made)
+    hidden_all, query_pre, key_pre, value_t, squares = made
+    w_out_rows = place_rows(
+        owners, [token_ring.blocks[k if k <= half else k - contexts] for k in range(contexts)], rows, own_rows
+    )
+    out_all = lax.all_gather(w_out_rows, "fsdp", axis=1, tiled=True).reshape(width, width)
+    down_all = lax.all_gather(w_down, "fsdp", axis=1, tiled=True)
+
+    squares = sum_over_ctx(squares, contexts)
+    inverse = lax.rsqrt(squares / width + EPSILON)
+    query_inv, key_inv = inverse[0:1], inverse[1:2]
+    grad_ring = RingGather(cotangent[0], ring)
+    grad_ring.advance(squares)
+
+    attended, query, key, key_t, log_rows = attend_forward(
+        starts, query_pre, key_pre, value_t, query_inv, key_inv, gain_query, gain_key, cosine, sine, size, prompt_rows, score_scale
+    )
+    sent = after(attended, grad_ring.from_before, grad_ring.from_after)
+    back = lax.all_to_all(
+        sent.reshape(contexts, rows, columns), "ctx", split_axis=0, concat_axis=0, tiled=True
+    )
+    grad_ring.advance(attended)
+    own_attended = jnp.transpose(back, (1, 0, 2)).reshape(rows, width)
+    inputs = tokens[0].astype(jnp.float32)
+    mixed = inputs + jnp.dot(own_attended, out_all, preferred_element_type=jnp.float32)
+    mixed_inv = lax.rsqrt(jnp.mean(mixed * mixed, axis=-1, keepdims=True) + EPSILON)
+    second = (mixed * mixed_inv * gain_ffn).astype(jnp.bfloat16)
+
+    second_ring = RingGather(second, ring)
+    weights = (gate_all, up_all, down_all)
+
+    def stage_info(offsets):
+        ranks = jnp.stack([all_ranks[k] for k in offsets])
+        stage_gates = jnp.stack([all_gates[k] for k in offsets])
+        if len(offsets) == 2:
+            return ranks, stage_gates, offsets[1] - 1
+        return ranks, stage_gates, contexts - (2 if offsets[0] == 0 else 1)
+
+    stages = [(0,)] + [(-step, step) for step in range(1, half)] + [(half,)]
+    infos = [stage_info(stage) for stage in stages]
+    result_terms, second_terms, slopes = {}, {}, {}
+    kept = kept_grads = None
+
+    def forward(step, *earlier):
+        nonlocal kept
+        ranks, stage_gates, at = infos[step]
+        ranks = after(ranks, *earlier) if earlier else ranks
+        blocks = [second_ring.blocks[k] for k in stages[step]]
+        made = experts_stage(
+            True, ranks, stage_gates, blocks, weights, (), kept, at, slots, all_slots
+        )
+        kept, slopes[step], terms = made[:2], made[2:4], made[4:]
+        result_terms.update(zip(stages[step], terms))
+        return terms[0]
+
+    def backward(step, *earlier, light=False):
+        nonlocal kept_grads
+        ranks, stage_gates, at = infos[step]
+        ranks = after(ranks, *earlier) if earlier else ranks
+        blocks = [grad_ring.blocks[k] for k in stages[step]]
+        made = experts_stage(
+            False,
+            ranks,
+            stage_gates,
+            blocks,
+            weights,
+            slopes[step],
+            kept_grads,
+            at,
+            slots,
+            all_slots,
+            light,
+        )
+        kept_grads, terms = made[:3], made[3:]
+        second_terms.update(zip(stages[step], terms))
+        return terms[0]
+
+    def weight_grad(left, right):
+        return jnp.einsum("emd,emf->edf", left, right, preferred_element_type=jnp.float32).astype(
+            jnp.bfloat16
+        )
+
+    second_ring.advance()
+    grad_second = (grad_ring.from_before, grad_ring.from_after)
+    done = forward(0)
+    done = backward(0, done, *grad_second, light=True)
+    for step in range(1, half):
+        near = [second_ring.blocks[k] for k in stages[step]]
+        second_ring.advance(done)
+        waits = (done,)
+        if step > 1:
+            waits += (grad_ring.from_before, grad_ring.from_after)
+        if step == half - 1:
+            waits = (done, grad_ring.blocks[half])
+        else:
+            grad_ring.advance(done, *near)
+        done = forward(step, *waits)
+        if step < half - 1:
+            done = backward(step, done, light=True)
+    done = forward(half, done)
+
+    second_sum, result_sum = RingScatter(ring), RingScatter(ring)
+    result_sum.advance(result_terms)
+    backward(half, done)
+    sent = second_sum.advance(second_terms, result_sum.to_before, result_sum.to_after)
+    sent += result_sum.prepare(result_terms, *sent)
+    result_sum.send()
+    backward(half - 1, *sent)
+    rows_taken, active = kept
+    route_grad, gate_grad, up_grad = kept_grads
+    sent = second_sum.advance(second_terms)
+    gate_product = weight_grad(
+        after(rows_taken, result_sum.to_before, result_sum.to_after, *sent), gate_grad
+    )
+    sent = second_sum.advance(second_terms, gate_product)
+    up_product = weight_grad(after(rows_taken, *sent), up_grad)
+    sent = second_sum.advance(second_terms, up_product)
+    result_sum.prepare(result_terms, *sent)
+    down_product = weight_grad(after(active, *result_sum.payload), route_grad)
+    second_grad = second_sum.finish(after(second_terms[0], down_product))
+
+    def fsdp_sum_low(product):
+        return lax.psum_scatter(product, "fsdp", scatter_dimension=1, tiled=True)
+
+    def fsdp_sum(product):
+        return fsdp_sum_low(product).astype(jnp.float32)
+
+    gate_w_grad = fsdp_sum(gate_product)
+    up_w_grad = fsdp_sum(up_product)
+
+    upstream = cotangent[0].astype(jnp.float32)
+    mixed_normed = mixed * mixed_inv
+    ffn_gain_grad = jnp.sum(second_grad * mixed_normed, axis=0)
+    scaled = second_grad * gain_ffn
+    mixed_grad = upstream + mixed_inv * (
+        scaled - mixed_normed * jnp.mean(scaled * mixed_normed, axis=-1, keepdims=True)
+    )
+    branch = mixed_grad.astype(jnp.bfloat16)
+    out_grad = out_grad_of(branch, out_all, contexts)
+    w_out_grad = lax.dot_general(
+        own_attended, after(branch, out_grad), (((0,), (0,)), ((), ())), preferred_element_type=jnp.float32
+    ).astype(jnp.bfloat16)
+    out_grad = lax.all_to_all(out_grad, "ctx", split_axis=0, concat_axis=0, tiled=True)
+    out_grad = out_grad.reshape(total, columns)
+    w_out_grad = fsdp_sum_low(
+        w_out_grad.reshape(contexts, splits * own_rows, width)
+    )
+    result_sum.send(out_grad)
+
+    query_scaled, key_scaled, value_grad, dots, query_gain_grad, key_gain_grad = attend_backward(
+        starts, query, key, key_t, value_t, out_grad, attended, log_rows, query_pre, key_pre, query_inv, key_inv, gain_query, gain_key, cosine, sine, size, prompt_rows, score_scale
+    )
+    dots = after(dots, result_sum.to_before, result_sum.to_after)
+    result_sum.prepare(result_terms, dots)
+    dots = sum_over_ctx(dots, contexts) / width
+    dots = after(dots, *result_sum.payload)
+    heads_grad = heads_grad_of(
+        query_scaled, key_scaled, value_grad, query_pre, key_pre, inverse, dots
+    )
+
+    def own_columns(grad):
+        return lax.dynamic_update_slice_in_dim(
+            jnp.zeros((width, 1), jnp.float32), grad, me * columns, 0
+        )
+
+    other_grads = jnp.concatenate(
+        [
+            ffn_gain_grad[:, None],
+            own_columns(query_gain_grad),
+            own_columns(key_gain_grad),
+            jnp.zeros((width, 125), jnp.float32),
+        ],
+        axis=1,
+    )
+    def term(offset, *earlier, **got):
+        at = after(owner(offset)[None], *earlier)
+        return hidden_term(at, heads_grad, w_t, w_out_grad, rows, **got)
+
+    down_w_grad = fsdp_sum(down_product)
+    hidden_sum = RingScatter(ring)
+    hidden_sum.payload = far = term(half)
+    hidden_sum.send()
+    result_sum.send(*far)
+    heads_product = heads_product_of(
+        heads_grad, hidden_all, after(other_grads, *far), contexts
+    )
+    heads_w_grad = fsdp_sum_low(after(heads_product, hidden_sum.to_before, hidden_sum.to_after))
+    done = (heads_product,)
+    for step in range(half - 1, 0, -1):
+        start = far[0].shape[0] if step == half - 1 else 0
+        if step == 1:
+            done = (result_sum.to_before, result_sum.to_after)
+        if step == half - 2:
+            done = (down_w_grad,)
+        hidden_sum.payload = (
+            term(-step, *done, got=hidden_sum.to_before),
+            term(step, *done, got=hidden_sum.to_after, start=start),
+        )
+        hidden_sum.send()
+        done = ()
+    hidden_grad, w_out_grad = own_term(
+        owner(0)[None], heads_grad, w_t, w_out_grad, rows, hidden_sum.to_before, hidden_sum.to_after
+    )
+    routed = result_sum.finish(result_terms[0])
+    output = (mixed + routed)[None]
+
+    heads_w_grad = lax.all_to_all(
+        heads_w_grad, "ctx", split_axis=0, concat_axis=0, tiled=True
+    ).astype(jnp.float32)
+    other_grads = jnp.sum(heads_w_grad[:, :, 3 * columns : 3 * columns + 3], axis=0)
+    heads_w_grad = jnp.transpose(
+        heads_w_grad[:, :, : 3 * columns].reshape(contexts, own_rows, 3, columns), (2, 1, 0, 3)
+    ).reshape(3, own_rows, width)
+
+    attn_gain_grad = jnp.sum(
+        w_query.astype(jnp.float32) * heads_w_grad[0]
+        + w_key.astype(jnp.float32) * heads_w_grad[1]
+        + w_value.astype(jnp.float32) * heads_w_grad[2],
+        axis=1,
+    ) / attn_gain.astype(jnp.float32)
+
+    attn_inv = lax.rsqrt(jnp.mean(inputs * inputs, axis=-1, keepdims=True) + EPSILON)
+    normed = inputs * attn_inv
+    scaled = hidden_grad * gain_attn
+    input_grad = mixed_grad + attn_inv * (
+        scaled - normed * jnp.mean(scaled * normed, axis=-1, keepdims=True)
+    )
+    return (
+        output,
+        input_grad[None],
+        attn_gain_grad,
+        other_grads[:, 1],
+        other_grads[:, 2],
+        other_grads[:, 0],
+        heads_w_grad[0],
+        heads_w_grad[1],
+        heads_w_grad[2],
+        w_out_grad,
+        gate_w_grad,
+        up_w_grad,
+        down_w_grad,
+    )
+
+
 def solution(mesh):
+    contexts = mesh.shape["ctx"]
+    fits = contexts == 8
     placed = (
         P("fsdp", "ctx", None),
         P("fsdp", "ctx", None),
@@ -463,7 +1725,7 @@
         P("ctx", "fsdp", None),
     )
     return jax.shard_map(
-        shards,
+        shards_by_heads if fits else shards_wide,
         mesh=mesh,
         in_specs=placed,
         out_specs=(

time: 4940 us -> 1450 us (0.29)
  waiting for transfers between devices: 3370 us -> 484 us
  matrix products: 810 us -> 102 us
  Pallas kernels: 0 us -> 573 us
  local copies, waits for them, and re-layouts: 434 us -> 63.6 us
  blocking collectives: 86.2 us -> 0 us
  other arithmetic: 168 us -> 100 us
  starting transfers between devices: 38.1 us -> 93.3 us
    all_to_all x4 -> x3, waiting for transfers between devices: 1510 us -> 75.8 us  [the longest x1 39 us: shards_by_heads(): lax.all_to_all(out_grad, 'ctx', split_axis=0, concat_axis=0, tiled=True)]
    reduce_scatter x9 -> x5, waiting for transfers between devices: 1280 us -> 0.05 us  [fsdp_sum_low(): return lax.psum_scatter(product, 'fsdp', scatter_dimension=1, tiled=True)]
    dot_general x43 -> x6, matrix products: 810 us -> 102 us  [the longest x3 85.8 us: weight_grad(): jnp.einsum('emd,emf->edf', left, right, preferred_element_type=jnp.float32)]
    pallas_call x0 -> x28, Pallas kernels: none -> 573 us  [the longest x10 312 us: experts_stage(): pl.pallas_call(partial(kernel, count=count, slots=slots, aliased=len(held...]
    all_gather x9 -> x5, waiting for transfers between devices: 579 us -> 23 us  [the longest x1 23 us: shards_by_heads(): gate_all = lax.all_gather(after(w_gate, pieces), 'fsdp', axis=1, tiled=True)]
    ppermute x0 -> x61, waiting for transfers between devices: none -> 382 us  [the longest x9 119 us: advance(): self.from_after = lax.ppermute(past, 'ctx', self.down)]
    unnamed x2 -> x0, blocking collectives: 86.2 us -> none
    dynamic_update_slice x12 -> x2, local copies, waits for them, and re-layouts: 85.1 us -> 0.94 us  [own_columns(): lax.dynamic_update_slice_in_dim(jnp.zeros((width, 1), jnp.float32), grad,...]
  transfers between devices with their start and end apart: 22 -> 74, of which waited for: 20 -> 30; matrix products, arithmetic and copies ran while one was open for 14% -> 14% of each run, Pallas kernels for 0% -> 37%
where the time goes in v1:
time: 1450 us; the launch traced here: 1430 us
  Pallas kernels  573 us (40%)
  waiting for transfers between devices  484 us (33%)
  matrix products  102 us (7%)
  other arithmetic  100 us (7%)
  starting transfers between devices  93.3 us (6%)
  local copies, waits for them, and re-layouts  63.6 us (4%)
  between operations  15.8 us (1%)
    pallas_call x10, Pallas kernels, experts_stage(): pl.pallas_call(partial(kernel, count=count, slots=slots, aliased=len(held...  312 us
    ppermute x9, waiting for transfers between devices, advance(): self.from_after = lax.ppermute(past, 'ctx', self.down)  119 us
    ppermute x12, waiting for transfers between devices, send(): self.to_after = lax.ppermute(past, 'ctx', self.up)  117 us
    ppermute x12, waiting for transfers between devices, send(): self.to_before = lax.ppermute(before, 'ctx', self.down)  87 us
    dot_general x3, matrix products, weight_grad(): jnp.einsum('emd,emf->edf', left, right, preferred_element_type=jnp.float32)  85.8 us
    pallas_call x1, Pallas kernels, attend_backward(): pl.pallas_call(partial(attend_backward_kernel, size=size, prompt_rows=pro...  76.2 us
    pallas_call x1, Pallas kernels, attend_forward(): pl.pallas_call(partial(attend_forward_kernel, size=size, prompt_rows=prom...  49.6 us
    pallas_call x7, Pallas kernels, hidden_term(): pl.pallas_call(partial(hidden_term_kernel, start=start, halves=halves), g...  41.9 us
  transfers between devices with their start and end apart: 74, of which 30 were waited for; matrix products, arithmetic and copies ran while one was open for 14% of the time, Pallas kernels for 37%

profile of v1, /device:TPU:14, one launch (start us, length us, event | category | flops | bytes accessed | tf_op | source)
XLA Modules:
  0.0 1431.9 jit_solution(245182544748650072)
XLA Ops:
  46.5 50.8 %collective-permute-done.4.refs_2_.refs_1_ = bf16[576,2048]{1,0:T(8,128)(2,1)S(1)} collective-permute-done((bf16[576,2048]{1,0:T(8,128)(2,1)S(1)}, bf16[576,2048]{1,0:T(8,128)(2,1)S(1)}, u32[]{:S(2)}, u32[]{:S(2)}) %collective-permute-start.4) | collective-permute-done | bytes 2359328 | tf_op jit(solution)/shard_map/ppermute | solution.py:1278
  99.4 50.5 %collective-permute-done.5.refs_4_.refs_2_ = bf16[576,2048]{1,0:T(8,128)(2,1)} collective-permute-done((bf16[576,2048]{1,0:T(8,128)(2,1)S(1)}, bf16[576,2048]{1,0:T(8,128)(2,1)}, u32[]{:S(2)}, u32[]{:S(2)}) %collective-permute-start.5) | collective-permute-done | bytes 2359328 | tf_op jit(solution)/shard_map/ppermute | solution.py:1278
  163.0 21.3 %project.3 = (bf16[4096,2048]{1,0:T(8,128)(2,1)}, f32[256,4096]{1,0:T(8,128)}, f32[256,4096]{1,0:T(8,128)}, bf16[256,4096]{1,0:T(8,128)(2,1)}, f32[2,4096]{1,0:T(2,128)}) custom-call(s32[5]{0:T(128)} %compare_select_fusion.12.places, bf16[576,2048]{1,0:T(8,128)(2,1)} %copy-done.7, bf16[576,2048]{1,0:T(8,128)(2,1)} %copy-done.12, ...), custom_call_target="tpu_custom_call" | custom-call | flops 8053063680 | bytes 30670848 | tf_op jit(solution)/shard_map/project/pallas_call | solution.py:825
  184.3 17.4 %collective-permute-done.6.refs_1_.refs_3_ = bf16[576,2048]{1,0:T(8,128)(2,1)} collective-permute-done((bf16[576,2048]{1,0:T(8,128)(2,1)}, bf16[576,2048]{1,0:T(8,128)(2,1)}, u32[]{:S(2)}, u32[]{:S(2)}) %collective-permute-start.6) | collective-permute-done | bytes 2359328 | tf_op jit(solution)/shard_map/ppermute | solution.py:1278
  208.6 21.3 %collective-permute-done.13 = bf16[288,2048]{1,0:T(8,128)(2,1)S(1)} collective-permute-done((bf16[288,2048]{1,0:T(8,128)(2,1)S(1)}, bf16[288,2048]{1,0:T(8,128)(2,1)S(1)}, u32[]{:S(2)}, u32[]{:S(2)}) %collective-permute-start.13) | collective-permute-done | bytes 1179680 | tf_op jit(solution)/shard_map/ppermute | solution.py:1283
  238.2 10.4 project.4
  248.6 6.7 project.5
  276.1 49.6 %attend_forward.1 = (bf16[4096,256]{1,0:T(8,128)(2,1)}, bf16[4096,256]{1,0:T(8,128)(2,1)}, bf16[4096,256]{1,0:T(8,128)(2,1)}, bf16[256,4096]{1,0:T(8,128)(2,1)}, f32[2,4096]{1,0:T(2,128)}) custom-call(s32[3]{0:T(128)} %bitcast_subtract_fusion.starts, f32[256,4096]{1,0:T(8,128)} %get-tuple-element.167.query_pre, f32[256,4096]{1,0:T(8,128)} %get-tuple-element.168.key_pre, ...), custom_call_target="tpu_custom_call" | custom-call | flops 25769803776 | bytes 20971520 | tf_op jit(solution)/shard_map/attend_forward/pallas_call | solution.py:597
  334.6 36.8 %all-to-all-done = bf16[8,512,256]{2,1,0:T(8,128)(2,1)} async-done(((bf16[8,512,256]{2,1,0:T(8,128)(2,1)}), bf16[8,512,256]{2,1,0:T(8,128)(2,1)}, u32[]{:S(2)}, u32[]{:S(2)}) %all-to-all-start) | async-done | bytes 2097184 | tf_op jit(solution)/shard_map/all_to_all | solution.py:1480
  371.4 7.7 multiply_reduce_fusion.2
  391.4 23.0 %all-gather.12.cloned.1.call-done.refs_3_.refs_4_ = bf16[2,2048,1024]{2,1,0:T(8,128)(2,1)} async-done(((bf16[2,512,1024]{2,1,0:T(8,128)(2,1)}), bf16[2,2048,1024]{2,1,0:T(8,128)(2,1)}) %all-gather.12.cloned.1.call-update) | async-done | bytes 8388624 | tf_op jit(solution)/shard_map/all_gather | solution.py:1429
  414.5 24.4 %experts_forward.5 = (bf16[2,2560,2048]{2,1,0:T(8,128)(2,1)}, bf16[2,2560,1024]{2,1,0:T(8,128)(2,1)}, bf16[2,320,1024]{2,1,0:T(8,128)(2,1)}, bf16[2,320,1024]{2,1,0:T(8,128)(2,1)}, bf16[512,2048]{1,0:T(8,128)(2,1)}) custom-call(s32[1,2,1,512]{3,2,1,0:T(1,128)} %get-tuple-element.179.refs_0_, f32[1,2,1,512]{3,2,1,0:T(1,128)} %get-tuple-element.328.refs_1_, ...), custom_call_target="tpu_custom_call" | custom-call | flops 10737418240 | bytes 33554432 | tf_op jit(solution)/shard_map/experts_forward/pallas_call | solution.py:1228
  438.9 22.7 %experts_backward.5 = (bf16[2,2560,2048]{2,1,0:T(8,128)(2,1)}, bf16[2,2560,1024]{2,1,0:T(8,128)(2,1)}, bf16[2,2560,1024]{2,1,0:T(8,128)(2,1)}, bf16[512,2048]{1,0:T(8,128)(2,1)}) custom-call(s32[1,2,1,512]{3,2,1,0:T(1,128)} %get-tuple-element.179.refs_0_, f32[1,2,1,512]{3,2,1,0:T(1,128)} %get-tuple-element.328.refs_1_, bf16[512,2048]{1,0:T(8,128)(2,1)} %bitcast.158, ...), custom_call_target="tpu_custom_call" | custom-call | tf_op jit(solution)/shard_map/experts_backward/pallas_call | solution.py:1228
  466.6 36.9 %experts_forward.6 = (bf16[2,2560,2048]{2,1,0:T(8,128)(2,1)}, bf16[2,2560,1024]{2,1,0:T(8,128)(2,1)}, bf16[2,640,1024]{2,1,0:T(8,128)(2,1)}, bf16[2,640,1024]{2,...) custom-call(s32[2,2,1,512]{3,2,1,0:T(1,128)} %pad_add_fusion.2.refs_, ...), custom_call_target="tpu_custom_call", output_to_operand_aliasing={{0}: (7, {}), {1}: (8, {})} | custom-call | flops 21474836480 | bytes 41943040 | tf_op jit(solution)/shard_map/experts_forward/pallas_call | solution.py:1228
  503.5 35.5 %experts_backward.6 = (bf16[2,2560,2048]{2,1,0:T(8,128)(2,1)}, bf16[2,2560,1024]{2,1,0:T(8,128)(2,1)}, bf16[2,2560,1024]{2,1,0:T(8,128)(2,1)}, bf16[512,2048]{1,0:T(8,128)(2,1)}, bf16[512,2048]{1,0:T(8,128)(2,1)}) custom-call(s32[2,2,1,512]{3,2,1,0:T(1,128)} %pad_add_fusion.2.refs_0_, ...), custom_call_target="tpu_custom_call", output_to_operand_aliasing={{0}: (9, {}), {1}: (10, {}), {2}: (11, {})} | custom-call | tf_op jit(solution)/shard_map/experts_backward/pallas_call | solution.py:1228
  539.1 15.7 %collective-permute-done.26.refs_2_ = bf16[512,2048]{1,0:T(8,128)(2,1)} collective-permute-done((bf16[512,2048]{1,0:T(8,128)(2,1)}, bf16[512,2048]{1,0:T(8,128)(2,1)}, u32[]{:S(2)}, u32[]{:S(2)}) %collective-permute-start.26) | collective-permute-done | bytes 2097184 | tf_op jit(solution)/shard_map/ppermute | solution.py:1277
  561.6 37.2 %experts_forward.7 = (bf16[2,2560,2048]{2,1,0:T(8,128)(2,1)}, bf16[2,2560,1024]{2,1,0:T(8,128)(2,1)}, bf16[2,640,1024]{2,1,0:T(8,128)(2,1)}, bf16[2,640,1024]{2,...) custom-call(s32[2,2,1,512]{3,2,1,0:T(1,128)} %pad_add_fusion.1.refs_, ...), custom_call_target="tpu_custom_call", output_to_operand_aliasing={{0}: (7, {}), {1}: (8, {})} | custom-call | flops 21474836480 | bytes 41943040 | tf_op jit(solution)/shard_map/experts_forward/pallas_call | solution.py:1228
  598.8 36.0 %experts_backward.7 = (bf16[2,2560,2048]{2,1,0:T(8,128)(2,1)}, bf16[2,2560,1024]{2,1,0:T(8,128)(2,1)}, bf16[2,2560,1024]{2,1,0:T(8,128)(2,1)}, bf16[512,2048]{1,0:T(8,128)(2,1)}, bf16[512,2048]{1,0:T(8,128)(2,1)}) custom-call(s32[2,2,1,512]{3,2,1,0:T(1,128)} %pad_add_fusion.1.refs_0_, ...), custom_call_target="tpu_custom_call", output_to_operand_aliasing={{0}: (9, {}), {1}: (10, {}), {2}: (11, {})} | custom-call | tf_op jit(solution)/shard_map/experts_backward/pallas_call | solution.py:1228
  642.7 37.1 %experts_forward.8 = (bf16[2,2560,2048]{2,1,0:T(8,128)(2,1)}, bf16[2,2560,1024]{2,1,0:T(8,128)(2,1)}, bf16[2,640,1024]{2,1,0:T(8,128)(2,1)}, bf16[2,640,1024]{2,...) custom-call(s32[2,2,1,512]{3,2,1,0:T(1,128)} %pad_add_fusion.refs_0_, ...), custom_call_target="tpu_custom_call", output_to_operand_aliasing={{0}: (7, {}), {1}: (8, {})} | custom-call | flops 21474836480 | bytes 41943040 | tf_op jit(solution)/shard_map/experts_forward/pallas_call | solution.py:1228
  683.0 24.2 %experts_forward.9 = (bf16[2,2560,2048]{2,1,0:T(8,128)(2,1)}, bf16[2,2560,1024]{2,1,0:T(8,128)(2,1)}, bf16[2,320,1024]{2,1,0:T(8,128)(2,1)}, bf16[2,320,1024]{2,1,0:T(8,128)(2,1)}, bf16[512,2048]{1,0:T(8,128)(2,1)}) custom-call(s32[1,2,1,512]{3,2,1,0:T(1,128)} %get-tuple-element.224.refs_0_, ...), custom_call_target="tpu_custom_call", output_to_operand_aliasing={{0}: (6, {}), {1}: (7, {})} | custom-call | flops 10737418240 | bytes 33554432 | tf_op jit(solution)/shard_map/experts_forward/pallas_call | solution.py:1228
  716.6 22.6 %experts_backward.8 = (bf16[2,2560,2048]{2,1,0:T(8,128)(2,1)}, bf16[2,2560,1024]{2,1,0:T(8,128)(2,1)}, bf16[2,2560,1024]{2,1,0:T(8,128)(2,1)}, bf16[512,2048]{1,0:T(8,128)(2,1)}) custom-call(s32[1,2,1,512]{3,2,1,0:T(1,128)} %get-tuple-element.224.refs_0_, ...), custom_call_target="tpu_custom_call", output_to_operand_aliasing={{0}: (8, {}), {1}: (9, {}), {2}: (10, {})} | custom-call | flops 10737418240 | bytes 33554432 | tf_op jit(solution)/shard_map/experts_backward/pallas_call | solution.py:1228
  750.6 35.5 %experts_backward.9 = (bf16[2,2560,2048]{2,1,0:T(8,128)(2,1)}, bf16[2,2560,1024]{2,1,0:T(8,128)(2,1)}, bf16[2,2560,1024]{2,1,0:T(8,128)(2,1)}, bf16[512,2048]{1,0:T(8,128)(2,1)}, bf16[512,2048]{1,0:T(8,128)(2,1)}) custom-call(s32[2,2,1,512]{3,2,1,0:T(1,128)} %pad_add_fusion.refs_0_, ...), custom_call_target="tpu_custom_call", output_to_operand_aliasing={{0}: (9, {}), {1}: (10, {}), {2}: (11, {})} | custom-call | flops 21474836480 | bytes 41943040 | tf_op jit(solution)/shard_map/experts_backward/pallas_call | solution.py:1228
  788.2 23.5 %collective-permute-done.37 = bf16[256,2048]{1,0:T(8,128)(2,1)} collective-permute-done((bf16[256,2048]{1,0:T(8,128)(2,1)}, bf16[256,2048]{1,0:T(8,128)(2,1)}, u32[]{:S(2)}, u32[]{:S(2)}) %collective-permute-start.37) | collective-permute-done | bytes 1048608 | tf_op jit(solution)/shard_map/ppermute | solution.py:1322
  820.7 26.6 %convolution_convert_fusion.3 = bf16[2,2048,1024]{2,1,0:T(8,128)(2,1)} fusion(bf16[2,2560,2048]{2,1,0:T(8,128)(2,1)} %get-tuple-element.250, bf16[2,2560,1024]{2,1,0:T(8,128)(2,1)S(1)} %copy-done), kind=kOutput, calls=%fused_computation.7 | convolution fusion | flops 21479030784 | bytes 39845888 | tf_op jit(solution)/shard_map/emd,emf->edf/dot_general | solution.py:1540
  847.3 15.1 %collective-permute-done.42 = bf16[512,2048]{1,0:T(8,128)(2,1)} collective-permute-done((bf16[512,2048]{1,0:T(8,128)(2,1)}, bf16[512,2048]{1,0:T(8,128)(2,1)}, u32[]{:S(2)}, u32[]{:S(2)}) %collective-permute-start.42) | collective-permute-done | bytes 2097184 | tf_op jit(solution)/shard_map/ppermute | solution.py:1323
  872.1 29.5 %convolution_convert_fusion.2 = bf16[2,2048,1024]{2,1,0:T(8,128)(2,1)} fusion(bf16[2,2560,2048]{2,1,0:T(8,128)(2,1)} %get-tuple-element.250, bf16[2,2560,1024]{2,1,0:T(8,128)(2,1)} %get-tuple-element.251), kind=kOutput, calls=%fused_computation.6 | convolution fusion | flops 21479030784 | bytes 39845888 | tf_op jit(solution)/shard_map/emd,emf->edf/dot_general | solution.py:1540
  901.6 7.2 collective-permute-done.43
  924.3 29.7 %convolution_convert_fusion.1 = bf16[2,1024,2048]{2,1,0:T(8,128)(2,1)} fusion(bf16[2,2560,1024]{2,1,0:T(8,128)(2,1)} %get-tuple-element.257, bf16[2,2560,2048]{2,1,0:T(8,128)(2,1)} %get-tuple-element.258), kind=kOutput, calls=%fused_computation.5 | convolution fusion | flops 21479030784 | bytes 39845888 | tf_op jit(solution)/shard_map/emd,emf->edf/dot_general | solution.py:1540
  963.4 5.8 fusion.31
  969.2 10.7 out_grad.1
  980.0 8.3 convolution_convert_fusion
  990.5 6.4 all-to-all-start.1
  997.4 39.0 %all-to-all-done.1 = bf16[8,512,256]{2,1,0:T(8,128)(2,1)} async-done(((bf16[8,512,256]{2,1,0:T(8,128)(2,1)}), bf16[8,512,256]{2,1,0:T(8,128)(2,1)}, u32[]{:S(2)}, u32[]{:S(2)}) %all-to-all-start.1) | async-done | bytes 2097184 | tf_op jit(solution)/shard_map/all_to_all | solution.py:1604
  1038.5 76.2 %attend_backward.1 = (f32[256,4096]{1,0:T(8,128)}, f32[256,4096]{1,0:T(8,128)}, bf16[256,4096]{1,0:T(8,128)(2,1)}, f32[2,4096]{1,0:T(2,128)}, f32[256,1]{1,0:T(8,128)}, /*index=5*/f32[256,1]{1,0:T(8,128)}) custom-call(s32[3]{0:T(128)} %bitcast_subtract_fusion.starts, bf16[4096,256]{1,0:T(8,128)(2,1)} %get-tuple-element.262.query, ...), custom_call_target="tpu_custom_call" | custom-call | flops 51539607552 | bytes 41943040 | tf_op jit(solution)/shard_map/attend_backward/pallas_call | solution.py:759
  1131.8 9.8 heads_grad.1
  1149.2 21.1 %heads_product.1 = bf16[8,256,896]{2,1,0:T(8,128)(2,1)} custom-call(bf16[768,4096]{1,0:T(8,128)(2,1)} %heads_grad.1, bf16[4096,2048]{1,0:T(8,128)(2,1)} %get-tuple-element.282.hidden, f32[2048,128]{1,0:T(8,128)} %maximum_maximum_fusion.others), custom_call_target="tpu_custom_call" | custom-call | flops 12884901888 | bytes 23068672 | tf_op jit(solution)/shard_map/heads_product/pallas_call | solution.py:1049
  1179.5 5.7 hidden_term.11
  1190.1 33.0 %collective-permute-done.54.refs_0_ = bf16[576,2048]{1,0:T(8,128)(2,1)S(1)} collective-permute-done((bf16[576,2048]{1,0:T(8,128)(2,1)}, bf16[576,2048]{1,0:T(8,128)(2,1)S(1)}, u32[]{:S(2)}, u32[]{:S(2)}) %collective-permute-start.54) | collective-permute-done | bytes 2359328 | tf_op jit(solution)/shard_map/ppermute | solution.py:1322
  1224.6 6.8 hidden_term.9
  1231.6 6.1 hidden_term.12
  1242.0 86.5 %collective-permute-done.52 = bf16[512,2048]{1,0:T(8,128)(2,1)} collective-permute-done((bf16[512,2048]{1,0:T(8,128)(2,1)}, bf16[512,2048]{1,0:T(8,128)(2,1)}, u32[]{:S(2)}, u32[]{:S(2)}) %collective-permute-start.52) | collective-permute-done | bytes 2097184 | tf_op jit(solution)/shard_map/ppermute | solution.py:1323
  1330.0 6.0 hidden_term.10
  1337.3 6.0 hidden_term.13
  1353.5 5.7 add_bitcast_fusion
  1359.2 6.2 all-to-all-start.2
  1365.5 26.3 %collective-permute-done.56.before = bf16[576,2048]{1,0:T(8,128)(2,1)} collective-permute-done((bf16[576,2048]{1,0:T(8,128)(2,1)}, bf16[576,2048]{1,0:T(8,128)(2,1)}, u32[]{:S(2)}, u32[]{:S(2)}) %collective-permute-start.56) | collective-permute-done | bytes 2359328 | tf_op jit(solution)/shard_map/ppermute | solution.py:1322
  1391.8 8.4 collective-permute-done.60.past
  1400.2 7.0 own_term.1
  (406 shorter events, 279.6 us)
Async XLA Ops:
  7.2 145.3 %all-gather.6.cloned.1.call-start = ((), (), s32[]{:S(2)}) async-start(), calls=%async_computation.8 | async-start | bytes 4587520 | tf_op jit(solution)/shard_map/all_gather | solution.py:1430
  43.1 160.0 %all-gather.8.cloned.1.call-start = ((), (), s32[]{:S(2)}) async-start(), calls=%async_computation.9 | async-start | bytes 10485760 | tf_op jit(solution)/shard_map/all_gather | solution.py:1431
  43.9 327.5 %all-gather.10.cloned.1.call-start = ((), (), s32[]{:S(2)}) async-start(), calls=%async_computation.10 | async-start | bytes 10485760 | tf_op jit(solution)/shard_map/all_gather | solution.py:1467
  44.1 53.2 %collective-permute-start.4 = (bf16[576,2048]{1,0:T(8,128)(2,1)S(1)}, bf16[576,2048]{1,0:T(8,128)(2,1)S(1)}, u32[]{:S(2)}, u32[]{:S(2)}) collective-permute-start(bf16[576,2048]{1,0:T(8,128)(2,1)S(1)} %pad_maximum_fusion.refs_0_), channel_id=1, source_target_pairs={{8,0},{16,8},{24,16},{28,24},{20,28},{12,20},{4,12},{0,4},{9,1},{1... | collective-permute-start | bytes 7077896 | tf_op jit(solution)/shard_map/ppermute | solution.py:1278
  45.5 53.2 %collective-permute-start.1 = (bf16[576,2048]{1,0:T(8,128)(2,1)S(1)}, bf16[576,2048]{1,0:T(8,128)(2,1)S(1)}, u32[]{:S(2)}, u32[]{:S(2)}) collective-permute-start(bf16[576,2048]{1,0:T(8,128)(2,1)S(1)} %pad_maximum_fusion.refs_0_), channel_id=1, source_target_pairs={{0,8},{8,16},{16,24},{24,28},{28,20},{20,12},{12,4},{4,0},{1,9},{9... | collective-permute-start | bytes 7077896 | tf_op jit(solution)/shard_map/ppermute | solution.py:1277
  97.4 52.5 %collective-permute-start.5 = (bf16[576,2048]{1,0:T(8,128)(2,1)S(1)}, bf16[576,2048]{1,0:T(8,128)(2,1)}, u32[]{:S(2)}, u32[]{:S(2)}) collective-permute-start(bf16[576,2048]{1,0:T(8,128)(2,1)S(1)} %collective-permute-done.4.refs_2_.refs_1_), channel_id=1, source_target_pairs={{8,0},{16,8},{24,16},{28,24},{20,28},{12,20},{4,12},{0,4},{9,1},{1... | collective-permute-start | bytes 7077896 | tf_op jit(solution)/shard_map/ppermute | solution.py:1278
  98.8 52.5 %collective-permute-start.2 = (bf16[576,2048]{1,0:T(8,128)(2,1)S(1)}, bf16[576,2048]{1,0:T(8,128)(2,1)}, u32[]{:S(2)}, u32[]{:S(2)}) collective-permute-start(bf16[576,2048]{1,0:T(8,128)(2,1)S(1)} %collective-permute-done.1.refs_1_.refs_7_), channel_id=1, source_target_pairs={{0,8},{8,16},{16,24},{24,28},{28,20},{20,12},{12,4},{4,0},{1,9},{9... | collective-permute-start | bytes 7077896 | tf_op jit(solution)/shard_map/ppermute | solution.py:1277
  149.9 51.8 %collective-permute-start.6 = (bf16[576,2048]{1,0:T(8,128)(2,1)}, bf16[576,2048]{1,0:T(8,128)(2,1)}, u32[]{:S(2)}, u32[]{:S(2)}) collective-permute-start(bf16[576,2048]{1,0:T(8,128)(2,1)} %collective-permute-done.5.refs_4_.refs_2_), channel_id=1, source_target_pairs={{8,0},{16,8},{24,16},{28,24},{20,28},{12,20},{4,12},{0,4},{9,1},{1... | collective-permute-start | bytes 7077896 | tf_op jit(solution)/shard_map/ppermute | solution.py:1278
  151.3 51.8 %collective-permute-start.3 = (bf16[576,2048]{1,0:T(8,128)(2,1)}, bf16[576,2048]{1,0:T(8,128)(2,1)}, u32[]{:S(2)}, u32[]{:S(2)}) collective-permute-start(bf16[576,2048]{1,0:T(8,128)(2,1)} %collective-permute-done.2.refs_3_.refs_6_), channel_id=1, source_target_pairs={{0,8},{8,16},{16,24},{24,28},{28,20},{20,12},{12,4},{4,0},{1,9},{9... | collective-permute-start | bytes 7077896 | tf_op jit(solution)/shard_map/ppermute | solution.py:1277
  236.5 155.0 %all-gather.14.cloned.1.call-start = ((), (), s32[]{:S(2)}) async-start(), calls=%async_computation.12 | async-start | bytes 10485760 | tf_op jit(solution)/shard_map/all_gather | solution.py:1468
  237.1 177.4 %all-gather.12.cloned.1.call-start = ((), (), s32[]{:S(2)}) async-start(), calls=%async_computation.11 | async-start | bytes 10485760 | tf_op jit(solution)/shard_map/all_gather | solution.py:1429
  273.3 52.4 %collective-permute-start.18 = (bf16[512,2048]{1,0:T(8,128)(2,1)}, bf16[512,2048]{1,0:T(8,128)(2,1)}, u32[]{:S(2)}, u32[]{:S(2)}) collective-permute-start(bf16[512,2048]{1,0:T(8,128)(2,1)} %bitcast.156), channel_id=1, source_target_pairs={{0,8},{8,16},{16,24},{24,28},{28,20},{20,12},{12,4},{4,0},{1,9},{9... | collective-permute-start | bytes 6291464 | tf_op jit(solution)/shard_map/ppermute | solution.py:1277
  274.3 51.4 %collective-permute-start.19 = (bf16[512,2048]{1,0:T(8,128)(2,1)}, bf16[512,2048]{1,0:T(8,128)(2,1)}, u32[]{:S(2)}, u32[]{:S(2)}) collective-permute-start(bf16[512,2048]{1,0:T(8,128)(2,1)} %bitcast.157), channel_id=1, source_target_pairs={{8,0},{16,8},{24,16},{28,24},{20,28},{12,20},{4,12},{0,4},{9,1},{1... | collective-permute-start | bytes 6291464 | tf_op jit(solution)/shard_map/ppermute | solution.py:1278
  325.7 45.7 %all-to-all-start = ((bf16[8,512,256]{2,1,0:T(8,128)(2,1)}), bf16[8,512,256]{2,1,0:T(8,128)(2,1)}, u32[]{:S(2)}, u32[]{:S(2)}) async-start(bf16[8,512,256]{2,1,0:T(8,128)(2,1)} %bitcast.169), calls=%async_computation | async-start | bytes 4194304 | tf_op jit(solution)/shard_map/all_to_all | solution.py:1480
  330.6 811.0 %reduce-scatter.6.cloned.1.call-start = ((), (), s32[]{:S(2)}) async-start(), calls=%async_computation.13 | async-start | bytes 10485760 | tf_op jit(solution)/shard_map/reduce_scatter | solution.py:1584
  332.5 106.4 %collective-permute-start.20 = (bf16[512,2048]{1,0:T(8,128)(2,1)}, bf16[512,2048]{1,0:T(8,128)(2,1)}, u32[]{:S(2)}, u32[]{:S(2)}) collective-permute-start(bf16[512,2048]{1,0:T(8,128)(2,1)} %collective-permute-done.18.refs_2_), channel_id=1, source_target_pairs={{0,8},{8,16},{16,24},{24,28},{28,20},{20,12},{12,4},{4,0},{1,9},{9... | collective-permute-start | bytes 6291464 | tf_op jit(solution)/shard_map/ppermute | solution.py:1277
  333.1 105.8 %collective-permute-start.21 = (bf16[512,2048]{1,0:T(8,128)(2,1)}, bf16[512,2048]{1,0:T(8,128)(2,1)}, u32[]{:S(2)}, u32[]{:S(2)}) collective-permute-start(bf16[512,2048]{1,0:T(8,128)(2,1)} %collective-permute-done.19.refs_3_), channel_id=1, source_target_pairs={{8,0},{16,8},{24,16},{28,24},{20,28},{12,20},{4,12},{0,4},{9,1},{1... | collective-permute-start | bytes 6291464 | tf_op jit(solution)/shard_map/ppermute | solution.py:1278
  381.2 80.5 %collective-permute-start.22 = (bf16[512,2048]{1,0:T(8,128)(2,1)S(1)}, bf16[512,2048]{1,0:T(8,128)(2,1)}, u32[]{:S(2)}, u32[]{:S(2)}) collective-permute-start(bf16[512,2048]{1,0:T(8,128)(2,1)S(1)} %multiply_convert_fusion.refs_2_), channel_id=1, source_target_pairs={{0,8},{8,16},{16,24},{24,28},{28,20},{20,12},{12,4},{4,0},{1,9},{9... | collective-permute-start | bytes 6291464 | tf_op jit(solution)/shard_map/ppermute | solution.py:1277
  386.7 74.9 %collective-permute-start.23 = (bf16[512,2048]{1,0:T(8,128)(2,1)S(1)}, bf16[512,2048]{1,0:T(8,128)(2,1)}, u32[]{:S(2)}, u32[]{:S(2)}) collective-permute-start(bf16[512,2048]{1,0:T(8,128)(2,1)S(1)} %multiply_convert_fusion.refs_2_), channel_id=1, source_target_pairs={{8,0},{16,8},{24,16},{28,24},{20,28},{12,20},{4,12},{0,4},{9,1},{1... | collective-permute-start | bytes 6291464 | tf_op jit(solution)/shard_map/ppermute | solution.py:1278
  461.7 77.3 %collective-permute-start.24 = (bf16[512,2048]{1,0:T(8,128)(2,1)}, bf16[512,2048]{1,0:T(8,128)(2,1)S(1)}, u32[]{:S(2)}, u32[]{:S(2)}) collective-permute-start(bf16[512,2048]{1,0:T(8,128)(2,1)} %collective-permute-done.20.refs_2_), channel_id=1, source_target_pairs={{0,8},{8,16},{16,24},{24,28},{28,20},{20,12},{12,4},{4,0},{1,9},{9... | collective-permute-start | bytes 6291464 | tf_op jit(solution)/shard_map/ppermute | solution.py:1277
  462.3 76.8 %collective-permute-start.25 = (bf16[512,2048]{1,0:T(8,128)(2,1)}, bf16[512,2048]{1,0:T(8,128)(2,1)}, u32[]{:S(2)}, u32[]{:S(2)}) collective-permute-start(bf16[512,2048]{1,0:T(8,128)(2,1)} %collective-permute-done.21.refs_3_), channel_id=1, source_target_pairs={{8,0},{16,8},{24,16},{28,24},{20,28},{12,20},{4,12},{0,4},{9,1},{1... | collective-permute-start | bytes 6291464 | tf_op jit(solution)/shard_map/ppermute | solution.py:1278
  463.8 91.0 %collective-permute-start.26 = (bf16[512,2048]{1,0:T(8,128)(2,1)}, bf16[512,2048]{1,0:T(8,128)(2,1)}, u32[]{:S(2)}, u32[]{:S(2)}) collective-permute-start(bf16[512,2048]{1,0:T(8,128)(2,1)} %collective-permute-done.22.refs_2_), channel_id=1, source_target_pairs={{0,8},{8,16},{16,24},{24,28},{28,20},{20,12},{12,4},{4,0},{1,9},{9... | collective-permute-start | bytes 6291464 | tf_op jit(solution)/shard_map/ppermute | solution.py:1277
  464.3 90.7 %collective-permute-start.27 = (bf16[512,2048]{1,0:T(8,128)(2,1)}, bf16[512,2048]{1,0:T(8,128)(2,1)}, u32[]{:S(2)}, u32[]{:S(2)}) collective-permute-start(bf16[512,2048]{1,0:T(8,128)(2,1)} %collective-permute-done.23.refs_3_), channel_id=1, source_target_pairs={{8,0},{16,8},{24,16},{28,24},{20,28},{12,20},{4,12},{0,4},{9,1},{1... | collective-permute-start | bytes 6291464 | tf_op jit(solution)/shard_map/ppermute | solution.py:1278
  555.1 79.6 %collective-permute-start.28 = (bf16[256,2048]{1,0:T(8,128)(2,1)S(1)}, bf16[256,2048]{1,0:T(8,128)(2,1)}, u32[]{:S(2)}, u32[]{:S(2)}) collective-permute-start(bf16[256,2048]{1,0:T(8,128)(2,1)S(1)} %slice.260), channel_id=1, source_target_pairs={{0,8},{8,16},{16,24},{24,28},{28,20},{20,12},{12,4},{4,0},{1,9},{9... | collective-permute-start | bytes 3145736 | tf_op jit(solution)/shard_map/ppermute | solution.py:1283
  557.8 78.2 %collective-permute-start.29 = (bf16[256,2048]{1,0:T(8,128)(2,1)}, bf16[256,2048]{1,0:T(8,128)(2,1)S(1)}, u32[]{:S(2)}, u32[]{:S(2)}) collective-permute-start(bf16[256,2048]{1,0:T(8,128)(2,1)} %slice.261), channel_id=1, source_target_pairs={{8,0},{16,8},{24,16},{28,24},{20,28},{12,20},{4,12},{0,4},{9,1},{1... | collective-permute-start | bytes 3145736 | tf_op jit(solution)/shard_map/ppermute | solution.py:1284
  559.6 76.6 %collective-permute-start.30 = (bf16[512,2048]{1,0:T(8,128)(2,1)}, bf16[512,2048]{1,0:T(8,128)(2,1)}, u32[]{:S(2)}, u32[]{:S(2)}) collective-permute-start(bf16[512,2048]{1,0:T(8,128)(2,1)} %collective-permute-done.26.refs_2_), channel_id=1, source_target_pairs={{0,8},{8,16},{16,24},{24,28},{28,20},{20,12},{12,4},{4,0},{1,9},{9... | collective-permute-start | bytes 6291464 | tf_op jit(solution)/shard_map/ppermute | solution.py:1277
  559.9 76.3 %collective-permute-start.31 = (bf16[512,2048]{1,0:T(8,128)(2,1)}, bf16[512,2048]{1,0:T(8,128)(2,1)}, u32[]{:S(2)}, u32[]{:S(2)}) collective-permute-start(bf16[512,2048]{1,0:T(8,128)(2,1)} %collective-permute-done.27.refs_3_), channel_id=1, source_target_pairs={{8,0},{16,8},{24,16},{28,24},{20,28},{12,20},{4,12},{0,4},{9,1},{1... | collective-permute-start | bytes 6291464 | tf_op jit(solution)/shard_map/ppermute | solution.py:1278
  744.5 74.9 %collective-permute-start.36 = (bf16[512,2048]{1,0:T(8,128)(2,1)}, bf16[512,2048]{1,0:T(8,128)(2,1)S(1)}, u32[]{:S(2)}, u32[]{:S(2)}) collective-permute-start(bf16[512,2048]{1,0:T(8,128)(2,1)} %pad_maximum_fusion.2), channel_id=1, source_target_pairs={{8,0},{16,8},{24,16},{28,24},{20,28},{12,20},{4,12},{0,4},{9,1},{1... | collective-permute-start | bytes 6291464 | tf_op jit(solution)/shard_map/ppermute | solution.py:1322
  748.1 71.4 %collective-permute-start.39 = (bf16[512,2048]{1,0:T(8,128)(2,1)}, bf16[512,2048]{1,0:T(8,128)(2,1)}, u32[]{:S(2)}, u32[]{:S(2)}) collective-permute-start(bf16[512,2048]{1,0:T(8,128)(2,1)} %pad_maximum_fusion.3), channel_id=1, source_target_pairs={{0,8},{8,16},{16,24},{24,28},{28,20},{20,12},{12,4},{4,0},{1,9},{9... | collective-permute-start | bytes 6291464 | tf_op jit(solution)/shard_map/ppermute | solution.py:1323
  748.6 63.1 %collective-permute-start.37 = (bf16[256,2048]{1,0:T(8,128)(2,1)}, bf16[256,2048]{1,0:T(8,128)(2,1)}, u32[]{:S(2)}, u32[]{:S(2)}) collective-permute-start(bf16[256,2048]{1,0:T(8,128)(2,1)} %get-tuple-element.308), channel_id=1, source_target_pairs={{8,0},{16,8},{24,16},{28,24},{20,28},{12,20},{4,12},{0,4},{9,1},{1... | collective-permute-start | bytes 3145736 | tf_op jit(solution)/shard_map/ppermute | solution.py:1322
  750.1 66.4 %collective-permute-start.40 = (bf16[256,2048]{1,0:T(8,128)(2,1)}, bf16[256,2048]{1,0:T(8,128)(2,1)S(1)}, u32[]{:S(2)}, u32[]{:S(2)}) collective-permute-start(bf16[256,2048]{1,0:T(8,128)(2,1)} %get-tuple-element.307), channel_id=1, source_target_pairs={{0,8},{8,16},{16,24},{24,28},{28,20},{20,12},{12,4},{4,0},{1,9},{9... | collective-permute-start | bytes 3145736 | tf_op jit(solution)/shard_map/ppermute | solution.py:1323
  815.0 51.6 %collective-permute-start.38 = (bf16[512,2048]{1,0:T(8,128)(2,1)}, bf16[512,2048]{1,0:T(8,128)(2,1)}, u32[]{:S(2)}, u32[]{:S(2)}) collective-permute-start(bf16[512,2048]{1,0:T(8,128)(2,1)} %pad_maximum_fusion.4), channel_id=1, source_target_pairs={{8,0},{16,8},{24,16},{28,24},{20,28},{12,20},{4,12},{0,4},{9,1},{1... | collective-permute-start | bytes 6291464 | tf_op jit(solution)/shard_map/ppermute | solution.py:1322
  988.3 197.6 %reduce-scatter.8.cloned.1.call-start = ((), (), s32[]{:S(2)}) async-start(), calls=%async_computation.14 | async-start | bytes 10485760 | tf_op jit(solution)/shard_map/reduce_scatter | solution.py:1584
  989.0 356.2 %reduce-scatter.12.cloned.1.call-start = ((), (), s32[]{:S(2)}) async-start(), calls=%async_computation.16 | async-start | bytes 10485760 | tf_op jit(solution)/shard_map/reduce_scatter | solution.py:1584
  989.8 359.5 %reduce-scatter.14.cloned.1.call-start = ((), (), s32[]{:S(2)}) async-start(), calls=%async_computation.17 | async-start | bytes 10485760 | tf_op jit(solution)/shard_map/reduce_scatter | solution.py:1584
  990.5 45.9 %all-to-all-start.1 = ((bf16[8,512,256]{2,1,0:T(8,128)(2,1)}), bf16[8,512,256]{2,1,0:T(8,128)(2,1)}, u32[]{:S(2)}, u32[]{:S(2)}) async-start(bf16[8,512,256]{2,1,0:T(8,128)(2,1)} %out_grad.1), calls=%async_computation.1 | async-start | bytes 4194304 | tf_op jit(solution)/shard_map/all_to_all | solution.py:1604
  997.0 362.3 %reduce-scatter.10.cloned.1.call-start = ((), (), s32[]{:S(2)}) async-start(), calls=%async_computation.15 | async-start | bytes 4587520 | tf_op jit(solution)/shard_map/reduce_scatter | solution.py:1584
  1036.5 79.4 %collective-permute-start.46 = (bf16[512,2048]{1,0:T(8,128)(2,1)}, bf16[512,2048]{1,0:T(8,128)(2,1)}, u32[]{:S(2)}, u32[]{:S(2)}) collective-permute-start(bf16[512,2048]{1,0:T(8,128)(2,1)} %add_convert_fusion.3), channel_id=1, source_target_pairs={{8,0},{16,8},{24,16},{28,24},{20,28},{12,20},{4,12},{0,4},{9,1},{1... | collective-permute-start | bytes 6291464 | tf_op jit(solution)/shard_map/ppermute | solution.py:1322
  1036.5 79.4 %collective-permute-start.47 = (bf16[512,2048]{1,0:T(8,128)(2,1)S(1)}, bf16[512,2048]{1,0:T(8,128)(2,1)}, u32[]{:S(2)}, u32[]{:S(2)}) collective-permute-start(bf16[512,2048]{1,0:T(8,128)(2,1)S(1)} %copy-done.22), channel_id=1, source_target_pairs={{0,8},{8,16},{16,24},{24,28},{28,20},{20,12},{12,4},{4,0},{1,9},{9... | collective-permute-start | bytes 6291464 | tf_op jit(solution)/shard_map/ppermute | solution.py:1323
  1177.0 46.2 %collective-permute-start.54 = (bf16[576,2048]{1,0:T(8,128)(2,1)}, bf16[576,2048]{1,0:T(8,128)(2,1)S(1)}, u32[]{:S(2)}, u32[]{:S(2)}) collective-permute-start(bf16[576,2048]{1,0:T(8,128)(2,1)} %hidden_term.8), channel_id=1, source_target_pairs={{8,0},{16,8},{24,16},{28,24},{20,28},{12,20},{4,12},{0,4},{9,1},{1... | collective-permute-start | bytes 7077896 | tf_op jit(solution)/shard_map/ppermute | solution.py:1322
  1185.2 46.4 %collective-permute-start.58 = (bf16[576,2048]{1,0:T(8,128)(2,1)}, bf16[576,2048]{1,0:T(8,128)(2,1)}, u32[]{:S(2)}, u32[]{:S(2)}) collective-permute-start(bf16[576,2048]{1,0:T(8,128)(2,1)} %hidden_term.11), channel_id=1, source_target_pairs={{0,8},{8,16},{16,24},{24,28},{28,20},{20,12},{12,4},{4,0},{1,9},{9... | collective-permute-start | bytes 7077896 | tf_op jit(solution)/shard_map/ppermute | solution.py:1323
  1231.4 97.2 %collective-permute-start.55 = (bf16[576,2048]{1,0:T(8,128)(2,1)}, bf16[576,2048]{1,0:T(8,128)(2,1)S(1)}, u32[]{:S(2)}, u32[]{:S(2)}) collective-permute-start(bf16[576,2048]{1,0:T(8,128)(2,1)} %hidden_term.9), channel_id=1, source_target_pairs={{8,0},{16,8},{24,16},{28,24},{20,28},{12,20},{4,12},{0,4},{9,1},{1... | collective-permute-start | bytes 7077896 | tf_op jit(solution)/shard_map/ppermute | solution.py:1322
  1237.7 99.5 %collective-permute-start.59 = (bf16[576,2048]{1,0:T(8,128)(2,1)}, bf16[576,2048]{1,0:T(8,128)(2,1)}, u32[]{:S(2)}, u32[]{:S(2)}) collective-permute-start(bf16[576,2048]{1,0:T(8,128)(2,1)} %hidden_term.12), channel_id=1, source_target_pairs={{0,8},{8,16},{16,24},{24,28},{28,20},{20,12},{12,4},{4,0},{1,9},{9... | collective-permute-start | bytes 7077896 | tf_op jit(solution)/shard_map/ppermute | solution.py:1323
  1240.0 88.6 %collective-permute-start.52 = (bf16[512,2048]{1,0:T(8,128)(2,1)}, bf16[512,2048]{1,0:T(8,128)(2,1)}, u32[]{:S(2)}, u32[]{:S(2)}) collective-permute-start(bf16[512,2048]{1,0:T(8,128)(2,1)} %add_convert_fusion), channel_id=1, source_target_pairs={{0,8},{8,16},{16,24},{24,28},{28,20},{20,12},{12,4},{4,0},{1,9},{9... | collective-permute-start | bytes 6291464 | tf_op jit(solution)/shard_map/ppermute | solution.py:1323
  1241.5 87.1 %collective-permute-start.51 = (bf16[512,2048]{1,0:T(8,128)(2,1)}, bf16[512,2048]{1,0:T(8,128)(2,1)}, u32[]{:S(2)}, u32[]{:S(2)}) collective-permute-start(bf16[512,2048]{1,0:T(8,128)(2,1)} %add_convert_fusion.1), channel_id=1, source_target_pairs={{8,0},{16,8},{24,16},{28,24},{20,28},{12,20},{4,12},{0,4},{9,1},{1... | collective-permute-start | bytes 6291464 | tf_op jit(solution)/shard_map/ppermute | solution.py:1322
  1336.0 55.8 %collective-permute-start.56 = (bf16[576,2048]{1,0:T(8,128)(2,1)}, bf16[576,2048]{1,0:T(8,128)(2,1)}, u32[]{:S(2)}, u32[]{:S(2)}) collective-permute-start(bf16[576,2048]{1,0:T(8,128)(2,1)} %hidden_term.10), channel_id=1, source_target_pairs={{8,0},{16,8},{24,16},{28,24},{20,28},{12,20},{4,12},{0,4},{9,1},{1... | collective-permute-start | bytes 7077896 | tf_op jit(solution)/shard_map/ppermute | solution.py:1322
  1343.3 56.9 %collective-permute-start.60 = (bf16[576,2048]{1,0:T(8,128)(2,1)}, bf16[576,2048]{1,0:T(8,128)(2,1)}, u32[]{:S(2)}, u32[]{:S(2)}) collective-permute-start(bf16[576,2048]{1,0:T(8,128)(2,1)} %hidden_term.13), channel_id=1, source_target_pairs={{0,8},{8,16},{16,24},{24,28},{28,20},{20,12},{12,4},{4,0},{1,9},{9... | collective-permute-start | bytes 7077896 | tf_op jit(solution)/shard_map/ppermute | solution.py:1323
  1359.2 56.7 %all-to-all-start.2 = ((bf16[8,64,896]{2,1,0:T(8,128)(2,1)}), bf16[8,64,896]{2,1,0:T(8,128)(2,1)S(1)}, u32[]{:S(2)}, u32[]{:S(2)}) async-start(bf16[8,64,896]{2,1,0:T(8,128)(2,1)} %reduce-scatter.10.cloned.1.call-done), calls=%async_computation.5 | async-start | bytes 1835008 | tf_op jit(solution)/shard_map/all_to_all | solution.py:1668
  (90 other events, 1510.0 us)
Sparse Core Ops, SparseCore 0:
  43.3 31.5 all-gather.5
  76.4 58.2 all-gather.7
  236.6 58.3 all-gather.9
  296.4 58.2 all-gather.13
  356.1 58.2 all-gather.11
  988.4 71.9 reduce-scatter.5
  1063.2 71.7 reduce-scatter.7
  1137.5 71.6 reduce-scatter.11
  1212.0 71.7 reduce-scatter.13
  1286.2 41.2 reduce-scatter.9

commit v2 on v1

--- a/solution.py
+++ b/solution.py
@@ -640,20 +640,13 @@
     key_gain,
     cosine,
     sine,
-    query_scaled,
-    key_scaled,
-    value_grad,
-    dots,
-    query_gain_grad,
-    key_gain_grad,
-    query_sum,
-    key_sum,
-    row_dot,
-    *,
+    *refs,
     size,
     prompt_rows,
     score_scale,
 ):
+    query_scaled, key_scaled, value_grad, query_gain_grad, key_gain_grad, dots = refs[-9:-3]
+    query_sum, key_sum, row_dot = refs[-3:]
     j = pl.program_id(0)
     half = HEAD // 2
     total, columns = key.shape
@@ -690,7 +683,7 @@
             prob_grads = [dot_nt(v, g) for v, g in zip(value_rows, grad_rows)]
             for h, span in enumerate(spans):
                 key_part, value_part = made[h]
-                prob = jnp.exp2(scores[h] - log_rows[h : h + 1, at])
+                prob = jnp.exp2(scores[h] - log_rows[h, :, at])
                 if masked:
                     prob = jnp.where(allowed[:, c * chunk : (c + 1) * chunk], prob, 0.0)
                 score_grad = (prob * (prob_grads[h] - row_dot[h : h + 1, at])).astype(jnp.bfloat16)
@@ -746,46 +739,46 @@
                 dots[place : place + 1, at] = summed
 
 
-def attend_backward(starts, query, key, key_t, value_t, out_grad, out, log_rows, query_pre, key_pre, query_inv, key_inv, query_gain, key_gain, cosine, sine, size, prompt_rows, score_scale):
+def attend_backward(starts, head, held, query, key, key_t, value_t, out_grad, out, log_rows, query_pre, key_pre, query_inv, key_inv, query_gain, key_gain, cosine, sine, size, prompt_rows, score_scale):
     columns, total = query_pre.shape
-    heads = columns // HEAD
     pairs = total * total // 2
-
-    def once(shape):
-        return pl.BlockSpec(shape, lambda j, s: (0, 0), pipeline_mode=pl.Buffered(1))
-
-    wide, tall, row = (columns, total), (total, columns), (1, total)
-    gain, table, per_head = (columns, 1), (HEAD // 2, total), (heads, total)
+    held = () if held is None else tuple(held)
+
+    def once(shape, index):
+        return pl.BlockSpec(shape, lambda j, s: index, pipeline_mode=pl.Buffered(1))
+
+    wide, tall = once((HEAD, total), (head, 0)), once((total, HEAD), (0, head))
+    row, table = once((1, total), (0, 0)), once((HEAD // 2, total), (0, 0))
+    gain, per_head = once((HEAD, 1), (head, 0)), once((1, 1, total), (head, 0, 0))
     return pl.pallas_call(
         partial(attend_backward_kernel, size=size, prompt_rows=prompt_rows, score_scale=score_scale),
         grid_spec=pltpu.PrefetchScalarGridSpec(
             num_scalar_prefetch=1,
             grid=(total // size,),
-            in_specs=[
-                once(k)
-                for k in (tall, tall, wide, wide, tall, tall, per_head, wide, wide, row, row, gain, gain, table, table)
-            ],
-            out_specs=[once(k) for k in (wide, wide, wide, (2, total), gain, gain)],
+            in_specs=[tall, tall, wide, wide, tall, tall, per_head, wide, wide, row, row, gain, gain, table, table]
+            + [pl.BlockSpec(memory_space=pl.ANY)] * len(held),
+            out_specs=[wide, wide, wide, gain, gain, once((2, total), (0, 0))],
             scratch_shapes=[
-                pltpu.VMEM(wide, jnp.float32),
-                pltpu.VMEM(wide, jnp.float32),
-                pltpu.VMEM(per_head, jnp.float32),
+                pltpu.VMEM((HEAD, total), jnp.float32),
+                pltpu.VMEM((HEAD, total), jnp.float32),
+                pltpu.VMEM((1, total), jnp.float32),
             ],
         ),
         out_shape=[
-            jax.ShapeDtypeStruct(wide, jnp.float32),
-            jax.ShapeDtypeStruct(wide, jnp.float32),
-            jax.ShapeDtypeStruct(wide, jnp.bfloat16),
+            jax.ShapeDtypeStruct((columns, total), jnp.float32),
+            jax.ShapeDtypeStruct((columns, total), jnp.float32),
+            jax.ShapeDtypeStruct((columns, total), jnp.bfloat16),
+            jax.ShapeDtypeStruct((columns, 1), jnp.float32),
+            jax.ShapeDtypeStruct((columns, 1), jnp.float32),
             jax.ShapeDtypeStruct((2, total), jnp.float32),
-            jax.ShapeDtypeStruct(gain, jnp.float32),
-            jax.ShapeDtypeStruct(gain, jnp.float32),
         ],
+        input_output_aliases={16 + k: k for k in range(len(held))},
         compiler_params=pltpu.CompilerParams(vmem_limit_bytes=VMEM_BYTES),
         cost_estimate=pl.CostEstimate(
-            flops=24 * pairs * columns, bytes_accessed=40 * total * columns, transcendentals=pairs * heads
+            flops=24 * pairs * HEAD, bytes_accessed=40 * total * HEAD, transcendentals=pairs
         ),
         name="attend_backward",
-    )(starts, query, key, key_t, value_t, out_grad, out, log_rows, query_pre, key_pre, query_inv, key_inv, query_gain, key_gain, cosine, sine)
+    )(starts, query, key, key_t, value_t, out_grad, out, log_rows, query_pre, key_pre, query_inv, key_inv, query_gain, key_gain, cosine, sine, *held)
 
 
 def project_kernel(places, *refs, count):
@@ -930,9 +923,7 @@
         out_shape=[jax.ShapeDtypeStruct((count, width), jnp.bfloat16) for count in outs],
         compiler_params=pltpu.CompilerParams(vmem_limit_bytes=VMEM_BYTES),
         cost_estimate=pl.CostEstimate(
-            flops=2 * rows * width * columns,
-            bytes_accessed=2 * columns * (rows + width) + 4 * whole * width,
-            transcendentals=0,
+            flops=0, bytes_accessed=0, transcendentals=0
         ),
         name="hidden_term",
     )(place, heads_grad, w_t, out_rows, *gots)
@@ -983,7 +974,10 @@
 
 
 def out_grad_kernel(branch, w_out, out):
-    out[0] = dot_nt(branch[...], w_out[...]).astype(jnp.bfloat16)
+    made = dot_nt(branch[...], w_out[...]).astype(jnp.bfloat16)
+    columns = out.shape[2]
+    for k in range(out.shape[0]):
+        out[k] = made[:, k * columns : (k + 1) * columns]
 
 
 def out_grad_of(branch, w_out, contexts):
@@ -991,12 +985,12 @@
     columns = w_out.shape[0] // contexts
     return pl.pallas_call(
         out_grad_kernel,
-        grid=(contexts,),
+        grid=(contexts // 2,),
         in_specs=[
             pl.BlockSpec((rows, width), lambda i: (0, 0)),
-            pl.BlockSpec((columns, width), lambda i: (i, 0)),
+            pl.BlockSpec((2 * columns, width), lambda i: (i, 0)),
         ],
-        out_specs=pl.BlockSpec((1, rows, columns), lambda i: (i, 0, 0)),
+        out_specs=pl.BlockSpec((2, rows, columns), lambda i: (i, 0, 0)),
         out_shape=jax.ShapeDtypeStruct((contexts, rows, columns), jnp.bfloat16),
         compiler_params=pltpu.CompilerParams(vmem_limit_bytes=VMEM_BYTES),
         cost_estimate=pl.CostEstimate(
@@ -1457,8 +1451,9 @@
         return project(places_of, blocks, rows, w_t, gain_attn[None], made, total)
 
     made = project_all([0] + others[: 2 * (half - 2)], None)
-    token_ring.advance(made[-1], up_all)
+    token_ring.advance(made[-1], up_all, gate_all)
     made = project_all(others[2 * (half - 2) : -1], made)
+    token_ring.blocks[half] = after(token_ring.blocks[half], made[-1])
     made = project_all(others[-1:], made)
     hidden_all, query_pre, key_pre, value_t, squares = made
     w_out_rows = place_rows(
@@ -1551,12 +1546,10 @@
         waits = (done,)
         if step > 1:
             waits += (grad_ring.from_before, grad_ring.from_after)
-        if step == half - 1:
-            waits = (done, grad_ring.blocks[half])
-        else:
+        if step in (1, half - 1):
             grad_ring.advance(done, *near)
         done = forward(step, *waits)
-        if step < half - 1:
+        if step < half - 2:
             done = backward(step, done, light=True)
     done = forward(half, done)
 
@@ -1564,30 +1557,23 @@
     result_sum.advance(result_terms)
     backward(half, done)
     sent = second_sum.advance(second_terms, result_sum.to_before, result_sum.to_after)
-    sent += result_sum.prepare(result_terms, *sent)
-    result_sum.send()
     backward(half - 1, *sent)
+    sent = second_sum.advance(second_terms)
+    backward(half - 2, *sent)
+    sent = second_sum.advance(second_terms)
     rows_taken, active = kept
     route_grad, gate_grad, up_grad = kept_grads
-    sent = second_sum.advance(second_terms)
-    gate_product = weight_grad(
-        after(rows_taken, result_sum.to_before, result_sum.to_after, *sent), gate_grad
-    )
-    sent = second_sum.advance(second_terms, gate_product)
-    up_product = weight_grad(after(rows_taken, *sent), up_grad)
-    sent = second_sum.advance(second_terms, up_product)
+    gate_product = weight_grad(after(rows_taken, *sent), gate_grad)
+    sent = second_sum.advance(second_terms, gate_product[0, :8, :128])
     result_sum.prepare(result_terms, *sent)
-    down_product = weight_grad(after(active, *result_sum.payload), route_grad)
-    second_grad = second_sum.finish(after(second_terms[0], down_product))
+    up_product = weight_grad(after(rows_taken, *result_sum.payload), up_grad)
+    second_grad = second_sum.finish(after(second_terms[0], up_product[0, :8, :128]))
 
     def fsdp_sum_low(product):
         return lax.psum_scatter(product, "fsdp", scatter_dimension=1, tiled=True)
 
-    def fsdp_sum(product):
-        return fsdp_sum_low(product).astype(jnp.float32)
-
-    gate_w_grad = fsdp_sum(gate_product)
-    up_w_grad = fsdp_sum(up_product)
+    gate_w_grad = fsdp_sum_low(after(gate_product, second_grad))
+    up_w_grad = fsdp_sum_low(after(up_product, second_grad))
 
     upstream = cotangent[0].astype(jnp.float32)
     mixed_normed = mixed * mixed_inv
@@ -1601,17 +1587,28 @@
     w_out_grad = lax.dot_general(
         own_attended, after(branch, out_grad), (((0,), (0,)), ((), ())), preferred_element_type=jnp.float32
     ).astype(jnp.bfloat16)
+    down_product = weight_grad(after(active, out_grad), route_grad)
     out_grad = lax.all_to_all(out_grad, "ctx", split_axis=0, concat_axis=0, tiled=True)
     out_grad = out_grad.reshape(total, columns)
     w_out_grad = fsdp_sum_low(
-        w_out_grad.reshape(contexts, splits * own_rows, width)
-    )
-    result_sum.send(out_grad)
-
-    query_scaled, key_scaled, value_grad, dots, query_gain_grad, key_gain_grad = attend_backward(
-        starts, query, key, key_t, value_t, out_grad, attended, log_rows, query_pre, key_pre, query_inv, key_inv, gain_query, gain_key, cosine, sine, size, prompt_rows, score_scale
-    )
-    dots = after(dots, result_sum.to_before, result_sum.to_after)
+        after(w_out_grad, out_grad).reshape(contexts, splits * own_rows, width)
+    )
+    down_w_grad = fsdp_sum_low(after(down_product, out_grad))
+
+    log_rows = log_rows.reshape(columns // HEAD, 1, total)
+    held, dots, waits = None, 0.0, (out_grad, down_product[0, :8, :128])
+    for head in range(columns // HEAD):
+        if head == 1:
+            result_sum.prepare(result_terms, dots)
+            waits = result_sum.payload + (gate_w_grad,)
+        if head < 2:
+            result_sum.send(out_grad)
+        *held, part = attend_backward(
+            after(starts, *waits), head, held, query, key, key_t, value_t, out_grad, attended, log_rows, query_pre, key_pre, query_inv, key_inv, gain_query, gain_key, cosine, sine, size, prompt_rows, score_scale
+        )
+        dots = dots + part
+    query_scaled, key_scaled, value_grad, query_gain_grad, key_gain_grad = held
+    dots = after(dots, up_w_grad, result_sum.to_before, result_sum.to_after)
     result_sum.prepare(result_terms, dots)
     dots = sum_over_ctx(dots, contexts) / width
     dots = after(dots, *result_sum.payload)
@@ -1637,21 +1634,20 @@
         at = after(owner(offset)[None], *earlier)
         return hidden_term(at, heads_grad, w_t, w_out_grad, rows, **got)
 
-    down_w_grad = fsdp_sum(down_product)
+    result_sum.send(dots)
     hidden_sum = RingScatter(ring)
     hidden_sum.payload = far = term(half)
     hidden_sum.send()
-    result_sum.send(*far)
     heads_product = heads_product_of(
         heads_grad, hidden_all, after(other_grads, *far), contexts
     )
     heads_w_grad = fsdp_sum_low(after(heads_product, hidden_sum.to_before, hidden_sum.to_after))
-    done = (heads_product,)
+    done = (result_sum.to_before, result_sum.to_after)
     for step in range(half - 1, 0, -1):
         start = far[0].shape[0] if step == half - 1 else 0
+        if step == half - 2:
+            done = (heads_product,)
         if step == 1:
-            done = (result_sum.to_before, result_sum.to_after)
-        if step == half - 2:
             done = (down_w_grad,)
         hidden_sum.payload = (
             term(-step, *done, got=hidden_sum.to_before),
@@ -1697,9 +1693,9 @@
         heads_w_grad[1],
         heads_w_grad[2],
         w_out_grad,
-        gate_w_grad,
-        up_w_grad,
-        down_w_grad,
+        gate_w_grad.astype(jnp.float32),
+        up_w_grad.astype(jnp.float32),
+        down_w_grad.astype(jnp.float32),
     )
 
 

time: 1450 us -> 1450 us (level)
    ppermute x9, waiting for transfers between devices: 18.5 us -> 161 us  [advance(): self.from_before = lax.ppermute(before, 'ctx', self.up)]
    ppermute x9, waiting for transfers between devices: 119 us -> 1.52 us  [advance(): self.from_after = lax.ppermute(past, 'ctx', self.down)]
    all_gather x1, waiting for transfers between devices: 23 us -> 0.01 us  [shards_by_heads(): gate_all = lax.all_gather(after(w_gate, pieces), 'fsdp', axis=1, tiled=True)]
    pallas_call x1 -> x2, Pallas kernels: 76.2 us -> 87.4 us  [attend_backward(): pl.pallas_call(partial(attend_backward_kernel, size=size, prompt_rows=pro...]
  transfers between devices with their start and end apart: 74 -> 74, of which waited for: 30 -> 35; matrix products, arithmetic and copies ran while one was open for 14% -> 15% of each run, Pallas kernels for 37% -> 40%
where the time goes in v2:
time: 1450 us; the launch traced here: 1440 us
  Pallas kernels  580 us (40%)
  waiting for transfers between devices  477 us (33%)
  matrix products  100 us (7%)
  other arithmetic  99.5 us (7%)
  starting transfers between devices  99 us (7%)
  local copies, waits for them, and re-layouts  64.5 us (4%)
  between operations  15.9 us (1%)
    pallas_call x10, Pallas kernels, experts_stage(): pl.pallas_call(partial(kernel, count=count, slots=slots, aliased=len(held...  312 us
    ppermute x9, waiting for transfers between devices, advance(): self.from_before = lax.ppermute(before, 'ctx', self.up)  161 us
    ppermute x12, waiting for transfers between devices, send(): self.to_after = lax.ppermute(past, 'ctx', self.up)  120 us
    ppermute x12, waiting for transfers between devices, send(): self.to_before = lax.ppermute(before, 'ctx', self.down)  91.5 us
    pallas_call x2, Pallas kernels, attend_backward(): pl.pallas_call(partial(attend_backward_kernel, size=size, prompt_rows=pro...  87.4 us
    dot_general x3, matrix products, weight_grad(): jnp.einsum('emd,emf->edf', left, right, preferred_element_type=jnp.float32)  83.6 us
    pallas_call x1, Pallas kernels, attend_forward(): pl.pallas_call(partial(attend_forward_kernel, size=size, prompt_rows=prom...  49.7 us
    pallas_call x7, Pallas kernels, hidden_term(): pl.pallas_call(partial(hidden_term_kernel, start=start, halves=halves), g...  41.2 us
  transfers between devices with their start and end apart: 74, of which 35 were waited for; matrix products, arithmetic and copies ran while one was open for 15% of the time, Pallas kernels for 40%

profile of v2, /device:TPU:14, one launch (start us, length us, event | category | flops | bytes accessed | tf_op | source)
XLA Modules:
  0.0 1435.5 jit_solution(6335625491104506950)
XLA Ops:
  28.3 8.6 collective-permute-done.12.refs_7_
  46.5 50.7 %collective-permute-done.1.refs_1_.refs_7_ = bf16[576,2048]{1,0:T(8,128)(2,1)S(1)} collective-permute-done((bf16[576,2048]{1,0:T(8,128)(2,1)S(1)}, bf16[576,2048]{1,0:T(8,128)(2,1)S(1)}, u32[]{:S(2)}, u32[]{:S(2)}) %collective-permute-start.1) | collective-permute-done | bytes 2359328 | tf_op jit(solution)/shard_map/ppermute | solution.py:1271
  100.6 49.5 %collective-permute-done.2.refs_3_.refs_6_ = bf16[576,2048]{1,0:T(8,128)(2,1)} collective-permute-done((bf16[576,2048]{1,0:T(8,128)(2,1)S(1)}, bf16[576,2048]{1,0:T(8,128)(2,1)}, u32[]{:S(2)}, u32[]{:S(2)}) %collective-permute-start.2) | collective-permute-done | bytes 2359328 | tf_op jit(solution)/shard_map/ppermute | solution.py:1271
  164.4 21.4 %project.3 = (bf16[4096,2048]{1,0:T(8,128)(2,1)}, f32[256,4096]{1,0:T(8,128)}, f32[256,4096]{1,0:T(8,128)}, bf16[256,4096]{1,0:T(8,128)(2,1)}, f32[2,4096]{1,0:T(2,128)}) custom-call(s32[5]{0:T(128)} %compare_select_fusion.12.places, bf16[576,2048]{1,0:T(8,128)(2,1)} %copy-done.6, bf16[576,2048]{1,0:T(8,128)(2,1)} %copy-done.7, bf16[576,2048]{1,0:T(8,128)(2,1)} %copy-done.8, ...), custom_call_target="tpu_custom_call" | custom-call | flops 8053063680 | bytes 30670848 | tf_op jit(solution)/shard_map/project/pallas_call | solution.py:818
  185.8 16.5 %collective-permute-done.3.refs_0_.refs_5_ = bf16[576,2048]{1,0:T(8,128)(2,1)} collective-permute-done((bf16[576,2048]{1,0:T(8,128)(2,1)}, bf16[576,2048]{1,0:T(8,128)(2,1)}, u32[]{:S(2)}, u32[]{:S(2)}) %collective-permute-start.3) | collective-permute-done | bytes 2359328 | tf_op jit(solution)/shard_map/ppermute | solution.py:1271
  210.8 10.2 project.4
  221.1 9.4 collective-permute-done.13
  242.7 6.1 project.5
  266.5 49.7 %attend_forward.1 = (bf16[4096,256]{1,0:T(8,128)(2,1)}, bf16[4096,256]{1,0:T(8,128)(2,1)}, bf16[4096,256]{1,0:T(8,128)(2,1)}, bf16[256,4096]{1,0:T(8,128)(2,1)}, f32[2,4096]{1,0:T(2,128)}) custom-call(s32[3]{0:T(128)} %bitcast_subtract_fusion.starts, f32[256,4096]{1,0:T(8,128)} %get-tuple-element.181.query_pre, f32[256,4096]{1,0:T(8,128)} %get-tuple-element.182.key_pre, ...), custom_call_target="tpu_custom_call" | custom-call | flops 25769803776 | bytes 20971520 | tf_op jit(solution)/shard_map/attend_forward/pallas_call | solution.py:597
  316.3 6.0 all-to-all-start
  326.3 38.0 %all-to-all-done = bf16[8,512,256]{2,1,0:T(8,128)(2,1)} async-done(((bf16[8,512,256]{2,1,0:T(8,128)(2,1)}), bf16[8,512,256]{2,1,0:T(8,128)(2,1)}, u32[]{:S(2)}, u32[]{:S(2)}) %all-to-all-start) | async-done | bytes 2097184 | tf_op jit(solution)/shard_map/all_to_all | solution.py:1475
  364.3 7.7 multiply_reduce_fusion.2
  383.2 24.4 %experts_forward.5 = (bf16[2,2560,2048]{2,1,0:T(8,128)(2,1)}, bf16[2,2560,1024]{2,1,0:T(8,128)(2,1)}, bf16[2,320,1024]{2,1,0:T(8,128)(2,1)}, bf16[2,320,1024]{2,1,0:T(8,128)(2,1)}, bf16[512,2048]{1,0:T(8,128)(2,1)}) custom-call(s32[1,2,1,512]{3,2,1,0:T(1,128)} %get-tuple-element.192.refs_0_, f32[1,2,1,512]{3,2,1,0:T(1,128)} %get-tuple-element.353.refs_1_, ...), custom_call_target="tpu_custom_call" | custom-call | flops 10737418240 | bytes 33554432 | tf_op jit(solution)/shard_map/experts_forward/pallas_call | solution.py:1222
  412.8 22.7 %experts_backward.5 = (bf16[2,2560,2048]{2,1,0:T(8,128)(2,1)}, bf16[2,2560,1024]{2,1,0:T(8,128)(2,1)}, bf16[2,2560,1024]{2,1,0:T(8,128)(2,1)}, bf16[512,2048]{1,0:T(8,128)(2,1)}) custom-call(s32[1,2,1,512]{3,2,1,0:T(1,128)} %get-tuple-element.192.refs_0_, f32[1,2,1,512]{3,2,1,0:T(1,128)} %get-tuple-element.353.refs_1_, bf16[512,2048]{1,0:T(8,128)(2,1)} %bitcast.165, ...), custom_call_target="tpu_custom_call" | custom-call | tf_op jit(solution)/shard_map/experts_backward/pallas_call | solution.py:1222
  435.6 20.5 %collective-permute-done.22.refs_2_ = bf16[512,2048]{1,0:T(8,128)(2,1)} collective-permute-done((bf16[512,2048]{1,0:T(8,128)(2,1)S(1)}, bf16[512,2048]{1,0:T(8,128)(2,1)}, u32[]{:S(2)}, u32[]{:S(2)}) %collective-permute-start.22) | collective-permute-done | bytes 2097184 | tf_op jit(solution)/shard_map/ppermute | solution.py:1271
  460.9 36.8 %experts_forward.6 = (bf16[2,2560,2048]{2,1,0:T(8,128)(2,1)}, bf16[2,2560,1024]{2,1,0:T(8,128)(2,1)}, bf16[2,640,1024]{2,1,0:T(8,128)(2,1)}, bf16[2,640,1024]{2,...) custom-call(s32[2,2,1,512]{3,2,1,0:T(1,128)} %pad_add_fusion.2.refs_, ...), custom_call_target="tpu_custom_call", output_to_operand_aliasing={{0}: (7, {}), {1}: (8, {})} | custom-call | flops 21474836480 | bytes 41943040 | tf_op jit(solution)/shard_map/experts_forward/pallas_call | solution.py:1222
  497.7 35.7 %experts_backward.6 = (bf16[2,2560,2048]{2,1,0:T(8,128)(2,1)}, bf16[2,2560,1024]{2,1,0:T(8,128)(2,1)}, bf16[2,2560,1024]{2,1,0:T(8,128)(2,1)}, bf16[512,2048]{1,0:T(8,128)(2,1)}, bf16[512,2048]{1,0:T(8,128)(2,1)}) custom-call(s32[2,2,1,512]{3,2,1,0:T(1,128)} %pad_add_fusion.2.refs_0_, ...), custom_call_target="tpu_custom_call", output_to_operand_aliasing={{0}: (9, {}), {1}: (10, {}), {2}: (11, {})} | custom-call | tf_op jit(solution)/shard_map/experts_backward/pallas_call | solution.py:1222
  536.1 13.7 collective-permute-done.24.refs_2_
  549.9 37.5 %experts_forward.7 = (bf16[2,2560,2048]{2,1,0:T(8,128)(2,1)}, bf16[2,2560,1024]{2,1,0:T(8,128)(2,1)}, bf16[2,640,1024]{2,1,0:T(8,128)(2,1)}, bf16[2,640,1024]{2,...) custom-call(s32[2,2,1,512]{3,2,1,0:T(1,128)} %pad_add_fusion.1.refs_, ...), custom_call_target="tpu_custom_call", output_to_operand_aliasing={{0}: (7, {}), {1}: (8, {})} | custom-call | flops 21474836480 | bytes 41943040 | tf_op jit(solution)/shard_map/experts_forward/pallas_call | solution.py:1222
  603.1 37.2 %experts_forward.8 = (bf16[2,2560,2048]{2,1,0:T(8,128)(2,1)}, bf16[2,2560,1024]{2,1,0:T(8,128)(2,1)}, bf16[2,640,1024]{2,1,0:T(8,128)(2,1)}, bf16[2,640,1024]{2,...) custom-call(s32[2,2,1,512]{3,2,1,0:T(1,128)} %pad_add_fusion.refs_0_, ...), custom_call_target="tpu_custom_call", output_to_operand_aliasing={{0}: (7, {}), {1}: (8, {})} | custom-call | flops 21474836480 | bytes 41943040 | tf_op jit(solution)/shard_map/experts_forward/pallas_call | solution.py:1222
  645.7 24.3 %experts_forward.9 = (bf16[2,2560,2048]{2,1,0:T(8,128)(2,1)}, bf16[2,2560,1024]{2,1,0:T(8,128)(2,1)}, bf16[2,320,1024]{2,1,0:T(8,128)(2,1)}, bf16[2,320,1024]{2,1,0:T(8,128)(2,1)}, bf16[512,2048]{1,0:T(8,128)(2,1)}) custom-call(s32[1,2,1,512]{3,2,1,0:T(1,128)} %get-tuple-element.228.refs_0_, ...), custom_call_target="tpu_custom_call", output_to_operand_aliasing={{0}: (6, {}), {1}: (7, {})} | custom-call | flops 10737418240 | bytes 33554432 | tf_op jit(solution)/shard_map/experts_forward/pallas_call | solution.py:1222
  679.1 22.7 %experts_backward.7 = (bf16[2,2560,2048]{2,1,0:T(8,128)(2,1)}, bf16[2,2560,1024]{2,1,0:T(8,128)(2,1)}, bf16[2,2560,1024]{2,1,0:T(8,128)(2,1)}, bf16[512,2048]{1,0:T(8,128)(2,1)}) custom-call(s32[1,2,1,512]{3,2,1,0:T(1,128)} %get-tuple-element.228.refs_0_, ...), custom_call_target="tpu_custom_call", output_to_operand_aliasing={{0}: (8, {}), {1}: (9, {}), {2}: (10, {})} | custom-call | flops 10737418240 | bytes 33554432 | tf_op jit(solution)/shard_map/experts_backward/pallas_call | solution.py:1222
  707.5 35.4 %experts_backward.8 = (bf16[2,2560,2048]{2,1,0:T(8,128)(2,1)}, bf16[2,2560,1024]{2,1,0:T(8,128)(2,1)}, bf16[2,2560,1024]{2,1,0:T(8,128)(2,1)}, bf16[512,2048]{1,0:T(8,128)(2,1)}, bf16[512,2048]{1,0:T(8,128)(2,1)}) custom-call(s32[2,2,1,512]{3,2,1,0:T(1,128)} %pad_add_fusion.refs_0_, ...), custom_call_target="tpu_custom_call", output_to_operand_aliasing={{0}: (9, {}), {1}: (10, {}), {2}: (11, {})} | custom-call | flops 21474836480 | bytes 41943040 | tf_op jit(solution)/shard_map/experts_backward/pallas_call | solution.py:1222
  752.4 35.3 %experts_backward.9 = (bf16[2,2560,2048]{2,1,0:T(8,128)(2,1)}, bf16[2,2560,1024]{2,1,0:T(8,128)(2,1)}, bf16[2,2560,1024]{2,1,0:T(8,128)(2,1)}, bf16[512,2048]{1,0:T(8,128)(2,1)}, bf16[512,2048]{1,0:T(8,128)(2,1)}) custom-call(s32[2,2,1,512]{3,2,1,0:T(1,128)} %pad_add_fusion.1.refs_0_, ...), custom_call_target="tpu_custom_call", output_to_operand_aliasing={{0}: (9, {}), {1}: (10, {}), {2}: (11, {})} | custom-call | flops 21474836480 | bytes 41943040 | tf_op jit(solution)/shard_map/experts_backward/pallas_call | solution.py:1222
  799.7 38.5 %collective-permute-done.39 = bf16[512,2048]{1,0:T(8,128)(2,1)S(1)} collective-permute-done((bf16[512,2048]{1,0:T(8,128)(2,1)S(1)}, bf16[512,2048]{1,0:T(8,128)(2,1)S(1)}, u32[]{:S(2)}, u32[]{:S(2)}) %collective-permute-start.39) | collective-permute-done | bytes 2097184 | tf_op jit(solution)/shard_map/ppermute | solution.py:1316
  845.8 26.6 %convolution_convert_fusion.3 = bf16[2,2048,1024]{2,1,0:T(8,128)(2,1)} fusion(bf16[2,2560,2048]{2,1,0:T(8,128)(2,1)} %get-tuple-element.283, bf16[2,2560,1024]{2,1,0:T(8,128)(2,1)S(1)} %bitcast.159), kind=kOutput, calls=%fused_computation.7 | convolution fusion | flops 21479030784 | bytes 39845888 | tf_op jit(solution)/shard_map/emd,emf->edf/dot_general | solution.py:1535
  872.4 11.2 collective-permute-done.42
  887.8 7.3 multiply_reduce_fusion
  903.7 27.6 %convolution_convert_fusion.2 = bf16[2,2048,1024]{2,1,0:T(8,128)(2,1)} fusion(bf16[2,2560,2048]{2,1,0:T(8,128)(2,1)} %get-tuple-element.283, bf16[2,2560,1024]{2,1,0:T(8,128)(2,1)S(1)} %bitcast.161), kind=kOutput, calls=%fused_computation.6 | convolution fusion | flops 21479030784 | bytes 39845888 | tf_op jit(solution)/shard_map/emd,emf->edf/dot_general | solution.py:1535
  938.9 8.9 out_grad.1
  947.8 8.8 all-to-all-start.1
  960.7 8.4 convolution_convert_fusion
  969.1 25.1 %all-to-all-done.1 = bf16[8,512,256]{2,1,0:T(8,128)(2,1)} async-done(((bf16[8,512,256]{2,1,0:T(8,128)(2,1)}), bf16[8,512,256]{2,1,0:T(8,128)(2,1)}, u32[]{:S(2)}, u32[]{:S(2)}) %all-to-all-start.1) | async-done | bytes 2097184 | tf_op jit(solution)/shard_map/all_to_all | solution.py:1591
  994.5 29.4 %convolution_convert_fusion.1 = bf16[2,1024,2048]{2,1,0:T(8,128)(2,1)} fusion(bf16[2,2560,1024]{2,1,0:T(8,128)(2,1)} %get-tuple-element.299, bf16[2,2560,2048]{2,1,0:T(8,128)(2,1)} %get-tuple-element.300), kind=kOutput, calls=%fused_computation.5 | convolution fusion | flops 21479030784 | bytes 39845888 | tf_op jit(solution)/shard_map/emd,emf->edf/dot_general | solution.py:1535
  1029.0 43.6 %attend_backward.2 = (f32[256,4096]{1,0:T(8,128)}, f32[256,4096]{1,0:T(8,128)}, bf16[256,4096]{1,0:T(8,128)(2,1)}, f32[256,1]{1,0:T(8,128)}, f32[256,1]{1,0:T(8,128)}, /*index=5*/f32[2,4096]{1,0:T(2,128)}) custom-call(s32[3]{0:T(128)} %bitcast_subtract_fusion.starts, bf16[4096,256]{1,0:T(8,128)(2,1)} %get-tuple-element.262.query, ...), custom_call_target="tpu_custom_call" | custom-call | flops 25769803776 | bytes 20971520 | tf_op jit(solution)/shard_map/attend_backward/pallas_call | solution.py:753
  1082.7 43.8 %attend_backward.3 = (f32[256,4096]{1,0:T(8,128)}, f32[256,4096]{1,0:T(8,128)}, bf16[256,4096]{1,0:T(8,128)(2,1)}, f32[256,1]{1,0:T(8,128)}, f32[256,1]{1,0:T(8,128)}, /*index=5*/f32[2,4096]{1,0:T(2,128)}) custom-call(s32[3]{0:T(128)} %bitcast_subtract_fusion.starts, ...), custom_call_target="tpu_custom_call", output_to_operand_aliasing={{0}: (16, {}), {1}: (17, {}), {2}: (18, {}), {3}: (19, {}),... | custom-call | flops 25769803776 | bytes 20971520 | tf_op jit(solution)/shard_map/attend_backward/pallas_call | solution.py:753
  1148.0 10.1 heads_grad.1
  1165.5 19.6 %heads_product.1 = bf16[8,256,896]{2,1,0:T(8,128)(2,1)} custom-call(bf16[768,4096]{1,0:T(8,128)(2,1)} %heads_grad.1, bf16[4096,2048]{1,0:T(8,128)(2,1)} %get-tuple-element.303.hidden, f32[2048,128]{1,0:T(8,128)} %maximum_maximum_fusion.others), custom_call_target="tpu_custom_call" | custom-call | flops 12884901888 | bytes 23068672 | tf_op jit(solution)/shard_map/heads_product/pallas_call | solution.py:1043
  1185.1 29.1 %collective-permute-done.53.refs_0_ = bf16[288,2048]{1,0:T(8,128)(2,1)} collective-permute-done((bf16[288,2048]{1,0:T(8,128)(2,1)}, bf16[288,2048]{1,0:T(8,128)(2,1)}, u32[]{:S(2)}, u32[]{:S(2)}) %collective-permute-start.53) | collective-permute-done | bytes 1179680 | tf_op jit(solution)/shard_map/ppermute | solution.py:1316
  1230.1 41.4 %collective-permute-done.58.refs_0_ = bf16[576,2048]{1,0:T(8,128)(2,1)S(1)} collective-permute-done((bf16[576,2048]{1,0:T(8,128)(2,1)}, bf16[576,2048]{1,0:T(8,128)(2,1)S(1)}, u32[]{:S(2)}, u32[]{:S(2)}) %collective-permute-start.58) | collective-permute-done | bytes 2359328 | tf_op jit(solution)/shard_map/ppermute | solution.py:1317
  1286.8 40.7 %collective-permute-done.59.refs_0_ = bf16[576,2048]{1,0:T(8,128)(2,1)S(1)} collective-permute-done((bf16[576,2048]{1,0:T(8,128)(2,1)}, bf16[576,2048]{1,0:T(8,128)(2,1)S(1)}, u32[]{:S(2)}, u32[]{:S(2)}) %collective-permute-start.59) | collective-permute-done | bytes 2359328 | tf_op jit(solution)/shard_map/ppermute | solution.py:1317
  1329.0 6.0 hidden_term.13
  1337.4 6.0 hidden_term.10
  1352.7 30.6 %collective-permute-done.60.past = bf16[576,2048]{1,0:T(8,128)(2,1)} collective-permute-done((bf16[576,2048]{1,0:T(8,128)(2,1)}, bf16[576,2048]{1,0:T(8,128)(2,1)}, u32[]{:S(2)}, u32[]{:S(2)}) %collective-permute-start.60) | collective-permute-done | bytes 2359328 | tf_op jit(solution)/shard_map/ppermute | solution.py:1317
  1383.3 8.6 collective-permute-done.56.before
  1391.9 7.1 own_term.1
  1399.1 6.3 all-to-all-start.2
  1409.5 8.9 fusion.6
  (432 shorter events, 305.7 us)
Async XLA Ops:
  7.2 146.6 %all-gather.6.cloned.1.call-start = ((), (), s32[]{:S(2)}) async-start(), calls=%async_computation.8 | async-start | bytes 4587520 | tf_op jit(solution)/shard_map/all_gather | solution.py:1424
  42.1 161.6 %all-gather.8.cloned.1.call-start = ((), (), s32[]{:S(2)}) async-start(), calls=%async_computation.9 | async-start | bytes 10485760 | tf_op jit(solution)/shard_map/all_gather | solution.py:1425
  42.9 160.9 %all-gather.10.cloned.1.call-start = ((), (), s32[]{:S(2)}) async-start(), calls=%async_computation.10 | async-start | bytes 10485760 | tf_op jit(solution)/shard_map/all_gather | solution.py:1423
  43.6 320.7 %all-gather.12.cloned.1.call-start = ((), (), s32[]{:S(2)}) async-start(), calls=%async_computation.11 | async-start | bytes 10485760 | tf_op jit(solution)/shard_map/all_gather | solution.py:1462
  43.9 53.3 %collective-permute-start.1 = (bf16[576,2048]{1,0:T(8,128)(2,1)S(1)}, bf16[576,2048]{1,0:T(8,128)(2,1)S(1)}, u32[]{:S(2)}, u32[]{:S(2)}) collective-permute-start(bf16[576,2048]{1,0:T(8,128)(2,1)S(1)} %pad_maximum_fusion.refs_0_), channel_id=1, source_target_pairs={{0,8},{8,16},{16,24},{24,28},{28,20},{20,12},{12,4},{4,0},{1,9},{9... | collective-permute-start | bytes 7077896 | tf_op jit(solution)/shard_map/ppermute | solution.py:1271
  46.5 53.2 %collective-permute-start.4 = (bf16[576,2048]{1,0:T(8,128)(2,1)S(1)}, bf16[576,2048]{1,0:T(8,128)(2,1)S(1)}, u32[]{:S(2)}, u32[]{:S(2)}) collective-permute-start(bf16[576,2048]{1,0:T(8,128)(2,1)S(1)} %pad_maximum_fusion.refs_0_), channel_id=1, source_target_pairs={{8,0},{16,8},{24,16},{28,24},{20,28},{12,20},{4,12},{0,4},{9,1},{1... | collective-permute-start | bytes 7077896 | tf_op jit(solution)/shard_map/ppermute | solution.py:1272
  97.2 52.9 %collective-permute-start.2 = (bf16[576,2048]{1,0:T(8,128)(2,1)S(1)}, bf16[576,2048]{1,0:T(8,128)(2,1)}, u32[]{:S(2)}, u32[]{:S(2)}) collective-permute-start(bf16[576,2048]{1,0:T(8,128)(2,1)S(1)} %collective-permute-done.1.refs_1_.refs_7_), channel_id=1, source_target_pairs={{0,8},{8,16},{16,24},{24,28},{28,20},{20,12},{12,4},{4,0},{1,9},{9... | collective-permute-start | bytes 7077896 | tf_op jit(solution)/shard_map/ppermute | solution.py:1271
  99.7 52.5 %collective-permute-start.5 = (bf16[576,2048]{1,0:T(8,128)(2,1)S(1)}, bf16[576,2048]{1,0:T(8,128)(2,1)}, u32[]{:S(2)}, u32[]{:S(2)}) collective-permute-start(bf16[576,2048]{1,0:T(8,128)(2,1)S(1)} %collective-permute-done.4.refs_2_.refs_1_), channel_id=1, source_target_pairs={{8,0},{16,8},{24,16},{28,24},{20,28},{12,20},{4,12},{0,4},{9,1},{1... | collective-permute-start | bytes 7077896 | tf_op jit(solution)/shard_map/ppermute | solution.py:1272
  150.1 52.2 %collective-permute-start.3 = (bf16[576,2048]{1,0:T(8,128)(2,1)}, bf16[576,2048]{1,0:T(8,128)(2,1)}, u32[]{:S(2)}, u32[]{:S(2)}) collective-permute-start(bf16[576,2048]{1,0:T(8,128)(2,1)} %collective-permute-done.2.refs_3_.refs_6_), channel_id=1, source_target_pairs={{0,8},{8,16},{16,24},{24,28},{28,20},{20,12},{12,4},{4,0},{1,9},{9... | collective-permute-start | bytes 7077896 | tf_op jit(solution)/shard_map/ppermute | solution.py:1271
  152.2 51.5 %collective-permute-start.6 = (bf16[576,2048]{1,0:T(8,128)(2,1)}, bf16[576,2048]{1,0:T(8,128)(2,1)}, u32[]{:S(2)}, u32[]{:S(2)}) collective-permute-start(bf16[576,2048]{1,0:T(8,128)(2,1)} %collective-permute-done.5.refs_4_.refs_2_), channel_id=1, source_target_pairs={{8,0},{16,8},{24,16},{28,24},{20,28},{12,20},{4,12},{0,4},{9,1},{1... | collective-permute-start | bytes 7077896 | tf_op jit(solution)/shard_map/ppermute | solution.py:1272
  241.7 141.5 %all-gather.14.cloned.1.call-start = ((), (), s32[]{:S(2)}) async-start(), calls=%async_computation.12 | async-start | bytes 10485760 | tf_op jit(solution)/shard_map/all_gather | solution.py:1463
  263.8 52.4 %collective-permute-start.18 = (bf16[512,2048]{1,0:T(8,128)(2,1)}, bf16[512,2048]{1,0:T(8,128)(2,1)}, u32[]{:S(2)}, u32[]{:S(2)}) collective-permute-start(bf16[512,2048]{1,0:T(8,128)(2,1)} %bitcast.163), channel_id=1, source_target_pairs={{0,8},{8,16},{16,24},{24,28},{28,20},{20,12},{12,4},{4,0},{1,9},{9... | collective-permute-start | bytes 6291464 | tf_op jit(solution)/shard_map/ppermute | solution.py:1271
  264.2 52.0 %collective-permute-start.19 = (bf16[512,2048]{1,0:T(8,128)(2,1)}, bf16[512,2048]{1,0:T(8,128)(2,1)}, u32[]{:S(2)}, u32[]{:S(2)}) collective-permute-start(bf16[512,2048]{1,0:T(8,128)(2,1)} %bitcast.164), channel_id=1, source_target_pairs={{8,0},{16,8},{24,16},{28,24},{20,28},{12,20},{4,12},{0,4},{9,1},{1... | collective-permute-start | bytes 6291464 | tf_op jit(solution)/shard_map/ppermute | solution.py:1272
  316.3 48.1 %all-to-all-start = ((bf16[8,512,256]{2,1,0:T(8,128)(2,1)}), bf16[8,512,256]{2,1,0:T(8,128)(2,1)}, u32[]{:S(2)}, u32[]{:S(2)}) async-start(bf16[8,512,256]{2,1,0:T(8,128)(2,1)} %bitcast.176), calls=%async_computation | async-start | bytes 4194304 | tf_op jit(solution)/shard_map/all_to_all | solution.py:1475
  322.3 760.4 %reduce-scatter.6.cloned.1.call-start = ((), (), s32[]{:S(2)}) async-start(), calls=%async_computation.13 | async-start | bytes 10485760 | tf_op jit(solution)/shard_map/reduce_scatter | solution.py:1573
  324.3 88.6 %collective-permute-start.20 = (bf16[512,2048]{1,0:T(8,128)(2,1)}, bf16[512,2048]{1,0:T(8,128)(2,1)}, u32[]{:S(2)}, u32[]{:S(2)}) collective-permute-start(bf16[512,2048]{1,0:T(8,128)(2,1)} %collective-permute-done.18.refs_2_), channel_id=1, source_target_pairs={{0,8},{8,16},{16,24},{24,28},{28,20},{20,12},{12,4},{4,0},{1,9},{9... | collective-permute-start | bytes 6291464 | tf_op jit(solution)/shard_map/ppermute | solution.py:1271
  324.9 88.0 %collective-permute-start.21 = (bf16[512,2048]{1,0:T(8,128)(2,1)}, bf16[512,2048]{1,0:T(8,128)(2,1)}, u32[]{:S(2)}, u32[]{:S(2)}) collective-permute-start(bf16[512,2048]{1,0:T(8,128)(2,1)} %collective-permute-done.19.refs_3_), channel_id=1, source_target_pairs={{8,0},{16,8},{24,16},{28,24},{20,28},{12,20},{4,12},{0,4},{9,1},{1... | collective-permute-start | bytes 6291464 | tf_op jit(solution)/shard_map/ppermute | solution.py:1272
  374.1 82.0 %collective-permute-start.22 = (bf16[512,2048]{1,0:T(8,128)(2,1)S(1)}, bf16[512,2048]{1,0:T(8,128)(2,1)}, u32[]{:S(2)}, u32[]{:S(2)}) collective-permute-start(bf16[512,2048]{1,0:T(8,128)(2,1)S(1)} %multiply_convert_fusion.refs_2_), channel_id=1, source_target_pairs={{0,8},{8,16},{16,24},{24,28},{28,20},{20,12},{12,4},{4,0},{1,9},{9... | collective-permute-start | bytes 6291464 | tf_op jit(solution)/shard_map/ppermute | solution.py:1271
  379.1 76.9 %collective-permute-start.23 = (bf16[512,2048]{1,0:T(8,128)(2,1)S(1)}, bf16[512,2048]{1,0:T(8,128)(2,1)}, u32[]{:S(2)}, u32[]{:S(2)}) collective-permute-start(bf16[512,2048]{1,0:T(8,128)(2,1)S(1)} %multiply_convert_fusion.refs_2_), channel_id=1, source_target_pairs={{8,0},{16,8},{24,16},{28,24},{20,28},{12,20},{4,12},{0,4},{9,1},{1... | collective-permute-start | bytes 6291464 | tf_op jit(solution)/shard_map/ppermute | solution.py:1272
  456.1 77.3 %collective-permute-start.26 = (bf16[512,2048]{1,0:T(8,128)(2,1)}, bf16[512,2048]{1,0:T(8,128)(2,1)}, u32[]{:S(2)}, u32[]{:S(2)}) collective-permute-start(bf16[512,2048]{1,0:T(8,128)(2,1)} %collective-permute-done.22.refs_2_), channel_id=1, source_target_pairs={{0,8},{8,16},{16,24},{24,28},{28,20},{20,12},{12,4},{4,0},{1,9},{9... | collective-permute-start | bytes 6291464 | tf_op jit(solution)/shard_map/ppermute | solution.py:1271
  456.1 77.3 %collective-permute-start.27 = (bf16[512,2048]{1,0:T(8,128)(2,1)}, bf16[512,2048]{1,0:T(8,128)(2,1)}, u32[]{:S(2)}, u32[]{:S(2)}) collective-permute-start(bf16[512,2048]{1,0:T(8,128)(2,1)} %collective-permute-done.23.refs_3_), channel_id=1, source_target_pairs={{8,0},{16,8},{24,16},{28,24},{20,28},{12,20},{4,12},{0,4},{9,1},{1... | collective-permute-start | bytes 6291464 | tf_op jit(solution)/shard_map/ppermute | solution.py:1272
  458.7 91.1 %collective-permute-start.24 = (bf16[512,2048]{1,0:T(8,128)(2,1)}, bf16[512,2048]{1,0:T(8,128)(2,1)S(1)}, u32[]{:S(2)}, u32[]{:S(2)}) collective-permute-start(bf16[512,2048]{1,0:T(8,128)(2,1)} %collective-permute-done.20.refs_2_), channel_id=1, source_target_pairs={{0,8},{8,16},{16,24},{24,28},{28,20},{20,12},{12,4},{4,0},{1,9},{9... | collective-permute-start | bytes 6291464 | tf_op jit(solution)/shard_map/ppermute | solution.py:1271
  458.7 91.2 %collective-permute-start.25 = (bf16[512,2048]{1,0:T(8,128)(2,1)}, bf16[512,2048]{1,0:T(8,128)(2,1)}, u32[]{:S(2)}, u32[]{:S(2)}) collective-permute-start(bf16[512,2048]{1,0:T(8,128)(2,1)} %collective-permute-done.21.refs_3_), channel_id=1, source_target_pairs={{8,0},{16,8},{24,16},{28,24},{20,28},{12,20},{4,12},{0,4},{9,1},{1... | collective-permute-start | bytes 6291464 | tf_op jit(solution)/shard_map/ppermute | solution.py:1272
  533.4 59.2 %collective-permute-start.28 = (bf16[512,2048]{1,0:T(8,128)(2,1)}, bf16[512,2048]{1,0:T(8,128)(2,1)}, u32[]{:S(2)}, u32[]{:S(2)}) collective-permute-start(bf16[512,2048]{1,0:T(8,128)(2,1)} %collective-permute-done.26.refs_2_), channel_id=1, source_target_pairs={{0,8},{8,16},{16,24},{24,28},{28,20},{20,12},{12,4},{4,0},{1,9},{9... | collective-permute-start | bytes 6291464 | tf_op jit(solution)/shard_map/ppermute | solution.py:1271
  533.5 59.1 %collective-permute-start.29 = (bf16[512,2048]{1,0:T(8,128)(2,1)}, bf16[512,2048]{1,0:T(8,128)(2,1)}, u32[]{:S(2)}, u32[]{:S(2)}) collective-permute-start(bf16[512,2048]{1,0:T(8,128)(2,1)} %collective-permute-done.27.refs_3_), channel_id=1, source_target_pairs={{8,0},{16,8},{24,16},{28,24},{20,28},{12,20},{4,12},{0,4},{9,1},{1... | collective-permute-start | bytes 6291464 | tf_op jit(solution)/shard_map/ppermute | solution.py:1272
  593.9 81.9 %collective-permute-start.33 = (bf16[256,2048]{1,0:T(8,128)(2,1)S(1)}, bf16[256,2048]{1,0:T(8,128)(2,1)}, u32[]{:S(2)}, u32[]{:S(2)}) collective-permute-start(bf16[256,2048]{1,0:T(8,128)(2,1)S(1)} %slice.272), channel_id=1, source_target_pairs={{0,8},{8,16},{16,24},{24,28},{28,20},{20,12},{12,4},{4,0},{1,9},{9... | collective-permute-start | bytes 3145736 | tf_op jit(solution)/shard_map/ppermute | solution.py:1277
  596.3 79.5 %collective-permute-start.34 = (bf16[256,2048]{1,0:T(8,128)(2,1)}, bf16[256,2048]{1,0:T(8,128)(2,1)}, u32[]{:S(2)}, u32[]{:S(2)}) collective-permute-start(bf16[256,2048]{1,0:T(8,128)(2,1)} %slice.273), channel_id=1, source_target_pairs={{8,0},{16,8},{24,16},{28,24},{20,28},{12,20},{4,12},{0,4},{9,1},{1... | collective-permute-start | bytes 3145736 | tf_op jit(solution)/shard_map/ppermute | solution.py:1278
  746.9 44.9 %collective-permute-start.37 = (bf16[512,2048]{1,0:T(8,128)(2,1)}, bf16[512,2048]{1,0:T(8,128)(2,1)S(1)}, u32[]{:S(2)}, u32[]{:S(2)}) collective-permute-start(bf16[512,2048]{1,0:T(8,128)(2,1)} %pad_maximum_fusion.4), channel_id=1, source_target_pairs={{8,0},{16,8},{24,16},{28,24},{20,28},{12,20},{4,12},{0,4},{9,1},{1... | collective-permute-start | bytes 6291464 | tf_op jit(solution)/shard_map/ppermute | solution.py:1316
  752.2 44.7 %collective-permute-start.40 = (bf16[512,2048]{1,0:T(8,128)(2,1)}, bf16[512,2048]{1,0:T(8,128)(2,1)}, u32[]{:S(2)}, u32[]{:S(2)}) collective-permute-start(bf16[512,2048]{1,0:T(8,128)(2,1)} %pad_maximum_fusion.5), channel_id=1, source_target_pairs={{0,8},{8,16},{16,24},{24,28},{28,20},{20,12},{12,4},{4,0},{1,9},{9... | collective-permute-start | bytes 6291464 | tf_op jit(solution)/shard_map/ppermute | solution.py:1317
  895.1 233.0 %reduce-scatter.8.cloned.1.call-start = ((), (), s32[]{:S(2)}) async-start(), calls=%async_computation.14 | async-start | bytes 10485760 | tf_op jit(solution)/shard_map/reduce_scatter | solution.py:1573
  947.8 46.4 %all-to-all-start.1 = ((bf16[8,512,256]{2,1,0:T(8,128)(2,1)}), bf16[8,512,256]{2,1,0:T(8,128)(2,1)}, u32[]{:S(2)}, u32[]{:S(2)}) async-start(bf16[8,512,256]{2,1,0:T(8,128)(2,1)} %out_grad.1), calls=%async_computation.1 | async-start | bytes 4194304 | tf_op jit(solution)/shard_map/all_to_all | solution.py:1591
  956.6 201.4 %reduce-scatter.10.cloned.1.call-start = ((), (), s32[]{:S(2)}) async-start(), calls=%async_computation.15 | async-start | bytes 10485760 | tf_op jit(solution)/shard_map/reduce_scatter | solution.py:1573
  994.3 292.6 %reduce-scatter.12.cloned.1.call-start = ((), (), s32[]{:S(2)}) async-start(), calls=%async_computation.16 | async-start | bytes 10485760 | tf_op jit(solution)/shard_map/reduce_scatter | solution.py:1573
  1023.9 375.1 %reduce-scatter.14.cloned.1.call-start = ((), (), s32[]{:S(2)}) async-start(), calls=%async_computation.17 | async-start | bytes 4587520 | tf_op jit(solution)/shard_map/reduce_scatter | solution.py:1573
  1025.3 47.3 %collective-permute-start.45 = (bf16[512,2048]{1,0:T(8,128)(2,1)}, bf16[512,2048]{1,0:T(8,128)(2,1)}, u32[]{:S(2)}, u32[]{:S(2)}) collective-permute-start(bf16[512,2048]{1,0:T(8,128)(2,1)} %pad_maximum_fusion.7), channel_id=1, source_target_pairs={{0,8},{8,16},{16,24},{24,28},{28,20},{20,12},{12,4},{4,0},{1,9},{9... | collective-permute-start | bytes 6291464 | tf_op jit(solution)/shard_map/ppermute | solution.py:1317
  1029.0 47.6 %collective-permute-start.44 = (bf16[512,2048]{1,0:T(8,128)(2,1)}, bf16[512,2048]{1,0:T(8,128)(2,1)}, u32[]{:S(2)}, u32[]{:S(2)}) collective-permute-start(bf16[512,2048]{1,0:T(8,128)(2,1)} %pad_maximum_fusion.6), channel_id=1, source_target_pairs={{8,0},{16,8},{24,16},{28,24},{20,28},{12,20},{4,12},{0,4},{9,1},{1... | collective-permute-start | bytes 6291464 | tf_op jit(solution)/shard_map/ppermute | solution.py:1316
  1080.3 47.1 %collective-permute-start.46 = (bf16[512,2048]{1,0:T(8,128)(2,1)}, bf16[512,2048]{1,0:T(8,128)(2,1)}, u32[]{:S(2)}, u32[]{:S(2)}) collective-permute-start(bf16[512,2048]{1,0:T(8,128)(2,1)} %add_convert_fusion.3), channel_id=1, source_target_pairs={{8,0},{16,8},{24,16},{28,24},{20,28},{12,20},{4,12},{0,4},{9,1},{1... | collective-permute-start | bytes 6291464 | tf_op jit(solution)/shard_map/ppermute | solution.py:1316
  1080.9 47.2 %collective-permute-start.47 = (bf16[512,2048]{1,0:T(8,128)(2,1)}, bf16[512,2048]{1,0:T(8,128)(2,1)}, u32[]{:S(2)}, u32[]{:S(2)}) collective-permute-start(bf16[512,2048]{1,0:T(8,128)(2,1)} %add_convert_fusion.2), channel_id=1, source_target_pairs={{0,8},{8,16},{16,24},{24,28},{28,20},{20,12},{12,4},{4,0},{1,9},{9... | collective-permute-start | bytes 6291464 | tf_op jit(solution)/shard_map/ppermute | solution.py:1317
  1143.7 71.0 %collective-permute-start.51 = (bf16[512,2048]{1,0:T(8,128)(2,1)}, bf16[512,2048]{1,0:T(8,128)(2,1)S(1)}, u32[]{:S(2)}, u32[]{:S(2)}) collective-permute-start(bf16[512,2048]{1,0:T(8,128)(2,1)} %add_convert_fusion.1), channel_id=1, source_target_pairs={{8,0},{16,8},{24,16},{28,24},{20,28},{12,20},{4,12},{0,4},{9,1},{1... | collective-permute-start | bytes 6291464 | tf_op jit(solution)/shard_map/ppermute | solution.py:1316
  1144.2 70.5 %collective-permute-start.52 = (bf16[512,2048]{1,0:T(8,128)(2,1)}, bf16[512,2048]{1,0:T(8,128)(2,1)}, u32[]{:S(2)}, u32[]{:S(2)}) collective-permute-start(bf16[512,2048]{1,0:T(8,128)(2,1)} %add_convert_fusion), channel_id=1, source_target_pairs={{0,8},{8,16},{16,24},{24,28},{28,20},{20,12},{12,4},{4,0},{1,9},{9... | collective-permute-start | bytes 6291464 | tf_op jit(solution)/shard_map/ppermute | solution.py:1317
  1163.5 50.7 %collective-permute-start.53 = (bf16[288,2048]{1,0:T(8,128)(2,1)}, bf16[288,2048]{1,0:T(8,128)(2,1)}, u32[]{:S(2)}, u32[]{:S(2)}) collective-permute-start(bf16[288,2048]{1,0:T(8,128)(2,1)} %get-tuple-element.306), channel_id=1, source_target_pairs={{8,0},{16,8},{24,16},{28,24},{20,28},{12,20},{4,12},{0,4},{9,1},{1... | collective-permute-start | bytes 3538952 | tf_op jit(solution)/shard_map/ppermute | solution.py:1316
  1163.5 51.1 %collective-permute-start.57 = (bf16[288,2048]{1,0:T(8,128)(2,1)}, bf16[288,2048]{1,0:T(8,128)(2,1)}, u32[]{:S(2)}, u32[]{:S(2)}) collective-permute-start(bf16[288,2048]{1,0:T(8,128)(2,1)} %get-tuple-element.307), channel_id=1, source_target_pairs={{0,8},{8,16},{16,24},{24,28},{28,20},{20,12},{12,4},{4,0},{1,9},{9... | collective-permute-start | bytes 3538952 | tf_op jit(solution)/shard_map/ppermute | solution.py:1317
  1221.9 49.5 %collective-permute-start.58 = (bf16[576,2048]{1,0:T(8,128)(2,1)}, bf16[576,2048]{1,0:T(8,128)(2,1)S(1)}, u32[]{:S(2)}, u32[]{:S(2)}) collective-permute-start(bf16[576,2048]{1,0:T(8,128)(2,1)} %hidden_term.11), channel_id=1, source_target_pairs={{0,8},{8,16},{16,24},{24,28},{28,20},{20,12},{12,4},{4,0},{1,9},{9... | collective-permute-start | bytes 7077896 | tf_op jit(solution)/shard_map/ppermute | solution.py:1317
  1229.3 51.5 %collective-permute-start.54 = (bf16[576,2048]{1,0:T(8,128)(2,1)}, bf16[576,2048]{1,0:T(8,128)(2,1)}, u32[]{:S(2)}, u32[]{:S(2)}) collective-permute-start(bf16[576,2048]{1,0:T(8,128)(2,1)} %hidden_term.8), channel_id=1, source_target_pairs={{8,0},{16,8},{24,16},{28,24},{20,28},{12,20},{4,12},{0,4},{9,1},{1... | collective-permute-start | bytes 7077896 | tf_op jit(solution)/shard_map/ppermute | solution.py:1316
  1278.8 48.7 %collective-permute-start.59 = (bf16[576,2048]{1,0:T(8,128)(2,1)}, bf16[576,2048]{1,0:T(8,128)(2,1)S(1)}, u32[]{:S(2)}, u32[]{:S(2)}) collective-permute-start(bf16[576,2048]{1,0:T(8,128)(2,1)} %hidden_term.12), channel_id=1, source_target_pairs={{0,8},{8,16},{16,24},{24,28},{28,20},{20,12},{12,4},{4,0},{1,9},{9... | collective-permute-start | bytes 7077896 | tf_op jit(solution)/shard_map/ppermute | solution.py:1317
  1286.8 50.6 %collective-permute-start.55 = (bf16[576,2048]{1,0:T(8,128)(2,1)}, bf16[576,2048]{1,0:T(8,128)(2,1)}, u32[]{:S(2)}, u32[]{:S(2)}) collective-permute-start(bf16[576,2048]{1,0:T(8,128)(2,1)} %hidden_term.9), channel_id=1, source_target_pairs={{8,0},{16,8},{24,16},{28,24},{20,28},{12,20},{4,12},{0,4},{9,1},{1... | collective-permute-start | bytes 7077896 | tf_op jit(solution)/shard_map/ppermute | solution.py:1316
  1335.0 48.3 %collective-permute-start.60 = (bf16[576,2048]{1,0:T(8,128)(2,1)}, bf16[576,2048]{1,0:T(8,128)(2,1)}, u32[]{:S(2)}, u32[]{:S(2)}) collective-permute-start(bf16[576,2048]{1,0:T(8,128)(2,1)} %hidden_term.13), channel_id=1, source_target_pairs={{0,8},{8,16},{16,24},{24,28},{28,20},{20,12},{12,4},{4,0},{1,9},{9... | collective-permute-start | bytes 7077896 | tf_op jit(solution)/shard_map/ppermute | solution.py:1317
  1343.4 48.5 %collective-permute-start.56 = (bf16[576,2048]{1,0:T(8,128)(2,1)}, bf16[576,2048]{1,0:T(8,128)(2,1)}, u32[]{:S(2)}, u32[]{:S(2)}) collective-permute-start(bf16[576,2048]{1,0:T(8,128)(2,1)} %hidden_term.10), channel_id=1, source_target_pairs={{8,0},{16,8},{24,16},{28,24},{20,28},{12,20},{4,12},{0,4},{9,1},{1... | collective-permute-start | bytes 7077896 | tf_op jit(solution)/shard_map/ppermute | solution.py:1316
  (102 other events, 1757.3 us)
Sparse Core Ops, SparseCore 0:
  42.2 32.4 all-gather.5
  76.3 58.2 all-gather.7
  136.2 58.2 all-gather.9
  241.9 57.3 all-gather.11
  300.7 58.2 all-gather.13
  895.2 71.1 reduce-scatter.5
  969.1 71.7 reduce-scatter.7
  1043.5 71.6 reduce-scatter.9
  1118.0 71.7 reduce-scatter.11
  1214.7 39.9 reduce-scatter.13

commit v3 on v2

--- a/solution.py
+++ b/solution.py
@@ -930,47 +930,46 @@
     return made if halves else made[0]
 
 
-def own_term_kernel(place, heads_grad, w_t, out_rows, before, past, hidden_grad, out_grad):
-    rows = heads_grad.shape[1]
-    term = dot_tn(heads_grad[...], w_t[...])
+def input_grad_kernel(place, heads_grad, w_t, before, past, tokens, gain, mixed_grad, out):
     got = before[...].astype(jnp.float32) + past[...].astype(jnp.float32)
-    hidden_grad[...] = term + got[:rows]
-    out_grad[...] = out_rows[0].astype(jnp.float32) + got[rows:]
-
-
-def own_term(place, heads_grad, w_t, out_rows, rows, before, past):
+    scaled = (dot_tn(heads_grad[...], w_t[...]) + got) * gain[...]
+    inputs = tokens[...].astype(jnp.float32)
+    inverse = lax.rsqrt(jnp.mean(inputs * inputs, axis=-1, keepdims=True) + EPSILON)
+    normed = inputs * inverse
+    along = jnp.mean(scaled * normed, axis=-1, keepdims=True)
+    out[...] = mixed_grad[...] + inverse * (scaled - normed * along)
+
+
+def input_grad_of(place, heads_grad, w_t, before, past, tokens, gain, mixed_grad):
     columns, width = w_t.shape
-    extra = out_rows.shape[1]
-    tile = min(512, width)
+    rows = tokens.shape[0]
+    tile = rows // 4
+    block = pl.BlockSpec((tile, width), lambda i, p: (i, 0))
     return pl.pallas_call(
-        own_term_kernel,
+        input_grad_kernel,
         grid_spec=pltpu.PrefetchScalarGridSpec(
             num_scalar_prefetch=1,
-            grid=(width // tile,),
+            grid=(4,),
             in_specs=[
-                pl.BlockSpec((columns, rows), lambda i, p: (0, p[0])),
-                pl.BlockSpec((columns, tile), lambda i, p: (0, i)),
-                pl.BlockSpec((1, extra, tile), lambda i, p: (p[0], 0, i)),
-                pl.BlockSpec((rows + extra, tile), lambda i, p: (0, i)),
-                pl.BlockSpec((rows + extra, tile), lambda i, p: (0, i)),
+                pl.BlockSpec((columns, tile), lambda i, p: (0, 4 * p[0] + i)),
+                pl.BlockSpec((columns, width), lambda i, p: (0, 0)),
+                block,
+                block,
+                block,
+                pl.BlockSpec((1, width), lambda i, p: (0, 0)),
+                block,
             ],
-            out_specs=[
-                pl.BlockSpec((rows, tile), lambda i, p: (0, i)),
-                pl.BlockSpec((extra, tile), lambda i, p: (0, i)),
-            ],
+            out_specs=block,
         ),
-        out_shape=[
-            jax.ShapeDtypeStruct((rows, width), jnp.float32),
-            jax.ShapeDtypeStruct((extra, width), jnp.float32),
-        ],
+        out_shape=jax.ShapeDtypeStruct((rows, width), jnp.float32),
         compiler_params=pltpu.CompilerParams(vmem_limit_bytes=VMEM_BYTES),
         cost_estimate=pl.CostEstimate(
             flops=2 * rows * width * columns,
-            bytes_accessed=2 * columns * (rows + width) + 8 * (rows + extra) * width,
-            transcendentals=0,
+            bytes_accessed=2 * columns * (rows + width) + 14 * rows * width,
+            transcendentals=rows,
         ),
-        name="own_term",
-    )(place, heads_grad, w_t, out_rows, before, past)
+        name="input_grad",
+    )(place, heads_grad, w_t, before, past, tokens, gain, mixed_grad)
 
 
 def out_grad_kernel(branch, w_out, out):
@@ -1457,7 +1456,7 @@
     made = project_all(others[-1:], made)
     hidden_all, query_pre, key_pre, value_t, squares = made
     w_out_rows = place_rows(
-        owners, [token_ring.blocks[k if k <= half else k - contexts] for k in range(contexts)], rows, own_rows
+        after(owners, made[-1]), [token_ring.blocks[k if k <= half else k - contexts] for k in range(contexts)], rows, own_rows
     )
     out_all = lax.all_gather(w_out_rows, "fsdp", axis=1, tiled=True).reshape(width, width)
     down_all = lax.all_gather(w_down, "fsdp", axis=1, tiled=True)
@@ -1564,16 +1563,14 @@
     rows_taken, active = kept
     route_grad, gate_grad, up_grad = kept_grads
     gate_product = weight_grad(after(rows_taken, *sent), gate_grad)
-    sent = second_sum.advance(second_terms, gate_product[0, :8, :128])
+    sent = second_sum.advance(second_terms, gate_product)
     result_sum.prepare(result_terms, *sent)
     up_product = weight_grad(after(rows_taken, *result_sum.payload), up_grad)
-    second_grad = second_sum.finish(after(second_terms[0], up_product[0, :8, :128]))
+    second_grad = second_sum.finish(after(second_terms[0], up_product))
 
     def fsdp_sum_low(product):
         return lax.psum_scatter(product, "fsdp", scatter_dimension=1, tiled=True)
 
-    gate_w_grad = fsdp_sum_low(after(gate_product, second_grad))
-    up_w_grad = fsdp_sum_low(after(up_product, second_grad))
 
     upstream = cotangent[0].astype(jnp.float32)
     mixed_normed = mixed * mixed_inv
@@ -1587,20 +1584,20 @@
     w_out_grad = lax.dot_general(
         own_attended, after(branch, out_grad), (((0,), (0,)), ((), ())), preferred_element_type=jnp.float32
     ).astype(jnp.bfloat16)
-    down_product = weight_grad(after(active, out_grad), route_grad)
     out_grad = lax.all_to_all(out_grad, "ctx", split_axis=0, concat_axis=0, tiled=True)
     out_grad = out_grad.reshape(total, columns)
     w_out_grad = fsdp_sum_low(
         after(w_out_grad, out_grad).reshape(contexts, splits * own_rows, width)
     )
-    down_w_grad = fsdp_sum_low(after(down_product, out_grad))
+    gate_w_grad = fsdp_sum_low(after(gate_product, out_grad))
+    up_w_grad = fsdp_sum_low(after(up_product, out_grad))
 
     log_rows = log_rows.reshape(columns // HEAD, 1, total)
-    held, dots, waits = None, 0.0, (out_grad, down_product[0, :8, :128])
+    held, dots, waits = None, 0.0, (out_grad,)
     for head in range(columns // HEAD):
         if head == 1:
             result_sum.prepare(result_terms, dots)
-            waits = result_sum.payload + (gate_w_grad,)
+            waits = result_sum.payload
         if head < 2:
             result_sum.send(out_grad)
         *held, part = attend_backward(
@@ -1608,7 +1605,7 @@
         )
         dots = dots + part
     query_scaled, key_scaled, value_grad, query_gain_grad, key_gain_grad = held
-    dots = after(dots, up_w_grad, result_sum.to_before, result_sum.to_after)
+    dots = after(dots, result_sum.to_before, result_sum.to_after)
     result_sum.prepare(result_terms, dots)
     dots = sum_over_ctx(dots, contexts) / width
     dots = after(dots, *result_sum.payload)
@@ -1646,24 +1643,40 @@
     for step in range(half - 1, 0, -1):
         start = far[0].shape[0] if step == half - 1 else 0
         if step == half - 2:
-            done = (heads_product,)
+            done = (heads_product, down_product, gate_w_grad)
         if step == 1:
-            done = (down_w_grad,)
-        hidden_sum.payload = (
+            done = (heads_w_grad, up_w_grad)
+        hidden_sum.payload = sent = (
             term(-step, *done, got=hidden_sum.to_before),
             term(step, *done, got=hidden_sum.to_after, start=start),
         )
         hidden_sum.send()
+        if step == half - 1:
+            down_product = weight_grad(after(active, *sent), route_grad)
+            down_w_grad = fsdp_sum_low(down_product)
+            heads_w_grad = lax.all_to_all(
+                heads_w_grad, "ctx", split_axis=0, concat_axis=0, tiled=True
+            )
         done = ()
-    hidden_grad, w_out_grad = own_term(
-        owner(0)[None], heads_grad, w_t, w_out_grad, rows, hidden_sum.to_before, hidden_sum.to_after
+    input_grad = input_grad_of(
+        owner(0)[None],
+        heads_grad,
+        w_t,
+        hidden_sum.to_before,
+        hidden_sum.to_after,
+        tokens[0],
+        gain_attn[None],
+        mixed_grad,
+    )
+    w_out_grad = (
+        lax.dynamic_index_in_dim(w_out_grad, me, 0, keepdims=False).astype(jnp.float32)
+        + hidden_sum.to_before[rows:].astype(jnp.float32)
+        + hidden_sum.to_after[rows:].astype(jnp.float32)
     )
     routed = result_sum.finish(result_terms[0])
     output = (mixed + routed)[None]
 
-    heads_w_grad = lax.all_to_all(
-        heads_w_grad, "ctx", split_axis=0, concat_axis=0, tiled=True
-    ).astype(jnp.float32)
+    heads_w_grad = heads_w_grad.astype(jnp.float32)
     other_grads = jnp.sum(heads_w_grad[:, :, 3 * columns : 3 * columns + 3], axis=0)
     heads_w_grad = jnp.transpose(
         heads_w_grad[:, :, : 3 * columns].reshape(contexts, own_rows, 3, columns), (2, 1, 0, 3)
@@ -1676,12 +1689,6 @@
         axis=1,
     ) / attn_gain.astype(jnp.float32)
 
-    attn_inv = lax.rsqrt(jnp.mean(inputs * inputs, axis=-1, keepdims=True) + EPSILON)
-    normed = inputs * attn_inv
-    scaled = hidden_grad * gain_attn
-    input_grad = mixed_grad + attn_inv * (
-        scaled - normed * jnp.mean(scaled * normed, axis=-1, keepdims=True)
-    )
     return (
         output,
         input_grad[None],

time: 1450 us -> 1390 us (0.959)
  waiting for transfers between devices: 477 us -> 414 us
    ppermute x12, waiting for transfers between devices: 120 us -> 56.5 us  [send(): self.to_after = lax.ppermute(past, 'ctx', self.up)]
    all_to_all x1, waiting for transfers between devices: 1.22 us -> 50.1 us  [shards_by_heads(): lax.all_to_all(heads_w_grad, 'ctx', split_axis=0, concat_axis=0, tiled=True)]
    ppermute x12, waiting for transfers between devices: 91.5 us -> 53.8 us  [send(): self.to_before = lax.ppermute(before, 'ctx', self.down)]
  transfers between devices with their start and end apart: 74 -> 74, of which waited for: 35 -> 32; matrix products, arithmetic and copies ran while one was open for 15% -> 16% of each run, Pallas kernels for 40% -> 41%
where the time goes in v3:
time: 1390 us; the launch traced here: 1370 us
  Pallas kernels  590 us (42%)
  waiting for transfers between devices  414 us (30%)
  matrix products  102 us (7%)
  other arithmetic  98.9 us (7%)
  starting transfers between devices  94.5 us (7%)
  local copies, waits for them, and re-layouts  57 us (4%)
  between operations  15.8 us (1%)
    pallas_call x10, Pallas kernels, experts_stage(): pl.pallas_call(partial(kernel, count=count, slots=slots, aliased=len(held...  313 us
    ppermute x9, waiting for transfers between devices, advance(): self.from_before = lax.ppermute(before, 'ctx', self.up)  159 us
    pallas_call x2, Pallas kernels, attend_backward(): pl.pallas_call(partial(attend_backward_kernel, size=size, prompt_rows=pro...  91 us
    dot_general x3, matrix products, weight_grad(): jnp.einsum('emd,emf->edf', left, right, preferred_element_type=jnp.float32)  85.5 us
    ppermute x12, waiting for transfers between devices, send(): self.to_after = lax.ppermute(past, 'ctx', self.up)  56.5 us
    ppermute x12, waiting for transfers between devices, send(): self.to_before = lax.ppermute(before, 'ctx', self.down)  53.8 us
    pallas_call x1, Pallas kernels, attend_forward(): pl.pallas_call(partial(attend_forward_kernel, size=size, prompt_rows=prom...  52.4 us
    all_to_all x1, waiting for transfers between devices, shards_by_heads(): lax.all_to_all(heads_w_grad, 'ctx', split_axis=0, concat_axis=0, tiled=True)  50.1 us
  transfers between devices with their start and end apart: 74, of which 32 were waited for; matrix products, arithmetic and copies ran while one was open for 16% of the time, Pallas kernels for 41%

profile of v3, /device:TPU:14, one launch (start us, length us, event | category | flops | bytes accessed | tf_op | source)
XLA Modules:
  0.0 1371.6 jit_solution(7855311692099309711)
XLA Ops:
  46.8 51.1 %collective-permute-done.1.refs_1_.refs_7_ = bf16[576,2048]{1,0:T(8,128)(2,1)S(1)} collective-permute-done((bf16[576,2048]{1,0:T(8,128)(2,1)S(1)}, bf16[576,2048]{1,0:T(8,128)(2,1)S(1)}, u32[]{:S(2)}, u32[]{:S(2)}) %collective-permute-start.1) | collective-permute-done | bytes 2359328 | tf_op jit(solution)/shard_map/ppermute | solution.py:1270
  100.0 50.5 %collective-permute-done.2.refs_3_.refs_6_ = bf16[576,2048]{1,0:T(8,128)(2,1)} collective-permute-done((bf16[576,2048]{1,0:T(8,128)(2,1)S(1)}, bf16[576,2048]{1,0:T(8,128)(2,1)}, u32[]{:S(2)}, u32[]{:S(2)}) %collective-permute-start.2) | collective-permute-done | bytes 2359328 | tf_op jit(solution)/shard_map/ppermute | solution.py:1270
  163.6 21.4 %project.3 = (bf16[4096,2048]{1,0:T(8,128)(2,1)}, f32[256,4096]{1,0:T(8,128)}, f32[256,4096]{1,0:T(8,128)}, bf16[256,4096]{1,0:T(8,128)(2,1)}, f32[2,4096]{1,0:T(2,128)}) custom-call(s32[5]{0:T(128)} %compare_select_fusion.12.places, bf16[576,2048]{1,0:T(8,128)(2,1)} %copy-done.4, bf16[576,2048]{1,0:T(8,128)(2,1)} %copy-done.10, ...), custom_call_target="tpu_custom_call" | custom-call | flops 8053063680 | bytes 30670848 | tf_op jit(solution)/shard_map/project/pallas_call | solution.py:818
  185.0 17.2 %collective-permute-done.3.refs_0_.refs_5_ = bf16[576,2048]{1,0:T(8,128)(2,1)S(1)} collective-permute-done((bf16[576,2048]{1,0:T(8,128)(2,1)}, bf16[576,2048]{1,0:T(8,128)(2,1)S(1)}, u32[]{:S(2)}, u32[]{:S(2)}) %collective-permute-start.3) | collective-permute-done | bytes 2359328 | tf_op jit(solution)/shard_map/ppermute | solution.py:1270
  209.4 10.2 project.4
  219.6 10.4 collective-permute-done.14
  237.1 6.0 project.5
  265.2 52.4 %attend_forward.1 = (bf16[4096,256]{1,0:T(8,128)(2,1)}, bf16[4096,256]{1,0:T(8,128)(2,1)}, bf16[4096,256]{1,0:T(8,128)(2,1)}, bf16[256,4096]{1,0:T(8,128)(2,1)}, f32[2,4096]{1,0:T(2,128)}) custom-call(s32[3]{0:T(128)} %bitcast_subtract_fusion.starts, f32[256,4096]{1,0:T(8,128)} %get-tuple-element.180.query_pre, f32[256,4096]{1,0:T(8,128)} %get-tuple-element.181.key_pre, ...), custom_call_target="tpu_custom_call" | custom-call | flops 25769803776 | bytes 20971520 | tf_op jit(solution)/shard_map/attend_forward/pallas_call | solution.py:597
  317.6 6.7 all-to-all-start
  328.3 35.2 %all-to-all-done = bf16[8,512,256]{2,1,0:T(8,128)(2,1)} async-done(((bf16[8,512,256]{2,1,0:T(8,128)(2,1)}), bf16[8,512,256]{2,1,0:T(8,128)(2,1)}, u32[]{:S(2)}, u32[]{:S(2)}) %all-to-all-start) | async-done | bytes 2097184 | tf_op jit(solution)/shard_map/all_to_all | solution.py:1474
  363.5 7.8 multiply_reduce_fusion.2
  382.1 24.4 %experts_forward.5 = (bf16[2,2560,2048]{2,1,0:T(8,128)(2,1)}, bf16[2,2560,1024]{2,1,0:T(8,128)(2,1)}, bf16[2,320,1024]{2,1,0:T(8,128)(2,1)}, bf16[2,320,1024]{2,1,0:T(8,128)(2,1)}, bf16[512,2048]{1,0:T(8,128)(2,1)}) custom-call(s32[1,2,1,512]{3,2,1,0:T(1,128)} %get-tuple-element.192.refs_0_, f32[1,2,1,512]{3,2,1,0:T(1,128)} %get-tuple-element.350.refs_1_, ...), custom_call_target="tpu_custom_call" | custom-call | flops 10737418240 | bytes 33554432 | tf_op jit(solution)/shard_map/experts_forward/pallas_call | solution.py:1221
  411.9 22.6 %experts_backward.5 = (bf16[2,2560,2048]{2,1,0:T(8,128)(2,1)}, bf16[2,2560,1024]{2,1,0:T(8,128)(2,1)}, bf16[2,2560,1024]{2,1,0:T(8,128)(2,1)}, bf16[512,2048]{1,0:T(8,128)(2,1)}) custom-call(s32[1,2,1,512]{3,2,1,0:T(1,128)} %get-tuple-element.192.refs_0_, f32[1,2,1,512]{3,2,1,0:T(1,128)} %get-tuple-element.350.refs_1_, bf16[512,2048]{1,0:T(8,128)(2,1)} %bitcast.155, ...), custom_call_target="tpu_custom_call" | custom-call | tf_op jit(solution)/shard_map/experts_backward/pallas_call | solution.py:1221
  434.6 18.9 %collective-permute-done.22.refs_2_ = bf16[512,2048]{1,0:T(8,128)(2,1)} collective-permute-done((bf16[512,2048]{1,0:T(8,128)(2,1)S(1)}, bf16[512,2048]{1,0:T(8,128)(2,1)}, u32[]{:S(2)}, u32[]{:S(2)}) %collective-permute-start.22) | collective-permute-done | bytes 2097184 | tf_op jit(solution)/shard_map/ppermute | solution.py:1270
  458.4 36.9 %experts_forward.6 = (bf16[2,2560,2048]{2,1,0:T(8,128)(2,1)}, bf16[2,2560,1024]{2,1,0:T(8,128)(2,1)}, bf16[2,640,1024]{2,1,0:T(8,128)(2,1)}, bf16[2,640,1024]{2,...) custom-call(s32[2,2,1,512]{3,2,1,0:T(1,128)} %pad_add_fusion.2.refs_, ...), custom_call_target="tpu_custom_call", output_to_operand_aliasing={{0}: (7, {}), {1}: (8, {})} | custom-call | flops 21474836480 | bytes 41943040 | tf_op jit(solution)/shard_map/experts_forward/pallas_call | solution.py:1221
  495.3 36.1 %experts_backward.6 = (bf16[2,2560,2048]{2,1,0:T(8,128)(2,1)}, bf16[2,2560,1024]{2,1,0:T(8,128)(2,1)}, bf16[2,2560,1024]{2,1,0:T(8,128)(2,1)}, bf16[512,2048]{1,0:T(8,128)(2,1)}, bf16[512,2048]{1,0:T(8,128)(2,1)}) custom-call(s32[2,2,1,512]{3,2,1,0:T(1,128)} %pad_add_fusion.2.refs_0_, ...), custom_call_target="tpu_custom_call", output_to_operand_aliasing={{0}: (9, {}), {1}: (10, {}), {2}: (11, {})} | custom-call | tf_op jit(solution)/shard_map/experts_backward/pallas_call | solution.py:1221
  534.0 13.2 collective-permute-done.24.refs_2_
  547.3 37.4 %experts_forward.7 = (bf16[2,2560,2048]{2,1,0:T(8,128)(2,1)}, bf16[2,2560,1024]{2,1,0:T(8,128)(2,1)}, bf16[2,640,1024]{2,1,0:T(8,128)(2,1)}, bf16[2,640,1024]{2,...) custom-call(s32[2,2,1,512]{3,2,1,0:T(1,128)} %pad_add_fusion.1.refs_, ...), custom_call_target="tpu_custom_call", output_to_operand_aliasing={{0}: (7, {}), {1}: (8, {})} | custom-call | flops 21474836480 | bytes 41943040 | tf_op jit(solution)/shard_map/experts_forward/pallas_call | solution.py:1221
  592.0 36.9 %experts_forward.8 = (bf16[2,2560,2048]{2,1,0:T(8,128)(2,1)}, bf16[2,2560,1024]{2,1,0:T(8,128)(2,1)}, bf16[2,640,1024]{2,1,0:T(8,128)(2,1)}, bf16[2,640,1024]{2,...) custom-call(s32[2,2,1,512]{3,2,1,0:T(1,128)} %pad_add_fusion.refs_0_, ...), custom_call_target="tpu_custom_call", output_to_operand_aliasing={{0}: (7, {}), {1}: (8, {})} | custom-call | flops 21474836480 | bytes 41943040 | tf_op jit(solution)/shard_map/experts_forward/pallas_call | solution.py:1221
  636.7 24.6 %experts_forward.9 = (bf16[2,2560,2048]{2,1,0:T(8,128)(2,1)}, bf16[2,2560,1024]{2,1,0:T(8,128)(2,1)}, bf16[2,320,1024]{2,1,0:T(8,128)(2,1)}, bf16[2,320,1024]{2,1,0:T(8,128)(2,1)}, bf16[512,2048]{1,0:T(8,128)(2,1)}) custom-call(s32[1,2,1,512]{3,2,1,0:T(1,128)} %get-tuple-element.228.refs_0_, ...), custom_call_target="tpu_custom_call", output_to_operand_aliasing={{0}: (6, {}), {1}: (7, {})} | custom-call | flops 10737418240 | bytes 33554432 | tf_op jit(solution)/shard_map/experts_forward/pallas_call | solution.py:1221
  669.6 22.7 %experts_backward.7 = (bf16[2,2560,2048]{2,1,0:T(8,128)(2,1)}, bf16[2,2560,1024]{2,1,0:T(8,128)(2,1)}, bf16[2,2560,1024]{2,1,0:T(8,128)(2,1)}, bf16[512,2048]{1,0:T(8,128)(2,1)}) custom-call(s32[1,2,1,512]{3,2,1,0:T(1,128)} %get-tuple-element.228.refs_0_, ...), custom_call_target="tpu_custom_call", output_to_operand_aliasing={{0}: (8, {}), {1}: (9, {}), {2}: (10, {})} | custom-call | flops 10737418240 | bytes 33554432 | tf_op jit(solution)/shard_map/experts_backward/pallas_call | solution.py:1221
  697.8 35.9 %experts_backward.8 = (bf16[2,2560,2048]{2,1,0:T(8,128)(2,1)}, bf16[2,2560,1024]{2,1,0:T(8,128)(2,1)}, bf16[2,2560,1024]{2,1,0:T(8,128)(2,1)}, bf16[512,2048]{1,0:T(8,128)(2,1)}, bf16[512,2048]{1,0:T(8,128)(2,1)}) custom-call(s32[2,2,1,512]{3,2,1,0:T(1,128)} %pad_add_fusion.refs_0_, ...), custom_call_target="tpu_custom_call", output_to_operand_aliasing={{0}: (9, {}), {1}: (10, {}), {2}: (11, {})} | custom-call | flops 21474836480 | bytes 41943040 | tf_op jit(solution)/shard_map/experts_backward/pallas_call | solution.py:1221
  743.0 35.5 %experts_backward.9 = (bf16[2,2560,2048]{2,1,0:T(8,128)(2,1)}, bf16[2,2560,1024]{2,1,0:T(8,128)(2,1)}, bf16[2,2560,1024]{2,1,0:T(8,128)(2,1)}, bf16[512,2048]{1,0:T(8,128)(2,1)}, bf16[512,2048]{1,0:T(8,128)(2,1)}) custom-call(s32[2,2,1,512]{3,2,1,0:T(1,128)} %pad_add_fusion.1.refs_0_, ...), custom_call_target="tpu_custom_call", output_to_operand_aliasing={{0}: (9, {}), {1}: (10, {}), {2}: (11, {})} | custom-call | flops 21474836480 | bytes 41943040 | tf_op jit(solution)/shard_map/experts_backward/pallas_call | solution.py:1221
  789.1 26.8 %convolution_convert_fusion.3 = bf16[2,2048,1024]{2,1,0:T(8,128)(2,1)} fusion(bf16[2,2560,2048]{2,1,0:T(8,128)(2,1)} %get-tuple-element.262, bf16[2,2560,1024]{2,1,0:T(8,128)(2,1)S(1)} %copy-done.2), kind=kOutput, calls=%fused_computation.4 | convolution fusion | flops 21479030784 | bytes 39845888 | tf_op jit(solution)/shard_map/emd,emf->edf/dot_general | solution.py:1534
  815.9 8.7 collective-permute-done.41
  839.4 26.9 %convolution_convert_fusion.2 = bf16[2,2048,1024]{2,1,0:T(8,128)(2,1)} fusion(bf16[2,2560,2048]{2,1,0:T(8,128)(2,1)} %get-tuple-element.262, bf16[2,2560,1024]{2,1,0:T(8,128)(2,1)S(1)} %bitcast.154), kind=kOutput, calls=%fused_computation.3 | convolution fusion | flops 21479030784 | bytes 39845888 | tf_op jit(solution)/shard_map/emd,emf->edf/dot_general | solution.py:1534
  878.3 5.8 fusion.24
  884.1 8.8 out_grad.1
  892.9 5.9 all-to-all-start.1
  903.4 8.3 convolution_convert_fusion
  911.7 23.1 %all-to-all-done.1 = bf16[8,512,256]{2,1,0:T(8,128)(2,1)} async-done(((bf16[8,512,256]{2,1,0:T(8,128)(2,1)}), bf16[8,512,256]{2,1,0:T(8,128)(2,1)}, u32[]{:S(2)}, u32[]{:S(2)}) %all-to-all-start.1) | async-done | bytes 2097184 | tf_op jit(solution)/shard_map/all_to_all | solution.py:1587
  940.2 45.4 %attend_backward.2 = (f32[256,4096]{1,0:T(8,128)}, f32[256,4096]{1,0:T(8,128)}, bf16[256,4096]{1,0:T(8,128)(2,1)}, f32[256,1]{1,0:T(8,128)}, f32[256,1]{1,0:T(8,128)}, /*index=5*/f32[2,4096]{1,0:T(2,128)}) custom-call(s32[3]{0:T(128)} %bitcast_subtract_fusion.starts, bf16[4096,256]{1,0:T(8,128)(2,1)} %get-tuple-element.268.query, ...), custom_call_target="tpu_custom_call" | custom-call | flops 25769803776 | bytes 20971520 | tf_op jit(solution)/shard_map/attend_backward/pallas_call | solution.py:753
  995.6 45.6 %attend_backward.3 = (f32[256,4096]{1,0:T(8,128)}, f32[256,4096]{1,0:T(8,128)}, bf16[256,4096]{1,0:T(8,128)(2,1)}, f32[256,1]{1,0:T(8,128)}, f32[256,1]{1,0:T(8,128)}, /*index=5*/f32[2,4096]{1,0:T(2,128)}) custom-call(s32[3]{0:T(128)} %bitcast_subtract_fusion.starts, ...), custom_call_target="tpu_custom_call", output_to_operand_aliasing={{0}: (16, {}), {1}: (17, {}), {2}: (18, {}), {3}: (19, {}),... | custom-call | flops 25769803776 | bytes 20971520 | tf_op jit(solution)/shard_map/attend_backward/pallas_call | solution.py:753
  1058.6 9.5 heads_grad.1
  1075.5 19.3 %heads_product.1 = bf16[8,256,896]{2,1,0:T(8,128)(2,1)} custom-call(bf16[768,4096]{1,0:T(8,128)(2,1)} %heads_grad.1, bf16[4096,2048]{1,0:T(8,128)(2,1)} %get-tuple-element.295.hidden, f32[2048,128]{1,0:T(8,128)} %maximum_maximum_fusion.others), custom_call_target="tpu_custom_call" | custom-call | flops 12884901888 | bytes 23068672 | tf_op jit(solution)/shard_map/heads_product/pallas_call | solution.py:1042
  1099.0 37.5 %collective-permute-done.52 = bf16[512,2048]{1,0:T(8,128)(2,1)S(1)} collective-permute-done((bf16[512,2048]{1,0:T(8,128)(2,1)}, bf16[512,2048]{1,0:T(8,128)(2,1)S(1)}, u32[]{:S(2)}, u32[]{:S(2)}) %collective-permute-start.52) | collective-permute-done | bytes 2097184 | tf_op jit(solution)/shard_map/ppermute | solution.py:1316
  1136.5 6.5 hidden_term.8
  1148.7 31.8 %convolution_convert_fusion.1 = bf16[2,1024,2048]{2,1,0:T(8,128)(2,1)} fusion(bf16[2,2560,1024]{2,1,0:T(8,128)(2,1)} %get-tuple-element.309, bf16[2,2560,2048]{2,1,0:T(8,128)(2,1)} %get-tuple-element.310), kind=kOutput, calls=%fused_computation.2 | convolution fusion | flops 21479030784 | bytes 39845888 | tf_op jit(solution)/shard_map/emd,emf->edf/dot_general | solution.py:1534
  1182.6 41.8 %collective-permute-done.55.refs_0_ = bf16[576,2048]{1,0:T(8,128)(2,1)S(1)} collective-permute-done((bf16[576,2048]{1,0:T(8,128)(2,1)}, bf16[576,2048]{1,0:T(8,128)(2,1)S(1)}, u32[]{:S(2)}, u32[]{:S(2)}) %collective-permute-start.55) | collective-permute-done | bytes 2359328 | tf_op jit(solution)/shard_map/ppermute | solution.py:1315
  1225.9 7.2 hidden_term.10
  1233.1 6.1 hidden_term.12
  1246.0 50.1 %all-to-all-done.2 = bf16[8,64,896]{2,1,0:T(8,128)(2,1)S(1)} async-done(((bf16[8,64,896]{2,1,0:T(8,128)(2,1)}), bf16[8,64,896]{2,1,0:T(8,128)(2,1)S(1)}, u32[]{:S(2)}, u32[]{:S(2)}) %all-to-all-start.2) | async-done | bytes 917536 | tf_op jit(solution)/shard_map/all_to_all | solution.py:1657
  1297.5 6.0 hidden_term.11
  1307.0 6.1 hidden_term.13
  1314.9 7.0 add_bitcast_fusion
  1335.9 6.2 collective-permute-done.57.before
  1342.1 7.2 collective-permute-done.60.past
  1349.2 9.1 input_grad.1
  (410 shorter events, 285.1 us)
Async XLA Ops:
  7.2 145.8 %all-gather.6.cloned.1.call-start = ((), (), s32[]{:S(2)}) async-start(), calls=%async_computation.8 | async-start | bytes 4587520 | tf_op jit(solution)/shard_map/all_gather | solution.py:1423
  43.0 159.6 %all-gather.8.cloned.1.call-start = ((), (), s32[]{:S(2)}) async-start(), calls=%async_computation.9 | async-start | bytes 10485760 | tf_op jit(solution)/shard_map/all_gather | solution.py:1424
  43.7 158.8 %all-gather.10.cloned.1.call-start = ((), (), s32[]{:S(2)}) async-start(), calls=%async_computation.10 | async-start | bytes 10485760 | tf_op jit(solution)/shard_map/all_gather | solution.py:1422
  44.4 319.1 %all-gather.12.cloned.1.call-start = ((), (), s32[]{:S(2)}) async-start(), calls=%async_computation.11 | async-start | bytes 10485760 | tf_op jit(solution)/shard_map/all_gather | solution.py:1461
  44.7 53.2 %collective-permute-start.1 = (bf16[576,2048]{1,0:T(8,128)(2,1)S(1)}, bf16[576,2048]{1,0:T(8,128)(2,1)S(1)}, u32[]{:S(2)}, u32[]{:S(2)}) collective-permute-start(bf16[576,2048]{1,0:T(8,128)(2,1)S(1)} %pad_maximum_fusion.refs_0_), channel_id=1, source_target_pairs={{0,8},{8,16},{16,24},{24,28},{28,20},{20,12},{12,4},{4,0},{1,9},{9... | collective-permute-start | bytes 7077896 | tf_op jit(solution)/shard_map/ppermute | solution.py:1270
  45.8 52.5 %collective-permute-start.4 = (bf16[576,2048]{1,0:T(8,128)(2,1)S(1)}, bf16[576,2048]{1,0:T(8,128)(2,1)S(1)}, u32[]{:S(2)}, u32[]{:S(2)}) collective-permute-start(bf16[576,2048]{1,0:T(8,128)(2,1)S(1)} %pad_maximum_fusion.refs_0_), channel_id=1, source_target_pairs={{8,0},{16,8},{24,16},{28,24},{20,28},{12,20},{4,12},{0,4},{9,1},{1... | collective-permute-start | bytes 7077896 | tf_op jit(solution)/shard_map/ppermute | solution.py:1271
  97.9 52.5 %collective-permute-start.2 = (bf16[576,2048]{1,0:T(8,128)(2,1)S(1)}, bf16[576,2048]{1,0:T(8,128)(2,1)}, u32[]{:S(2)}, u32[]{:S(2)}) collective-permute-start(bf16[576,2048]{1,0:T(8,128)(2,1)S(1)} %collective-permute-done.1.refs_1_.refs_7_), channel_id=1, source_target_pairs={{0,8},{8,16},{16,24},{24,28},{28,20},{20,12},{12,4},{4,0},{1,9},{9... | collective-permute-start | bytes 7077896 | tf_op jit(solution)/shard_map/ppermute | solution.py:1270
  98.2 52.5 %collective-permute-start.5 = (bf16[576,2048]{1,0:T(8,128)(2,1)S(1)}, bf16[576,2048]{1,0:T(8,128)(2,1)}, u32[]{:S(2)}, u32[]{:S(2)}) collective-permute-start(bf16[576,2048]{1,0:T(8,128)(2,1)S(1)} %collective-permute-done.4.refs_2_.refs_1_), channel_id=1, source_target_pairs={{8,0},{16,8},{24,16},{28,24},{20,28},{12,20},{4,12},{0,4},{9,1},{1... | collective-permute-start | bytes 7077896 | tf_op jit(solution)/shard_map/ppermute | solution.py:1271
  150.5 51.7 %collective-permute-start.3 = (bf16[576,2048]{1,0:T(8,128)(2,1)}, bf16[576,2048]{1,0:T(8,128)(2,1)S(1)}, u32[]{:S(2)}, u32[]{:S(2)}) collective-permute-start(bf16[576,2048]{1,0:T(8,128)(2,1)} %collective-permute-done.2.refs_3_.refs_6_), channel_id=1, source_target_pairs={{0,8},{8,16},{16,24},{24,28},{28,20},{20,12},{12,4},{4,0},{1,9},{9... | collective-permute-start | bytes 7077896 | tf_op jit(solution)/shard_map/ppermute | solution.py:1270
  150.8 51.8 %collective-permute-start.6 = (bf16[576,2048]{1,0:T(8,128)(2,1)}, bf16[576,2048]{1,0:T(8,128)(2,1)}, u32[]{:S(2)}, u32[]{:S(2)}) collective-permute-start(bf16[576,2048]{1,0:T(8,128)(2,1)} %collective-permute-done.5.refs_4_.refs_2_), channel_id=1, source_target_pairs={{8,0},{16,8},{24,16},{28,24},{20,28},{12,20},{4,12},{0,4},{9,1},{1... | collective-permute-start | bytes 7077896 | tf_op jit(solution)/shard_map/ppermute | solution.py:1271
  246.8 135.3 %all-gather.14.cloned.1.call-start = ((), (), s32[]{:S(2)}) async-start(), calls=%async_computation.12 | async-start | bytes 10485760 | tf_op jit(solution)/shard_map/all_gather | solution.py:1462
  262.5 55.1 %collective-permute-start.18 = (bf16[512,2048]{1,0:T(8,128)(2,1)S(1)}, bf16[512,2048]{1,0:T(8,128)(2,1)}, u32[]{:S(2)}, u32[]{:S(2)}) collective-permute-start(bf16[512,2048]{1,0:T(8,128)(2,1)S(1)} %bitcast.156), channel_id=1, source_target_pairs={{0,8},{8,16},{16,24},{24,28},{28,20},{20,12},{12,4},{4,0},{1,9},{9... | collective-permute-start | bytes 6291464 | tf_op jit(solution)/shard_map/ppermute | solution.py:1270
  263.0 54.6 %collective-permute-start.19 = (bf16[512,2048]{1,0:T(8,128)(2,1)S(1)}, bf16[512,2048]{1,0:T(8,128)(2,1)}, u32[]{:S(2)}, u32[]{:S(2)}) collective-permute-start(bf16[512,2048]{1,0:T(8,128)(2,1)S(1)} %bitcast.157), channel_id=1, source_target_pairs={{8,0},{16,8},{24,16},{28,24},{20,28},{12,20},{4,12},{0,4},{9,1},{1... | collective-permute-start | bytes 6291464 | tf_op jit(solution)/shard_map/ppermute | solution.py:1271
  317.6 45.9 %all-to-all-start = ((bf16[8,512,256]{2,1,0:T(8,128)(2,1)}), bf16[8,512,256]{2,1,0:T(8,128)(2,1)}, u32[]{:S(2)}, u32[]{:S(2)}) async-start(bf16[8,512,256]{2,1,0:T(8,128)(2,1)} %bitcast.171), calls=%async_computation | async-start | bytes 4194304 | tf_op jit(solution)/shard_map/all_to_all | solution.py:1474
  326.3 85.7 %collective-permute-start.20 = (bf16[512,2048]{1,0:T(8,128)(2,1)}, bf16[512,2048]{1,0:T(8,128)(2,1)}, u32[]{:S(2)}, u32[]{:S(2)}) collective-permute-start(bf16[512,2048]{1,0:T(8,128)(2,1)} %collective-permute-done.18.refs_2_), channel_id=1, source_target_pairs={{0,8},{8,16},{16,24},{24,28},{28,20},{20,12},{12,4},{4,0},{1,9},{9... | collective-permute-start | bytes 6291464 | tf_op jit(solution)/shard_map/ppermute | solution.py:1270
  326.9 85.1 %collective-permute-start.21 = (bf16[512,2048]{1,0:T(8,128)(2,1)}, bf16[512,2048]{1,0:T(8,128)(2,1)}, u32[]{:S(2)}, u32[]{:S(2)}) collective-permute-start(bf16[512,2048]{1,0:T(8,128)(2,1)} %collective-permute-done.19.refs_3_), channel_id=1, source_target_pairs={{8,0},{16,8},{24,16},{28,24},{20,28},{12,20},{4,12},{0,4},{9,1},{1... | collective-permute-start | bytes 6291464 | tf_op jit(solution)/shard_map/ppermute | solution.py:1271
  373.3 80.2 %collective-permute-start.22 = (bf16[512,2048]{1,0:T(8,128)(2,1)S(1)}, bf16[512,2048]{1,0:T(8,128)(2,1)}, u32[]{:S(2)}, u32[]{:S(2)}) collective-permute-start(bf16[512,2048]{1,0:T(8,128)(2,1)S(1)} %multiply_convert_fusion.refs_2_), channel_id=1, source_target_pairs={{0,8},{8,16},{16,24},{24,28},{28,20},{20,12},{12,4},{4,0},{1,9},{9... | collective-permute-start | bytes 6291464 | tf_op jit(solution)/shard_map/ppermute | solution.py:1270
  378.2 75.2 %collective-permute-start.23 = (bf16[512,2048]{1,0:T(8,128)(2,1)S(1)}, bf16[512,2048]{1,0:T(8,128)(2,1)}, u32[]{:S(2)}, u32[]{:S(2)}) collective-permute-start(bf16[512,2048]{1,0:T(8,128)(2,1)S(1)} %multiply_convert_fusion.refs_2_), channel_id=1, source_target_pairs={{8,0},{16,8},{24,16},{28,24},{20,28},{12,20},{4,12},{0,4},{9,1},{1... | collective-permute-start | bytes 6291464 | tf_op jit(solution)/shard_map/ppermute | solution.py:1271
  453.5 77.8 %collective-permute-start.26 = (bf16[512,2048]{1,0:T(8,128)(2,1)}, bf16[512,2048]{1,0:T(8,128)(2,1)}, u32[]{:S(2)}, u32[]{:S(2)}) collective-permute-start(bf16[512,2048]{1,0:T(8,128)(2,1)} %collective-permute-done.22.refs_2_), channel_id=1, source_target_pairs={{0,8},{8,16},{16,24},{24,28},{28,20},{20,12},{12,4},{4,0},{1,9},{9... | collective-permute-start | bytes 6291464 | tf_op jit(solution)/shard_map/ppermute | solution.py:1270
  453.5 77.9 %collective-permute-start.27 = (bf16[512,2048]{1,0:T(8,128)(2,1)}, bf16[512,2048]{1,0:T(8,128)(2,1)}, u32[]{:S(2)}, u32[]{:S(2)}) collective-permute-start(bf16[512,2048]{1,0:T(8,128)(2,1)} %collective-permute-done.23.refs_3_), channel_id=1, source_target_pairs={{8,0},{16,8},{24,16},{28,24},{20,28},{12,20},{4,12},{0,4},{9,1},{1... | collective-permute-start | bytes 6291464 | tf_op jit(solution)/shard_map/ppermute | solution.py:1271
  456.1 91.1 %collective-permute-start.24 = (bf16[512,2048]{1,0:T(8,128)(2,1)}, bf16[512,2048]{1,0:T(8,128)(2,1)S(1)}, u32[]{:S(2)}, u32[]{:S(2)}) collective-permute-start(bf16[512,2048]{1,0:T(8,128)(2,1)} %collective-permute-done.20.refs_2_), channel_id=1, source_target_pairs={{0,8},{8,16},{16,24},{24,28},{28,20},{20,12},{12,4},{4,0},{1,9},{9... | collective-permute-start | bytes 6291464 | tf_op jit(solution)/shard_map/ppermute | solution.py:1270
  456.1 91.2 %collective-permute-start.25 = (bf16[512,2048]{1,0:T(8,128)(2,1)}, bf16[512,2048]{1,0:T(8,128)(2,1)}, u32[]{:S(2)}, u32[]{:S(2)}) collective-permute-start(bf16[512,2048]{1,0:T(8,128)(2,1)} %collective-permute-done.21.refs_3_), channel_id=1, source_target_pairs={{8,0},{16,8},{24,16},{28,24},{20,28},{12,20},{4,12},{0,4},{9,1},{1... | collective-permute-start | bytes 6291464 | tf_op jit(solution)/shard_map/ppermute | solution.py:1271
  531.3 55.9 %collective-permute-start.28 = (bf16[512,2048]{1,0:T(8,128)(2,1)}, bf16[512,2048]{1,0:T(8,128)(2,1)}, u32[]{:S(2)}, u32[]{:S(2)}) collective-permute-start(bf16[512,2048]{1,0:T(8,128)(2,1)} %collective-permute-done.26.refs_2_), channel_id=1, source_target_pairs={{0,8},{8,16},{16,24},{24,28},{28,20},{20,12},{12,4},{4,0},{1,9},{9... | collective-permute-start | bytes 6291464 | tf_op jit(solution)/shard_map/ppermute | solution.py:1270
  531.4 55.8 %collective-permute-start.29 = (bf16[512,2048]{1,0:T(8,128)(2,1)}, bf16[512,2048]{1,0:T(8,128)(2,1)}, u32[]{:S(2)}, u32[]{:S(2)}) collective-permute-start(bf16[512,2048]{1,0:T(8,128)(2,1)} %collective-permute-done.27.refs_3_), channel_id=1, source_target_pairs={{8,0},{16,8},{24,16},{28,24},{20,28},{12,20},{4,12},{0,4},{9,1},{1... | collective-permute-start | bytes 6291464 | tf_op jit(solution)/shard_map/ppermute | solution.py:1271
  588.5 45.0 %collective-permute-start.31 = (bf16[256,2048]{1,0:T(8,128)(2,1)S(1)}, bf16[256,2048]{1,0:T(8,128)(2,1)}, u32[]{:S(2)}, u32[]{:S(2)}) collective-permute-start(bf16[256,2048]{1,0:T(8,128)(2,1)S(1)} %slice.273), channel_id=1, source_target_pairs={{8,0},{16,8},{24,16},{28,24},{20,28},{12,20},{4,12},{0,4},{9,1},{1... | collective-permute-start | bytes 3145736 | tf_op jit(solution)/shard_map/ppermute | solution.py:1277
  590.5 43.0 %collective-permute-start.30 = (bf16[256,2048]{1,0:T(8,128)(2,1)S(1)}, bf16[256,2048]{1,0:T(8,128)(2,1)}, u32[]{:S(2)}, u32[]{:S(2)}) collective-permute-start(bf16[256,2048]{1,0:T(8,128)(2,1)S(1)} %slice.272), channel_id=1, source_target_pairs={{0,8},{8,16},{16,24},{24,28},{28,20},{20,12},{12,4},{4,0},{1,9},{9... | collective-permute-start | bytes 3145736 | tf_op jit(solution)/shard_map/ppermute | solution.py:1276
  695.8 42.6 %collective-permute-start.36 = (bf16[256,2048]{1,0:T(8,128)(2,1)}, bf16[256,2048]{1,0:T(8,128)(2,1)}, u32[]{:S(2)}, u32[]{:S(2)}) collective-permute-start(bf16[256,2048]{1,0:T(8,128)(2,1)} %get-tuple-element.330), channel_id=1, source_target_pairs={{8,0},{16,8},{24,16},{28,24},{20,28},{12,20},{4,12},{0,4},{9,1},{1... | collective-permute-start | bytes 3145736 | tf_op jit(solution)/shard_map/ppermute | solution.py:1315
  737.8 40.7 %collective-permute-start.40 = (bf16[512,2048]{1,0:T(8,128)(2,1)}, bf16[512,2048]{1,0:T(8,128)(2,1)S(1)}, u32[]{:S(2)}, u32[]{:S(2)}) collective-permute-start(bf16[512,2048]{1,0:T(8,128)(2,1)} %pad_maximum_fusion.5), channel_id=1, source_target_pairs={{0,8},{8,16},{16,24},{24,28},{28,20},{20,12},{12,4},{4,0},{1,9},{9... | collective-permute-start | bytes 6291464 | tf_op jit(solution)/shard_map/ppermute | solution.py:1316
  741.7 41.5 %collective-permute-start.37 = (bf16[512,2048]{1,0:T(8,128)(2,1)}, bf16[512,2048]{1,0:T(8,128)(2,1)}, u32[]{:S(2)}, u32[]{:S(2)}) collective-permute-start(bf16[512,2048]{1,0:T(8,128)(2,1)} %pad_maximum_fusion.4), channel_id=1, source_target_pairs={{8,0},{16,8},{24,16},{28,24},{20,28},{12,20},{4,12},{0,4},{9,1},{1... | collective-permute-start | bytes 6291464 | tf_op jit(solution)/shard_map/ppermute | solution.py:1315
  782.5 42.1 %collective-permute-start.41 = (bf16[512,2048]{1,0:T(8,128)(2,1)}, bf16[512,2048]{1,0:T(8,128)(2,1)}, u32[]{:S(2)}, u32[]{:S(2)}) collective-permute-start(bf16[512,2048]{1,0:T(8,128)(2,1)} %add_convert_fusion.6), channel_id=1, source_target_pairs={{0,8},{8,16},{16,24},{24,28},{28,20},{20,12},{12,4},{4,0},{1,9},{9... | collective-permute-start | bytes 6291464 | tf_op jit(solution)/shard_map/ppermute | solution.py:1316
  787.7 41.9 %collective-permute-start.39 = (bf16[512,2048]{1,0:T(8,128)(2,1)}, bf16[512,2048]{1,0:T(8,128)(2,1)}, u32[]{:S(2)}, u32[]{:S(2)}) collective-permute-start(bf16[512,2048]{1,0:T(8,128)(2,1)} %add_convert_fusion.7), channel_id=1, source_target_pairs={{8,0},{16,8},{24,16},{28,24},{20,28},{12,20},{4,12},{0,4},{9,1},{1... | collective-permute-start | bytes 6291464 | tf_op jit(solution)/shard_map/ppermute | solution.py:1315
  828.3 40.0 %collective-permute-start.43 = (bf16[512,2048]{1,0:T(8,128)(2,1)}, bf16[512,2048]{1,0:T(8,128)(2,1)}, u32[]{:S(2)}, u32[]{:S(2)}) collective-permute-start(bf16[512,2048]{1,0:T(8,128)(2,1)} %add_convert_fusion.4), channel_id=1, source_target_pairs={{0,8},{8,16},{16,24},{24,28},{28,20},{20,12},{12,4},{4,0},{1,9},{9... | collective-permute-start | bytes 6291464 | tf_op jit(solution)/shard_map/ppermute | solution.py:1316
  833.5 39.6 %collective-permute-start.42 = (bf16[512,2048]{1,0:T(8,128)(2,1)}, bf16[512,2048]{1,0:T(8,128)(2,1)}, u32[]{:S(2)}, u32[]{:S(2)}) collective-permute-start(bf16[512,2048]{1,0:T(8,128)(2,1)} %add_convert_fusion.5), channel_id=1, source_target_pairs={{8,0},{16,8},{24,16},{28,24},{20,28},{12,20},{4,12},{0,4},{9,1},{1... | collective-permute-start | bytes 6291464 | tf_op jit(solution)/shard_map/ppermute | solution.py:1315
  892.9 41.9 %all-to-all-start.1 = ((bf16[8,512,256]{2,1,0:T(8,128)(2,1)}), bf16[8,512,256]{2,1,0:T(8,128)(2,1)}, u32[]{:S(2)}, u32[]{:S(2)}) async-start(bf16[8,512,256]{2,1,0:T(8,128)(2,1)} %out_grad.1), calls=%async_computation.1 | async-start | bytes 4194304 | tf_op jit(solution)/shard_map/all_to_all | solution.py:1587
  898.8 169.3 %reduce-scatter.6.cloned.1.call-start = ((), (), s32[]{:S(2)}) async-start(), calls=%async_computation.13 | async-start | bytes 10485760 | tf_op jit(solution)/shard_map/reduce_scatter | solution.py:1572
  934.9 247.8 %reduce-scatter.12.cloned.1.call-start = ((), (), s32[]{:S(2)}) async-start(), calls=%async_computation.16 | async-start | bytes 10485760 | tf_op jit(solution)/shard_map/reduce_scatter | solution.py:1572
  935.6 305.5 %reduce-scatter.8.cloned.1.call-start = ((), (), s32[]{:S(2)}) async-start(), calls=%async_computation.14 | async-start | bytes 4587520 | tf_op jit(solution)/shard_map/reduce_scatter | solution.py:1572
  936.8 48.8 %collective-permute-start.44 = (bf16[512,2048]{1,0:T(8,128)(2,1)}, bf16[512,2048]{1,0:T(8,128)(2,1)}, u32[]{:S(2)}, u32[]{:S(2)}) collective-permute-start(bf16[512,2048]{1,0:T(8,128)(2,1)} %pad_maximum_fusion.6), channel_id=1, source_target_pairs={{8,0},{16,8},{24,16},{28,24},{20,28},{12,20},{4,12},{0,4},{9,1},{1... | collective-permute-start | bytes 6291464 | tf_op jit(solution)/shard_map/ppermute | solution.py:1315
  938.2 51.3 %collective-permute-start.45 = (bf16[512,2048]{1,0:T(8,128)(2,1)}, bf16[512,2048]{1,0:T(8,128)(2,1)}, u32[]{:S(2)}, u32[]{:S(2)}) collective-permute-start(bf16[512,2048]{1,0:T(8,128)(2,1)} %pad_maximum_fusion.7), channel_id=1, source_target_pairs={{0,8},{8,16},{16,24},{24,28},{28,20},{20,12},{12,4},{4,0},{1,9},{9... | collective-permute-start | bytes 6291464 | tf_op jit(solution)/shard_map/ppermute | solution.py:1316
  993.2 50.0 %collective-permute-start.46 = (bf16[512,2048]{1,0:T(8,128)(2,1)}, bf16[512,2048]{1,0:T(8,128)(2,1)}, u32[]{:S(2)}, u32[]{:S(2)}) collective-permute-start(bf16[512,2048]{1,0:T(8,128)(2,1)} %add_convert_fusion.3), channel_id=1, source_target_pairs={{8,0},{16,8},{24,16},{28,24},{20,28},{12,20},{4,12},{0,4},{9,1},{1... | collective-permute-start | bytes 6291464 | tf_op jit(solution)/shard_map/ppermute | solution.py:1315
  993.9 49.3 %collective-permute-start.47 = (bf16[512,2048]{1,0:T(8,128)(2,1)}, bf16[512,2048]{1,0:T(8,128)(2,1)S(1)}, u32[]{:S(2)}, u32[]{:S(2)}) collective-permute-start(bf16[512,2048]{1,0:T(8,128)(2,1)} %add_convert_fusion.2), channel_id=1, source_target_pairs={{0,8},{8,16},{16,24},{24,28},{28,20},{20,12},{12,4},{4,0},{1,9},{9... | collective-permute-start | bytes 6291464 | tf_op jit(solution)/shard_map/ppermute | solution.py:1316
  1096.0 150.1 %reduce-scatter.10.cloned.1.call-start = ((), (), s32[]{:S(2)}) async-start(), calls=%async_computation.15 | async-start | bytes 10485760 | tf_op jit(solution)/shard_map/reduce_scatter | solution.py:1572
  1097.0 263.4 %reduce-scatter.14.cloned.1.call-start = ((), (), s32[]{:S(2)}) async-start(), calls=%async_computation.17 | async-start | bytes 10485760 | tf_op jit(solution)/shard_map/reduce_scatter | solution.py:1572
  1180.6 43.9 %collective-permute-start.55 = (bf16[576,2048]{1,0:T(8,128)(2,1)}, bf16[576,2048]{1,0:T(8,128)(2,1)S(1)}, u32[]{:S(2)}, u32[]{:S(2)}) collective-permute-start(bf16[576,2048]{1,0:T(8,128)(2,1)} %hidden_term.8), channel_id=1, source_target_pairs={{8,0},{16,8},{24,16},{28,24},{20,28},{12,20},{4,12},{0,4},{9,1},{1... | collective-permute-start | bytes 7077896 | tf_op jit(solution)/shard_map/ppermute | solution.py:1315
  1180.7 52.4 %collective-permute-start.58 = (bf16[576,2048]{1,0:T(8,128)(2,1)}, bf16[576,2048]{1,0:T(8,128)(2,1)}, u32[]{:S(2)}, u32[]{:S(2)}) collective-permute-start(bf16[576,2048]{1,0:T(8,128)(2,1)} %hidden_term.9), channel_id=1, source_target_pairs={{0,8},{8,16},{16,24},{24,28},{28,20},{20,12},{12,4},{4,0},{1,9},{9... | collective-permute-start | bytes 7077896 | tf_op jit(solution)/shard_map/ppermute | solution.py:1316
  1233.1 63.0 %collective-permute-start.56 = (bf16[576,2048]{1,0:T(8,128)(2,1)}, bf16[576,2048]{1,0:T(8,128)(2,1)S(1)}, u32[]{:S(2)}, u32[]{:S(2)}) collective-permute-start(bf16[576,2048]{1,0:T(8,128)(2,1)} %hidden_term.10), channel_id=1, source_target_pairs={{8,0},{16,8},{24,16},{28,24},{20,28},{12,20},{4,12},{0,4},{9,1},{1... | collective-permute-start | bytes 7077896 | tf_op jit(solution)/shard_map/ppermute | solution.py:1315
  1239.2 67.8 %collective-permute-start.59 = (bf16[576,2048]{1,0:T(8,128)(2,1)}, bf16[576,2048]{1,0:T(8,128)(2,1)}, u32[]{:S(2)}, u32[]{:S(2)}) collective-permute-start(bf16[576,2048]{1,0:T(8,128)(2,1)} %hidden_term.12), channel_id=1, source_target_pairs={{0,8},{8,16},{16,24},{24,28},{28,20},{20,12},{12,4},{4,0},{1,9},{9... | collective-permute-start | bytes 7077896 | tf_op jit(solution)/shard_map/ppermute | solution.py:1316
  1241.2 54.9 %all-to-all-start.2 = ((bf16[8,64,896]{2,1,0:T(8,128)(2,1)}), bf16[8,64,896]{2,1,0:T(8,128)(2,1)S(1)}, u32[]{:S(2)}, u32[]{:S(2)}) async-start(bf16[8,64,896]{2,1,0:T(8,128)(2,1)} %reduce-scatter.8.cloned.1.call-done), calls=%async_computation.4 | async-start | bytes 1835008 | tf_op jit(solution)/shard_map/all_to_all | solution.py:1657
  (93 other events, 1594.0 us)
Sparse Core Ops, SparseCore 0:
  43.1 31.5 all-gather.5
  76.3 58.2 all-gather.7
  136.1 58.2 all-gather.9
  246.9 57.9 all-gather.11
  306.3 58.2 all-gather.13
  935.0 76.6 reduce-scatter.5
  1014.5 71.7 reduce-scatter.11
  1096.1 44.7 reduce-scatter.7
  1143.6 71.7 reduce-scatter.9
  1217.8 71.6 reduce-scatter.13

commit v4 on v3

--- a/solution.py
+++ b/solution.py
@@ -1645,7 +1645,7 @@
         if step == half - 2:
             done = (heads_product, down_product, gate_w_grad)
         if step == 1:
-            done = (heads_w_grad, up_w_grad)
+            done = (up_w_grad,)
         hidden_sum.payload = sent = (
             term(-step, *done, got=hidden_sum.to_before),
             term(step, *done, got=hidden_sum.to_after, start=start),
@@ -1653,13 +1653,15 @@
         hidden_sum.send()
         if step == half - 1:
             down_product = weight_grad(after(active, *sent), route_grad)
-            down_w_grad = fsdp_sum_low(down_product)
+            down_w_grad = fsdp_sum_low(
+                after(down_product, hidden_sum.to_before, hidden_sum.to_after)
+            )
             heads_w_grad = lax.all_to_all(
                 heads_w_grad, "ctx", split_axis=0, concat_axis=0, tiled=True
             )
         done = ()
     input_grad = input_grad_of(
-        owner(0)[None],
+        after(owner(0)[None], heads_w_grad),
         heads_grad,
         w_t,
         hidden_sum.to_before,

time: 1390 us -> 1390 us (level); the launches traced: 1370 us -> 1390 us
  waiting for transfers between devices: 414 us -> 438 us
    all_to_all x1, waiting for transfers between devices: 50.1 us -> 2.9 us  [shards_by_heads(): lax.all_to_all(heads_w_grad, 'ctx', split_axis=0, concat_axis=0, tiled=True)]
    ppermute x12, waiting for transfers between devices: 53.8 us -> 94.6 us  [send(): self.to_before = lax.ppermute(before, 'ctx', self.down)]
    ppermute x12, waiting for transfers between devices: 56.5 us -> 76.8 us  [send(): self.to_after = lax.ppermute(past, 'ctx', self.up)]
  transfers between devices with their start and end apart: 74 -> 74, of which waited for: 32 -> 36; matrix products, arithmetic and copies ran while one was open for 16% -> 16% of each run, Pallas kernels for 41% -> 41%
where the time goes in v4:
time: 1390 us
  Pallas kernels  586 us (42%)
  waiting for transfers between devices  438 us (32%)
  other arithmetic  99.6 us (7%)
  matrix products  99.6 us (7%)
  starting transfers between devices  92.2 us (7%)
  local copies, waits for them, and re-layouts  57 us (4%)
  between operations  15.9 us (1%)
    pallas_call x10, Pallas kernels, experts_stage(): pl.pallas_call(partial(kernel, count=count, slots=slots, aliased=len(held...  313 us
    ppermute x9, waiting for transfers between devices, advance(): self.from_before = lax.ppermute(before, 'ctx', self.up)  163 us
    ppermute x12, waiting for transfers between devices, send(): self.to_before = lax.ppermute(before, 'ctx', self.down)  94.6 us
    pallas_call x2, Pallas kernels, attend_backward(): pl.pallas_call(partial(attend_backward_kernel, size=size, prompt_rows=pro...  89.4 us
    dot_general x3, matrix products, weight_grad(): jnp.einsum('emd,emf->edf', left, right, preferred_element_type=jnp.float32)  83.1 us
    ppermute x12, waiting for transfers between devices, send(): self.to_after = lax.ppermute(past, 'ctx', self.up)  76.8 us
    pallas_call x1, Pallas kernels, attend_forward(): pl.pallas_call(partial(attend_forward_kernel, size=size, prompt_rows=prom...  49.7 us
    pallas_call x7, Pallas kernels, hidden_term(): pl.pallas_call(partial(hidden_term_kernel, start=start, halves=halves), g...  42.1 us
  transfers between devices with their start and end apart: 74, of which 36 were waited for; matrix products, arithmetic and copies ran while one was open for 16% of the time, Pallas kernels for 41%

profile of v4, /device:TPU:14, one launch (start us, length us, event | category | flops | bytes accessed | tf_op | source)
XLA Modules:
  0.0 1388.4 jit_solution(12158901759813468970)
XLA Ops:
  46.8 51.1 %collective-permute-done.1.refs_1_.refs_7_ = bf16[576,2048]{1,0:T(8,128)(2,1)S(1)} collective-permute-done((bf16[576,2048]{1,0:T(8,128)(2,1)S(1)}, bf16[576,2048]{1,0:T(8,128)(2,1)S(1)}, u32[]{:S(2)}, u32[]{:S(2)}) %collective-permute-start.1) | collective-permute-done | bytes 2359328 | tf_op jit(solution)/shard_map/ppermute | solution.py:1270
  100.0 50.5 %collective-permute-done.2.refs_3_.refs_6_ = bf16[576,2048]{1,0:T(8,128)(2,1)} collective-permute-done((bf16[576,2048]{1,0:T(8,128)(2,1)S(1)}, bf16[576,2048]{1,0:T(8,128)(2,1)}, u32[]{:S(2)}, u32[]{:S(2)}) %collective-permute-start.2) | collective-permute-done | bytes 2359328 | tf_op jit(solution)/shard_map/ppermute | solution.py:1270
  163.6 21.4 %project.3 = (bf16[4096,2048]{1,0:T(8,128)(2,1)}, f32[256,4096]{1,0:T(8,128)}, f32[256,4096]{1,0:T(8,128)}, bf16[256,4096]{1,0:T(8,128)(2,1)}, f32[2,4096]{1,0:T(2,128)}) custom-call(s32[5]{0:T(128)} %compare_select_fusion.12.places, bf16[576,2048]{1,0:T(8,128)(2,1)} %copy-done.4, bf16[576,2048]{1,0:T(8,128)(2,1)} %copy-done.11, ...), custom_call_target="tpu_custom_call" | custom-call | flops 8053063680 | bytes 30670848 | tf_op jit(solution)/shard_map/project/pallas_call | solution.py:818
  185.0 17.2 %collective-permute-done.3.refs_0_.refs_5_ = bf16[576,2048]{1,0:T(8,128)(2,1)S(1)} collective-permute-done((bf16[576,2048]{1,0:T(8,128)(2,1)}, bf16[576,2048]{1,0:T(8,128)(2,1)S(1)}, u32[]{:S(2)}, u32[]{:S(2)}) %collective-permute-start.3) | collective-permute-done | bytes 2359328 | tf_op jit(solution)/shard_map/ppermute | solution.py:1270
  209.4 10.2 project.4
  219.6 10.4 collective-permute-done.14
  237.1 6.0 project.5
  265.2 49.7 %attend_forward.1 = (bf16[4096,256]{1,0:T(8,128)(2,1)}, bf16[4096,256]{1,0:T(8,128)(2,1)}, bf16[4096,256]{1,0:T(8,128)(2,1)}, bf16[256,4096]{1,0:T(8,128)(2,1)}, f32[2,4096]{1,0:T(2,128)}) custom-call(s32[3]{0:T(128)} %bitcast_subtract_fusion.starts, f32[256,4096]{1,0:T(8,128)} %get-tuple-element.182.query_pre, f32[256,4096]{1,0:T(8,128)} %get-tuple-element.183.key_pre, ...), custom_call_target="tpu_custom_call" | custom-call | flops 25769803776 | bytes 20971520 | tf_op jit(solution)/shard_map/attend_forward/pallas_call | solution.py:597
  314.9 6.7 all-to-all-start
  325.6 37.6 %all-to-all-done = bf16[8,512,256]{2,1,0:T(8,128)(2,1)} async-done(((bf16[8,512,256]{2,1,0:T(8,128)(2,1)}), bf16[8,512,256]{2,1,0:T(8,128)(2,1)}, u32[]{:S(2)}, u32[]{:S(2)}) %all-to-all-start) | async-done | bytes 2097184 | tf_op jit(solution)/shard_map/all_to_all | solution.py:1474
  363.3 7.8 multiply_reduce_fusion.2
  382.3 24.4 %experts_forward.5 = (bf16[2,2560,2048]{2,1,0:T(8,128)(2,1)}, bf16[2,2560,1024]{2,1,0:T(8,128)(2,1)}, bf16[2,320,1024]{2,1,0:T(8,128)(2,1)}, bf16[2,320,1024]{2,1,0:T(8,128)(2,1)}, bf16[512,2048]{1,0:T(8,128)(2,1)}) custom-call(s32[1,2,1,512]{3,2,1,0:T(1,128)} %get-tuple-element.194.refs_0_, f32[1,2,1,512]{3,2,1,0:T(1,128)} %get-tuple-element.354.refs_1_, ...), custom_call_target="tpu_custom_call" | custom-call | flops 10737418240 | bytes 33554432 | tf_op jit(solution)/shard_map/experts_forward/pallas_call | solution.py:1221
  412.1 22.6 %experts_backward.5 = (bf16[2,2560,2048]{2,1,0:T(8,128)(2,1)}, bf16[2,2560,1024]{2,1,0:T(8,128)(2,1)}, bf16[2,2560,1024]{2,1,0:T(8,128)(2,1)}, bf16[512,2048]{1,0:T(8,128)(2,1)}) custom-call(s32[1,2,1,512]{3,2,1,0:T(1,128)} %get-tuple-element.194.refs_0_, f32[1,2,1,512]{3,2,1,0:T(1,128)} %get-tuple-element.354.refs_1_, bf16[512,2048]{1,0:T(8,128)(2,1)} %bitcast.155, ...), custom_call_target="tpu_custom_call" | custom-call | tf_op jit(solution)/shard_map/experts_backward/pallas_call | solution.py:1221
  434.8 20.3 %collective-permute-done.22.refs_2_ = bf16[512,2048]{1,0:T(8,128)(2,1)} collective-permute-done((bf16[512,2048]{1,0:T(8,128)(2,1)S(1)}, bf16[512,2048]{1,0:T(8,128)(2,1)}, u32[]{:S(2)}, u32[]{:S(2)}) %collective-permute-start.22) | collective-permute-done | bytes 2097184 | tf_op jit(solution)/shard_map/ppermute | solution.py:1270
  459.9 36.9 %experts_forward.6 = (bf16[2,2560,2048]{2,1,0:T(8,128)(2,1)}, bf16[2,2560,1024]{2,1,0:T(8,128)(2,1)}, bf16[2,640,1024]{2,1,0:T(8,128)(2,1)}, bf16[2,640,1024]{2,...) custom-call(s32[2,2,1,512]{3,2,1,0:T(1,128)} %pad_add_fusion.2.refs_, ...), custom_call_target="tpu_custom_call", output_to_operand_aliasing={{0}: (7, {}), {1}: (8, {})} | custom-call | flops 21474836480 | bytes 41943040 | tf_op jit(solution)/shard_map/experts_forward/pallas_call | solution.py:1221
  496.8 36.1 %experts_backward.6 = (bf16[2,2560,2048]{2,1,0:T(8,128)(2,1)}, bf16[2,2560,1024]{2,1,0:T(8,128)(2,1)}, bf16[2,2560,1024]{2,1,0:T(8,128)(2,1)}, bf16[512,2048]{1,0:T(8,128)(2,1)}, bf16[512,2048]{1,0:T(8,128)(2,1)}) custom-call(s32[2,2,1,512]{3,2,1,0:T(1,128)} %pad_add_fusion.2.refs_0_, ...), custom_call_target="tpu_custom_call", output_to_operand_aliasing={{0}: (9, {}), {1}: (10, {}), {2}: (11, {})} | custom-call | tf_op jit(solution)/shard_map/experts_backward/pallas_call | solution.py:1221
  535.6 13.2 collective-permute-done.24.refs_2_
  548.9 37.4 %experts_forward.7 = (bf16[2,2560,2048]{2,1,0:T(8,128)(2,1)}, bf16[2,2560,1024]{2,1,0:T(8,128)(2,1)}, bf16[2,640,1024]{2,1,0:T(8,128)(2,1)}, bf16[2,640,1024]{2,...) custom-call(s32[2,2,1,512]{3,2,1,0:T(1,128)} %pad_add_fusion.1.refs_, ...), custom_call_target="tpu_custom_call", output_to_operand_aliasing={{0}: (7, {}), {1}: (8, {})} | custom-call | flops 21474836480 | bytes 41943040 | tf_op jit(solution)/shard_map/experts_forward/pallas_call | solution.py:1221
  596.3 36.9 %experts_forward.8 = (bf16[2,2560,2048]{2,1,0:T(8,128)(2,1)}, bf16[2,2560,1024]{2,1,0:T(8,128)(2,1)}, bf16[2,640,1024]{2,1,0:T(8,128)(2,1)}, bf16[2,640,1024]{2,...) custom-call(s32[2,2,1,512]{3,2,1,0:T(1,128)} %pad_add_fusion.refs_0_, ...), custom_call_target="tpu_custom_call", output_to_operand_aliasing={{0}: (7, {}), {1}: (8, {})} | custom-call | flops 21474836480 | bytes 41943040 | tf_op jit(solution)/shard_map/experts_forward/pallas_call | solution.py:1221
  641.0 24.6 %experts_forward.9 = (bf16[2,2560,2048]{2,1,0:T(8,128)(2,1)}, bf16[2,2560,1024]{2,1,0:T(8,128)(2,1)}, bf16[2,320,1024]{2,1,0:T(8,128)(2,1)}, bf16[2,320,1024]{2,1,0:T(8,128)(2,1)}, bf16[512,2048]{1,0:T(8,128)(2,1)}) custom-call(s32[1,2,1,512]{3,2,1,0:T(1,128)} %get-tuple-element.230.refs_0_, ...), custom_call_target="tpu_custom_call", output_to_operand_aliasing={{0}: (6, {}), {1}: (7, {})} | custom-call | flops 10737418240 | bytes 33554432 | tf_op jit(solution)/shard_map/experts_forward/pallas_call | solution.py:1221
  674.0 22.7 %experts_backward.7 = (bf16[2,2560,2048]{2,1,0:T(8,128)(2,1)}, bf16[2,2560,1024]{2,1,0:T(8,128)(2,1)}, bf16[2,2560,1024]{2,1,0:T(8,128)(2,1)}, bf16[512,2048]{1,0:T(8,128)(2,1)}) custom-call(s32[1,2,1,512]{3,2,1,0:T(1,128)} %get-tuple-element.230.refs_0_, ...), custom_call_target="tpu_custom_call", output_to_operand_aliasing={{0}: (8, {}), {1}: (9, {}), {2}: (10, {})} | custom-call | flops 10737418240 | bytes 33554432 | tf_op jit(solution)/shard_map/experts_backward/pallas_call | solution.py:1221
  702.2 35.9 %experts_backward.8 = (bf16[2,2560,2048]{2,1,0:T(8,128)(2,1)}, bf16[2,2560,1024]{2,1,0:T(8,128)(2,1)}, bf16[2,2560,1024]{2,1,0:T(8,128)(2,1)}, bf16[512,2048]{1,0:T(8,128)(2,1)}, bf16[512,2048]{1,0:T(8,128)(2,1)}) custom-call(s32[2,2,1,512]{3,2,1,0:T(1,128)} %pad_add_fusion.refs_0_, ...), custom_call_target="tpu_custom_call", output_to_operand_aliasing={{0}: (9, {}), {1}: (10, {}), {2}: (11, {})} | custom-call | flops 21474836480 | bytes 41943040 | tf_op jit(solution)/shard_map/experts_backward/pallas_call | solution.py:1221
  747.8 35.5 %experts_backward.9 = (bf16[2,2560,2048]{2,1,0:T(8,128)(2,1)}, bf16[2,2560,1024]{2,1,0:T(8,128)(2,1)}, bf16[2,2560,1024]{2,1,0:T(8,128)(2,1)}, bf16[512,2048]{1,0:T(8,128)(2,1)}, bf16[512,2048]{1,0:T(8,128)(2,1)}) custom-call(s32[2,2,1,512]{3,2,1,0:T(1,128)} %pad_add_fusion.1.refs_0_, ...), custom_call_target="tpu_custom_call", output_to_operand_aliasing={{0}: (9, {}), {1}: (10, {}), {2}: (11, {})} | custom-call | flops 21474836480 | bytes 41943040 | tf_op jit(solution)/shard_map/experts_backward/pallas_call | solution.py:1221
  797.3 26.8 %convolution_convert_fusion.3 = bf16[2,2048,1024]{2,1,0:T(8,128)(2,1)} fusion(bf16[2,2560,2048]{2,1,0:T(8,128)(2,1)} %get-tuple-element.264, bf16[2,2560,1024]{2,1,0:T(8,128)(2,1)S(1)} %copy-done.2), kind=kOutput, calls=%fused_computation.4 | convolution fusion | flops 21479030784 | bytes 39845888 | tf_op jit(solution)/shard_map/emd,emf->edf/dot_general | solution.py:1534
  824.1 10.6 collective-permute-done.41
  849.4 26.9 %convolution_convert_fusion.2 = bf16[2,2048,1024]{2,1,0:T(8,128)(2,1)} fusion(bf16[2,2560,2048]{2,1,0:T(8,128)(2,1)} %get-tuple-element.264, bf16[2,2560,1024]{2,1,0:T(8,128)(2,1)S(1)} %bitcast.154), kind=kOutput, calls=%fused_computation.3 | convolution fusion | flops 21479030784 | bytes 39845888 | tf_op jit(solution)/shard_map/emd,emf->edf/dot_general | solution.py:1534
  891.7 5.8 fusion.24
  897.5 8.8 out_grad.1
  906.3 5.8 all-to-all-start.1
  916.7 8.3 convolution_convert_fusion
  925.0 26.8 %all-to-all-done.1 = bf16[8,512,256]{2,1,0:T(8,128)(2,1)} async-done(((bf16[8,512,256]{2,1,0:T(8,128)(2,1)}), bf16[8,512,256]{2,1,0:T(8,128)(2,1)}, u32[]{:S(2)}, u32[]{:S(2)}) %all-to-all-start.1) | async-done | bytes 2097184 | tf_op jit(solution)/shard_map/all_to_all | solution.py:1587
  958.0 45.7 %attend_backward.2 = (f32[256,4096]{1,0:T(8,128)}, f32[256,4096]{1,0:T(8,128)}, bf16[256,4096]{1,0:T(8,128)(2,1)}, f32[256,1]{1,0:T(8,128)}, f32[256,1]{1,0:T(8,128)}, /*index=5*/f32[2,4096]{1,0:T(2,128)}) custom-call(s32[3]{0:T(128)} %bitcast_subtract_fusion.starts, bf16[4096,256]{1,0:T(8,128)(2,1)} %get-tuple-element.270.query, ...), custom_call_target="tpu_custom_call" | custom-call | flops 25769803776 | bytes 20971520 | tf_op jit(solution)/shard_map/attend_backward/pallas_call | solution.py:753
  1013.6 43.7 %attend_backward.3 = (f32[256,4096]{1,0:T(8,128)}, f32[256,4096]{1,0:T(8,128)}, bf16[256,4096]{1,0:T(8,128)(2,1)}, f32[256,1]{1,0:T(8,128)}, f32[256,1]{1,0:T(8,128)}, /*index=5*/f32[2,4096]{1,0:T(2,128)}) custom-call(s32[3]{0:T(128)} %bitcast_subtract_fusion.starts, ...), custom_call_target="tpu_custom_call", output_to_operand_aliasing={{0}: (16, {}), {1}: (17, {}), {2}: (18, {}), {3}: (19, {}),... | custom-call | flops 25769803776 | bytes 20971520 | tf_op jit(solution)/shard_map/attend_backward/pallas_call | solution.py:753
  1074.8 10.1 heads_grad.1
  1092.3 19.8 %heads_product.1 = bf16[8,256,896]{2,1,0:T(8,128)(2,1)} custom-call(bf16[768,4096]{1,0:T(8,128)(2,1)} %heads_grad.1, bf16[4096,2048]{1,0:T(8,128)(2,1)} %get-tuple-element.297.hidden, f32[2048,128]{1,0:T(8,128)} %maximum_maximum_fusion.others), custom_call_target="tpu_custom_call" | custom-call | flops 12884901888 | bytes 23068672 | tf_op jit(solution)/shard_map/heads_product/pallas_call | solution.py:1042
  1118.2 42.3 %collective-permute-done.52 = bf16[512,2048]{1,0:T(8,128)(2,1)S(1)} collective-permute-done((bf16[512,2048]{1,0:T(8,128)(2,1)}, bf16[512,2048]{1,0:T(8,128)(2,1)S(1)}, u32[]{:S(2)}, u32[]{:S(2)}) %collective-permute-start.52) | collective-permute-done | bytes 2097184 | tf_op jit(solution)/shard_map/ppermute | solution.py:1316
  1175.3 29.5 %convolution_convert_fusion.1 = bf16[2,1024,2048]{2,1,0:T(8,128)(2,1)} fusion(bf16[2,2560,1024]{2,1,0:T(8,128)(2,1)} %get-tuple-element.312, bf16[2,2560,2048]{2,1,0:T(8,128)(2,1)} %get-tuple-element.313), kind=kOutput, calls=%fused_computation.2 | convolution fusion | flops 21479030784 | bytes 39845888 | tf_op jit(solution)/shard_map/emd,emf->edf/dot_general | solution.py:1534
  1204.8 11.8 collective-permute-done.55.refs_0_
  1216.7 7.4 collective-permute-done.58.refs_0_
  1224.2 6.0 hidden_term.10
  1231.9 7.2 hidden_term.12
  1239.1 39.5 %collective-permute-done.56.refs_0_ = bf16[576,2048]{1,0:T(8,128)(2,1)S(1)} collective-permute-done((bf16[576,2048]{1,0:T(8,128)(2,1)}, bf16[576,2048]{1,0:T(8,128)(2,1)S(1)}, u32[]{:S(2)}, u32[]{:S(2)}) %collective-permute-start.56) | collective-permute-done | bytes 2359328 | tf_op jit(solution)/shard_map/ppermute | solution.py:1315
  1280.0 6.0 hidden_term.11
  1288.1 6.0 hidden_term.13
  1294.1 5.9 all-to-all-start.2
  1300.1 7.7 add_bitcast_fusion
  1312.8 35.7 %collective-permute-done.57.before = bf16[576,2048]{1,0:T(8,128)(2,1)S(1)} collective-permute-done((bf16[576,2048]{1,0:T(8,128)(2,1)}, bf16[576,2048]{1,0:T(8,128)(2,1)S(1)}, u32[]{:S(2)}, u32[]{:S(2)}) %collective-permute-start.57) | collective-permute-done | bytes 2359328 | tf_op jit(solution)/shard_map/ppermute | solution.py:1315
  1366.8 9.2 input_grad.1
  (410 shorter events, 304.1 us)
Async XLA Ops:
  7.2 145.8 %all-gather.6.cloned.1.call-start = ((), (), s32[]{:S(2)}) async-start(), calls=%async_computation.8 | async-start | bytes 4587520 | tf_op jit(solution)/shard_map/all_gather | solution.py:1423
  43.0 159.6 %all-gather.8.cloned.1.call-start = ((), (), s32[]{:S(2)}) async-start(), calls=%async_computation.9 | async-start | bytes 10485760 | tf_op jit(solution)/shard_map/all_gather | solution.py:1424
  43.7 158.8 %all-gather.10.cloned.1.call-start = ((), (), s32[]{:S(2)}) async-start(), calls=%async_computation.10 | async-start | bytes 10485760 | tf_op jit(solution)/shard_map/all_gather | solution.py:1422
  44.4 318.8 %all-gather.12.cloned.1.call-start = ((), (), s32[]{:S(2)}) async-start(), calls=%async_computation.11 | async-start | bytes 10485760 | tf_op jit(solution)/shard_map/all_gather | solution.py:1461
  44.7 53.2 %collective-permute-start.1 = (bf16[576,2048]{1,0:T(8,128)(2,1)S(1)}, bf16[576,2048]{1,0:T(8,128)(2,1)S(1)}, u32[]{:S(2)}, u32[]{:S(2)}) collective-permute-start(bf16[576,2048]{1,0:T(8,128)(2,1)S(1)} %pad_maximum_fusion.refs_0_), channel_id=1, source_target_pairs={{0,8},{8,16},{16,24},{24,28},{28,20},{20,12},{12,4},{4,0},{1,9},{9... | collective-permute-start | bytes 7077896 | tf_op jit(solution)/shard_map/ppermute | solution.py:1270
  45.8 52.5 %collective-permute-start.4 = (bf16[576,2048]{1,0:T(8,128)(2,1)S(1)}, bf16[576,2048]{1,0:T(8,128)(2,1)S(1)}, u32[]{:S(2)}, u32[]{:S(2)}) collective-permute-start(bf16[576,2048]{1,0:T(8,128)(2,1)S(1)} %pad_maximum_fusion.refs_0_), channel_id=1, source_target_pairs={{8,0},{16,8},{24,16},{28,24},{20,28},{12,20},{4,12},{0,4},{9,1},{1... | collective-permute-start | bytes 7077896 | tf_op jit(solution)/shard_map/ppermute | solution.py:1271
  97.9 52.5 %collective-permute-start.2 = (bf16[576,2048]{1,0:T(8,128)(2,1)S(1)}, bf16[576,2048]{1,0:T(8,128)(2,1)}, u32[]{:S(2)}, u32[]{:S(2)}) collective-permute-start(bf16[576,2048]{1,0:T(8,128)(2,1)S(1)} %collective-permute-done.1.refs_1_.refs_7_), channel_id=1, source_target_pairs={{0,8},{8,16},{16,24},{24,28},{28,20},{20,12},{12,4},{4,0},{1,9},{9... | collective-permute-start | bytes 7077896 | tf_op jit(solution)/shard_map/ppermute | solution.py:1270
  98.2 52.5 %collective-permute-start.5 = (bf16[576,2048]{1,0:T(8,128)(2,1)S(1)}, bf16[576,2048]{1,0:T(8,128)(2,1)}, u32[]{:S(2)}, u32[]{:S(2)}) collective-permute-start(bf16[576,2048]{1,0:T(8,128)(2,1)S(1)} %collective-permute-done.4.refs_2_.refs_1_), channel_id=1, source_target_pairs={{8,0},{16,8},{24,16},{28,24},{20,28},{12,20},{4,12},{0,4},{9,1},{1... | collective-permute-start | bytes 7077896 | tf_op jit(solution)/shard_map/ppermute | solution.py:1271
  150.5 51.7 %collective-permute-start.3 = (bf16[576,2048]{1,0:T(8,128)(2,1)}, bf16[576,2048]{1,0:T(8,128)(2,1)S(1)}, u32[]{:S(2)}, u32[]{:S(2)}) collective-permute-start(bf16[576,2048]{1,0:T(8,128)(2,1)} %collective-permute-done.2.refs_3_.refs_6_), channel_id=1, source_target_pairs={{0,8},{8,16},{16,24},{24,28},{28,20},{20,12},{12,4},{4,0},{1,9},{9... | collective-permute-start | bytes 7077896 | tf_op jit(solution)/shard_map/ppermute | solution.py:1270
  150.8 51.8 %collective-permute-start.6 = (bf16[576,2048]{1,0:T(8,128)(2,1)}, bf16[576,2048]{1,0:T(8,128)(2,1)}, u32[]{:S(2)}, u32[]{:S(2)}) collective-permute-start(bf16[576,2048]{1,0:T(8,128)(2,1)} %collective-permute-done.5.refs_4_.refs_2_), channel_id=1, source_target_pairs={{8,0},{16,8},{24,16},{28,24},{20,28},{12,20},{4,12},{0,4},{9,1},{1... | collective-permute-start | bytes 7077896 | tf_op jit(solution)/shard_map/ppermute | solution.py:1271
  246.8 135.5 %all-gather.14.cloned.1.call-start = ((), (), s32[]{:S(2)}) async-start(), calls=%async_computation.12 | async-start | bytes 10485760 | tf_op jit(solution)/shard_map/all_gather | solution.py:1462
  262.5 52.4 %collective-permute-start.18 = (bf16[512,2048]{1,0:T(8,128)(2,1)S(1)}, bf16[512,2048]{1,0:T(8,128)(2,1)}, u32[]{:S(2)}, u32[]{:S(2)}) collective-permute-start(bf16[512,2048]{1,0:T(8,128)(2,1)S(1)} %bitcast.156), channel_id=1, source_target_pairs={{0,8},{8,16},{16,24},{24,28},{28,20},{20,12},{12,4},{4,0},{1,9},{9... | collective-permute-start | bytes 6291464 | tf_op jit(solution)/shard_map/ppermute | solution.py:1270
  263.0 51.9 %collective-permute-start.19 = (bf16[512,2048]{1,0:T(8,128)(2,1)S(1)}, bf16[512,2048]{1,0:T(8,128)(2,1)}, u32[]{:S(2)}, u32[]{:S(2)}) collective-permute-start(bf16[512,2048]{1,0:T(8,128)(2,1)S(1)} %bitcast.157), channel_id=1, source_target_pairs={{8,0},{16,8},{24,16},{28,24},{20,28},{12,20},{4,12},{0,4},{9,1},{1... | collective-permute-start | bytes 6291464 | tf_op jit(solution)/shard_map/ppermute | solution.py:1271
  314.9 48.3 %all-to-all-start = ((bf16[8,512,256]{2,1,0:T(8,128)(2,1)}), bf16[8,512,256]{2,1,0:T(8,128)(2,1)}, u32[]{:S(2)}, u32[]{:S(2)}) async-start(bf16[8,512,256]{2,1,0:T(8,128)(2,1)} %bitcast.171), calls=%async_computation | async-start | bytes 4194304 | tf_op jit(solution)/shard_map/all_to_all | solution.py:1474
  323.5 88.6 %collective-permute-start.20 = (bf16[512,2048]{1,0:T(8,128)(2,1)}, bf16[512,2048]{1,0:T(8,128)(2,1)}, u32[]{:S(2)}, u32[]{:S(2)}) collective-permute-start(bf16[512,2048]{1,0:T(8,128)(2,1)} %collective-permute-done.18.refs_2_), channel_id=1, source_target_pairs={{0,8},{8,16},{16,24},{24,28},{28,20},{20,12},{12,4},{4,0},{1,9},{9... | collective-permute-start | bytes 6291464 | tf_op jit(solution)/shard_map/ppermute | solution.py:1270
  324.1 88.0 %collective-permute-start.21 = (bf16[512,2048]{1,0:T(8,128)(2,1)}, bf16[512,2048]{1,0:T(8,128)(2,1)}, u32[]{:S(2)}, u32[]{:S(2)}) collective-permute-start(bf16[512,2048]{1,0:T(8,128)(2,1)} %collective-permute-done.19.refs_3_), channel_id=1, source_target_pairs={{8,0},{16,8},{24,16},{28,24},{20,28},{12,20},{4,12},{0,4},{9,1},{1... | collective-permute-start | bytes 6291464 | tf_op jit(solution)/shard_map/ppermute | solution.py:1271
  373.1 81.9 %collective-permute-start.22 = (bf16[512,2048]{1,0:T(8,128)(2,1)S(1)}, bf16[512,2048]{1,0:T(8,128)(2,1)}, u32[]{:S(2)}, u32[]{:S(2)}) collective-permute-start(bf16[512,2048]{1,0:T(8,128)(2,1)S(1)} %multiply_convert_fusion.refs_2_), channel_id=1, source_target_pairs={{0,8},{8,16},{16,24},{24,28},{28,20},{20,12},{12,4},{4,0},{1,9},{9... | collective-permute-start | bytes 6291464 | tf_op jit(solution)/shard_map/ppermute | solution.py:1270
  378.4 76.6 %collective-permute-start.23 = (bf16[512,2048]{1,0:T(8,128)(2,1)S(1)}, bf16[512,2048]{1,0:T(8,128)(2,1)}, u32[]{:S(2)}, u32[]{:S(2)}) collective-permute-start(bf16[512,2048]{1,0:T(8,128)(2,1)S(1)} %multiply_convert_fusion.refs_2_), channel_id=1, source_target_pairs={{8,0},{16,8},{24,16},{28,24},{20,28},{12,20},{4,12},{0,4},{9,1},{1... | collective-permute-start | bytes 6291464 | tf_op jit(solution)/shard_map/ppermute | solution.py:1271
  455.0 77.8 %collective-permute-start.26 = (bf16[512,2048]{1,0:T(8,128)(2,1)}, bf16[512,2048]{1,0:T(8,128)(2,1)}, u32[]{:S(2)}, u32[]{:S(2)}) collective-permute-start(bf16[512,2048]{1,0:T(8,128)(2,1)} %collective-permute-done.22.refs_2_), channel_id=1, source_target_pairs={{0,8},{8,16},{16,24},{24,28},{28,20},{20,12},{12,4},{4,0},{1,9},{9... | collective-permute-start | bytes 6291464 | tf_op jit(solution)/shard_map/ppermute | solution.py:1270
  455.0 77.9 %collective-permute-start.27 = (bf16[512,2048]{1,0:T(8,128)(2,1)}, bf16[512,2048]{1,0:T(8,128)(2,1)}, u32[]{:S(2)}, u32[]{:S(2)}) collective-permute-start(bf16[512,2048]{1,0:T(8,128)(2,1)} %collective-permute-done.23.refs_3_), channel_id=1, source_target_pairs={{8,0},{16,8},{24,16},{28,24},{20,28},{12,20},{4,12},{0,4},{9,1},{1... | collective-permute-start | bytes 6291464 | tf_op jit(solution)/shard_map/ppermute | solution.py:1271
  457.7 91.1 %collective-permute-start.24 = (bf16[512,2048]{1,0:T(8,128)(2,1)}, bf16[512,2048]{1,0:T(8,128)(2,1)S(1)}, u32[]{:S(2)}, u32[]{:S(2)}) collective-permute-start(bf16[512,2048]{1,0:T(8,128)(2,1)} %collective-permute-done.20.refs_2_), channel_id=1, source_target_pairs={{0,8},{8,16},{16,24},{24,28},{28,20},{20,12},{12,4},{4,0},{1,9},{9... | collective-permute-start | bytes 6291464 | tf_op jit(solution)/shard_map/ppermute | solution.py:1270
  457.7 91.2 %collective-permute-start.25 = (bf16[512,2048]{1,0:T(8,128)(2,1)}, bf16[512,2048]{1,0:T(8,128)(2,1)}, u32[]{:S(2)}, u32[]{:S(2)}) collective-permute-start(bf16[512,2048]{1,0:T(8,128)(2,1)} %collective-permute-done.21.refs_3_), channel_id=1, source_target_pairs={{8,0},{16,8},{24,16},{28,24},{20,28},{12,20},{4,12},{0,4},{9,1},{1... | collective-permute-start | bytes 6291464 | tf_op jit(solution)/shard_map/ppermute | solution.py:1271
  532.9 58.6 %collective-permute-start.28 = (bf16[512,2048]{1,0:T(8,128)(2,1)}, bf16[512,2048]{1,0:T(8,128)(2,1)}, u32[]{:S(2)}, u32[]{:S(2)}) collective-permute-start(bf16[512,2048]{1,0:T(8,128)(2,1)} %collective-permute-done.26.refs_2_), channel_id=1, source_target_pairs={{0,8},{8,16},{16,24},{24,28},{28,20},{20,12},{12,4},{4,0},{1,9},{9... | collective-permute-start | bytes 6291464 | tf_op jit(solution)/shard_map/ppermute | solution.py:1270
  533.0 58.6 %collective-permute-start.29 = (bf16[512,2048]{1,0:T(8,128)(2,1)}, bf16[512,2048]{1,0:T(8,128)(2,1)}, u32[]{:S(2)}, u32[]{:S(2)}) collective-permute-start(bf16[512,2048]{1,0:T(8,128)(2,1)} %collective-permute-done.27.refs_3_), channel_id=1, source_target_pairs={{8,0},{16,8},{24,16},{28,24},{20,28},{12,20},{4,12},{0,4},{9,1},{1... | collective-permute-start | bytes 6291464 | tf_op jit(solution)/shard_map/ppermute | solution.py:1271
  592.9 45.0 %collective-permute-start.31 = (bf16[256,2048]{1,0:T(8,128)(2,1)S(1)}, bf16[256,2048]{1,0:T(8,128)(2,1)}, u32[]{:S(2)}, u32[]{:S(2)}) collective-permute-start(bf16[256,2048]{1,0:T(8,128)(2,1)S(1)} %slice.273), channel_id=1, source_target_pairs={{8,0},{16,8},{24,16},{28,24},{20,28},{12,20},{4,12},{0,4},{9,1},{1... | collective-permute-start | bytes 3145736 | tf_op jit(solution)/shard_map/ppermute | solution.py:1277
  742.1 44.7 %collective-permute-start.40 = (bf16[512,2048]{1,0:T(8,128)(2,1)}, bf16[512,2048]{1,0:T(8,128)(2,1)S(1)}, u32[]{:S(2)}, u32[]{:S(2)}) collective-permute-start(bf16[512,2048]{1,0:T(8,128)(2,1)} %pad_maximum_fusion.5), channel_id=1, source_target_pairs={{0,8},{8,16},{16,24},{24,28},{28,20},{20,12},{12,4},{4,0},{1,9},{9... | collective-permute-start | bytes 6291464 | tf_op jit(solution)/shard_map/ppermute | solution.py:1316
  746.1 45.0 %collective-permute-start.37 = (bf16[512,2048]{1,0:T(8,128)(2,1)}, bf16[512,2048]{1,0:T(8,128)(2,1)}, u32[]{:S(2)}, u32[]{:S(2)}) collective-permute-start(bf16[512,2048]{1,0:T(8,128)(2,1)} %pad_maximum_fusion.4), channel_id=1, source_target_pairs={{8,0},{16,8},{24,16},{28,24},{20,28},{12,20},{4,12},{0,4},{9,1},{1... | collective-permute-start | bytes 6291464 | tf_op jit(solution)/shard_map/ppermute | solution.py:1315
  790.8 44.0 %collective-permute-start.41 = (bf16[512,2048]{1,0:T(8,128)(2,1)}, bf16[512,2048]{1,0:T(8,128)(2,1)}, u32[]{:S(2)}, u32[]{:S(2)}) collective-permute-start(bf16[512,2048]{1,0:T(8,128)(2,1)} %add_convert_fusion.6), channel_id=1, source_target_pairs={{0,8},{8,16},{16,24},{24,28},{28,20},{20,12},{12,4},{4,0},{1,9},{9... | collective-permute-start | bytes 6291464 | tf_op jit(solution)/shard_map/ppermute | solution.py:1316
  795.6 44.0 %collective-permute-start.39 = (bf16[512,2048]{1,0:T(8,128)(2,1)}, bf16[512,2048]{1,0:T(8,128)(2,1)}, u32[]{:S(2)}, u32[]{:S(2)}) collective-permute-start(bf16[512,2048]{1,0:T(8,128)(2,1)} %add_convert_fusion.7), channel_id=1, source_target_pairs={{8,0},{16,8},{24,16},{28,24},{20,28},{12,20},{4,12},{0,4},{9,1},{1... | collective-permute-start | bytes 6291464 | tf_op jit(solution)/shard_map/ppermute | solution.py:1315
  906.3 45.5 %all-to-all-start.1 = ((bf16[8,512,256]{2,1,0:T(8,128)(2,1)}), bf16[8,512,256]{2,1,0:T(8,128)(2,1)}, u32[]{:S(2)}, u32[]{:S(2)}) async-start(bf16[8,512,256]{2,1,0:T(8,128)(2,1)} %out_grad.1), calls=%async_computation.1 | async-start | bytes 4194304 | tf_op jit(solution)/shard_map/all_to_all | solution.py:1587
  912.1 172.7 %reduce-scatter.6.cloned.1.call-start = ((), (), s32[]{:S(2)}) async-start(), calls=%async_computation.13 | async-start | bytes 10485760 | tf_op jit(solution)/shard_map/reduce_scatter | solution.py:1572
  951.8 272.3 %reduce-scatter.12.cloned.1.call-start = ((), (), s32[]{:S(2)}) async-start(), calls=%async_computation.16 | async-start | bytes 10485760 | tf_op jit(solution)/shard_map/reduce_scatter | solution.py:1572
  952.6 286.6 %reduce-scatter.10.cloned.1.call-start = ((), (), s32[]{:S(2)}) async-start(), calls=%async_computation.15 | async-start | bytes 10485760 | tf_op jit(solution)/shard_map/reduce_scatter | solution.py:1572
  953.3 340.8 %reduce-scatter.8.cloned.1.call-start = ((), (), s32[]{:S(2)}) async-start(), calls=%async_computation.14 | async-start | bytes 4587520 | tf_op jit(solution)/shard_map/reduce_scatter | solution.py:1572
  954.5 49.3 %collective-permute-start.44 = (bf16[512,2048]{1,0:T(8,128)(2,1)}, bf16[512,2048]{1,0:T(8,128)(2,1)}, u32[]{:S(2)}, u32[]{:S(2)}) collective-permute-start(bf16[512,2048]{1,0:T(8,128)(2,1)} %pad_maximum_fusion.6), channel_id=1, source_target_pairs={{8,0},{16,8},{24,16},{28,24},{20,28},{12,20},{4,12},{0,4},{9,1},{1... | collective-permute-start | bytes 6291464 | tf_op jit(solution)/shard_map/ppermute | solution.py:1315
  956.0 51.6 %collective-permute-start.45 = (bf16[512,2048]{1,0:T(8,128)(2,1)}, bf16[512,2048]{1,0:T(8,128)(2,1)}, u32[]{:S(2)}, u32[]{:S(2)}) collective-permute-start(bf16[512,2048]{1,0:T(8,128)(2,1)} %pad_maximum_fusion.7), channel_id=1, source_target_pairs={{0,8},{8,16},{16,24},{24,28},{28,20},{20,12},{12,4},{4,0},{1,9},{9... | collective-permute-start | bytes 6291464 | tf_op jit(solution)/shard_map/ppermute | solution.py:1316
  1011.3 47.9 %collective-permute-start.46 = (bf16[512,2048]{1,0:T(8,128)(2,1)}, bf16[512,2048]{1,0:T(8,128)(2,1)}, u32[]{:S(2)}, u32[]{:S(2)}) collective-permute-start(bf16[512,2048]{1,0:T(8,128)(2,1)} %add_convert_fusion.3), channel_id=1, source_target_pairs={{8,0},{16,8},{24,16},{28,24},{20,28},{12,20},{4,12},{0,4},{9,1},{1... | collective-permute-start | bytes 6291464 | tf_op jit(solution)/shard_map/ppermute | solution.py:1315
  1011.4 47.8 %collective-permute-start.47 = (bf16[512,2048]{1,0:T(8,128)(2,1)}, bf16[512,2048]{1,0:T(8,128)(2,1)S(1)}, u32[]{:S(2)}, u32[]{:S(2)}) collective-permute-start(bf16[512,2048]{1,0:T(8,128)(2,1)} %add_convert_fusion.2), channel_id=1, source_target_pairs={{0,8},{8,16},{16,24},{24,28},{28,20},{20,12},{12,4},{4,0},{1,9},{9... | collective-permute-start | bytes 6291464 | tf_op jit(solution)/shard_map/ppermute | solution.py:1316
  1116.1 261.1 %reduce-scatter.14.cloned.1.call-start = ((), (), s32[]{:S(2)}) async-start(), calls=%async_computation.17 | async-start | bytes 10485760 | tf_op jit(solution)/shard_map/reduce_scatter | solution.py:1572
  1116.2 44.4 %collective-permute-start.52 = (bf16[512,2048]{1,0:T(8,128)(2,1)}, bf16[512,2048]{1,0:T(8,128)(2,1)S(1)}, u32[]{:S(2)}, u32[]{:S(2)}) collective-permute-start(bf16[512,2048]{1,0:T(8,128)(2,1)} %add_convert_fusion), channel_id=1, source_target_pairs={{0,8},{8,16},{16,24},{24,28},{28,20},{20,12},{12,4},{4,0},{1,9},{9... | collective-permute-start | bytes 6291464 | tf_op jit(solution)/shard_map/ppermute | solution.py:1316
  1116.5 44.0 %collective-permute-start.51 = (bf16[512,2048]{1,0:T(8,128)(2,1)}, bf16[512,2048]{1,0:T(8,128)(2,1)}, u32[]{:S(2)}, u32[]{:S(2)}) collective-permute-start(bf16[512,2048]{1,0:T(8,128)(2,1)} %add_convert_fusion.1), channel_id=1, source_target_pairs={{8,0},{16,8},{24,16},{28,24},{20,28},{12,20},{4,12},{0,4},{9,1},{1... | collective-permute-start | bytes 6291464 | tf_op jit(solution)/shard_map/ppermute | solution.py:1315
  1167.6 49.1 %collective-permute-start.55 = (bf16[576,2048]{1,0:T(8,128)(2,1)}, bf16[576,2048]{1,0:T(8,128)(2,1)S(1)}, u32[]{:S(2)}, u32[]{:S(2)}) collective-permute-start(bf16[576,2048]{1,0:T(8,128)(2,1)} %hidden_term.8), channel_id=1, source_target_pairs={{8,0},{16,8},{24,16},{28,24},{20,28},{12,20},{4,12},{0,4},{9,1},{1... | collective-permute-start | bytes 7077896 | tf_op jit(solution)/shard_map/ppermute | solution.py:1315
  1174.5 49.5 %collective-permute-start.58 = (bf16[576,2048]{1,0:T(8,128)(2,1)}, bf16[576,2048]{1,0:T(8,128)(2,1)}, u32[]{:S(2)}, u32[]{:S(2)}) collective-permute-start(bf16[576,2048]{1,0:T(8,128)(2,1)} %hidden_term.9), channel_id=1, source_target_pairs={{0,8},{8,16},{16,24},{24,28},{28,20},{20,12},{12,4},{4,0},{1,9},{9... | collective-permute-start | bytes 7077896 | tf_op jit(solution)/shard_map/ppermute | solution.py:1316
  1230.1 48.5 %collective-permute-start.56 = (bf16[576,2048]{1,0:T(8,128)(2,1)}, bf16[576,2048]{1,0:T(8,128)(2,1)S(1)}, u32[]{:S(2)}, u32[]{:S(2)}) collective-permute-start(bf16[576,2048]{1,0:T(8,128)(2,1)} %hidden_term.10), channel_id=1, source_target_pairs={{8,0},{16,8},{24,16},{28,24},{20,28},{12,20},{4,12},{0,4},{9,1},{1... | collective-permute-start | bytes 7077896 | tf_op jit(solution)/shard_map/ppermute | solution.py:1315
  1239.1 49.0 %collective-permute-start.59 = (bf16[576,2048]{1,0:T(8,128)(2,1)}, bf16[576,2048]{1,0:T(8,128)(2,1)}, u32[]{:S(2)}, u32[]{:S(2)}) collective-permute-start(bf16[576,2048]{1,0:T(8,128)(2,1)} %hidden_term.12), channel_id=1, source_target_pairs={{0,8},{8,16},{16,24},{24,28},{28,20},{20,12},{12,4},{4,0},{1,9},{9... | collective-permute-start | bytes 7077896 | tf_op jit(solution)/shard_map/ppermute | solution.py:1316
  1286.0 62.5 %collective-permute-start.57 = (bf16[576,2048]{1,0:T(8,128)(2,1)}, bf16[576,2048]{1,0:T(8,128)(2,1)S(1)}, u32[]{:S(2)}, u32[]{:S(2)}) collective-permute-start(bf16[576,2048]{1,0:T(8,128)(2,1)} %hidden_term.11), channel_id=1, source_target_pairs={{8,0},{16,8},{24,16},{28,24},{20,28},{12,20},{4,12},{0,4},{9,1},{1... | collective-permute-start | bytes 7077896 | tf_op jit(solution)/shard_map/ppermute | solution.py:1315
  1294.1 60.1 %collective-permute-start.60 = (bf16[576,2048]{1,0:T(8,128)(2,1)}, bf16[576,2048]{1,0:T(8,128)(2,1)}, u32[]{:S(2)}, u32[]{:S(2)}) collective-permute-start(bf16[576,2048]{1,0:T(8,128)(2,1)} %hidden_term.13), channel_id=1, source_target_pairs={{0,8},{8,16},{16,24},{24,28},{28,20},{20,12},{12,4},{4,0},{1,9},{9... | collective-permute-start | bytes 7077896 | tf_op jit(solution)/shard_map/ppermute | solution.py:1316
  1294.1 64.9 %all-to-all-start.2 = ((bf16[8,64,896]{2,1,0:T(8,128)(2,1)}), bf16[8,64,896]{2,1,0:T(8,128)(2,1)S(1)}, u32[]{:S(2)}, u32[]{:S(2)}) async-start(bf16[8,64,896]{2,1,0:T(8,128)(2,1)} %reduce-scatter.8.cloned.1.call-done), calls=%async_computation.4 | async-start | bytes 1835008 | tf_op jit(solution)/shard_map/all_to_all | solution.py:1659
  (93 other events, 1739.8 us)
Sparse Core Ops, SparseCore 0:
  43.1 31.5 all-gather.5
  76.3 58.2 all-gather.7
  136.1 58.2 all-gather.9
  246.9 57.9 all-gather.11
  306.3 58.2 all-gather.13
  951.9 72.6 reduce-scatter.5
  1027.4 71.6 reduce-scatter.11
  1101.7 71.7 reduce-scatter.9
  1176.8 41.2 reduce-scatter.7
  1224.2 71.3 reduce-scatter.13

commit v5 on v4

--- a/solution.py
+++ b/solution.py
@@ -972,6 +972,53 @@
     )(place, heads_grad, w_t, before, past, tokens, gain, mixed_grad)
 
 
+def mixed_grad_kernel(own, before, past, mixed, cotangent, gain, mixed_grad, branch, gain_grad):
+    second_grad = (
+        own[...].astype(jnp.float32)
+        + before[...].astype(jnp.float32)
+        + past[...].astype(jnp.float32)
+    )
+    values = mixed[...]
+    inverse = lax.rsqrt(jnp.mean(values * values, axis=-1, keepdims=True) + EPSILON)
+    normed = values * inverse
+    scaled = second_grad * gain[...]
+    along = jnp.mean(scaled * normed, axis=-1, keepdims=True)
+    made = cotangent[...].astype(jnp.float32) + inverse * (scaled - normed * along)
+    mixed_grad[...] = made
+    branch[...] = made.astype(jnp.bfloat16)
+    part = jnp.sum(second_grad * normed, axis=0, keepdims=True)
+
+    @pl.when(pl.program_id(0) == 0)
+    def _():
+        gain_grad[...] = part
+
+    @pl.when(pl.program_id(0) > 0)
+    def _():
+        gain_grad[...] += part
+
+
+def mixed_grad_of(own, before, past, mixed, cotangent, gain):
+    rows, width = mixed.shape
+    block = pl.BlockSpec((rows // 4, width), lambda i: (i, 0))
+    line = pl.BlockSpec((1, width), lambda i: (0, 0))
+    return pl.pallas_call(
+        mixed_grad_kernel,
+        grid=(4,),
+        in_specs=[block] * 5 + [line],
+        out_specs=[block, block, line],
+        out_shape=[
+            jax.ShapeDtypeStruct((rows, width), jnp.float32),
+            jax.ShapeDtypeStruct((rows, width), jnp.bfloat16),
+            jax.ShapeDtypeStruct((1, width), jnp.float32),
+        ],
+        compiler_params=pltpu.CompilerParams(vmem_limit_bytes=VMEM_BYTES),
+        cost_estimate=pl.CostEstimate(
+            flops=16 * rows * width, bytes_accessed=18 * rows * width, transcendentals=rows
+        ),
+        name="mixed_grad",
+    )(own, before, past, mixed, cotangent, gain)
+
+
 def out_grad_kernel(branch, w_out, out):
     made = dot_nt(branch[...], w_out[...]).astype(jnp.bfloat16)
     columns = out.shape[2]
@@ -1088,14 +1135,28 @@
     return jnp.sum(jnp.where(match, gate_row, 0.0), axis=1, keepdims=True)
 
 
-def experts_forward_kernel(*refs, count, slots, aliased, tiles):
+def take_rows(match, pieces):
+    first, made = 0, 0.0
+    for piece in pieces:
+        last = first + piece.shape[0]
+        made = made + dot_nn(match[:, first:last], piece[...])
+        first = last
+    return made
+
+
+def pieces_of(refs, count):
+    size = len(refs) // count
+    return [refs[b * size : (b + 1) * size] for b in range(count)]
+
+
+def experts_forward_kernel(*refs, count, pieces, slots, aliased, tiles):
     ranks, gates = refs[:2]
-    blocks = refs[2 : 2 + count]
-    w_gate, w_up, w_down = refs[2 + count : 5 + count]
-    refs = refs[5 + count + aliased :]
+    blocks = pieces_of(refs[2 : 2 + pieces], count)
+    w_gate, w_up, w_down = refs[2 + pieces : 5 + pieces]
+    refs = refs[5 + pieces + aliased :]
     taken, active, gate_slope, up_slope = refs[:4]
-    outs = refs[4 : 4 + count]
-    made, weights = refs[4 + count :]
+    outs = pieces_of(refs[4 : 4 + pieces], count)
+    made, weights = refs[4 + pieces :]
     e, f = pl.program_id(0), pl.program_id(1)
     tile, wide_tile = w_gate.shape[2], w_down.shape[2]
 
@@ -1105,7 +1166,7 @@
             here = slice(b * slots, (b + 1) * slots)
             match = slot_match(ranks[b, e], slots)
             weights[here, :] = slot_gates(match, gates[b, e])
-            taken[0, here, :] = dot_nn(match.astype(jnp.bfloat16), blocks[b][...]).astype(
+            taken[0, here, :] = take_rows(match.astype(jnp.bfloat16), blocks[b]).astype(
                 jnp.bfloat16
             )
 
@@ -1140,17 +1201,21 @@
             match = slot_match(ranks[b, k], slots).astype(jnp.float32).astype(jnp.bfloat16)
             term = dot_tn(match, made[k, b * slots : (b + 1) * slots, :])
             summed = term if summed is None else summed + term
-        outs[b][...] = summed.astype(jnp.bfloat16)
-
-
-def experts_backward_kernel(*refs, count, slots, aliased, tiles):
+        first = 0
+        for out in outs[b]:
+            last = first + out.shape[0]
+            out[...] = summed[first:last].astype(jnp.bfloat16)
+            first = last
+
+
+def experts_backward_kernel(*refs, count, pieces, slots, aliased, tiles):
     ranks, gates = refs[:2]
-    blocks = refs[2 : 2 + count]
-    w_gate, w_up, w_down, gate_slope, up_slope = refs[2 + count : 7 + count]
-    refs = refs[7 + count + aliased :]
+    blocks = pieces_of(refs[2 : 2 + pieces], count)
+    w_gate, w_up, w_down, gate_slope, up_slope = refs[2 + pieces : 7 + pieces]
+    refs = refs[7 + pieces + aliased :]
     taken, gate_grad, up_grad = refs[:3]
-    outs = refs[3 : 3 + count]
-    (made,) = refs[3 + count :]
+    outs = pieces_of(refs[3 : 3 + pieces], count)
+    (made,) = refs[3 + pieces :]
     e, f = pl.program_id(0), pl.program_id(1)
     tile, wide_tile = w_down.shape[1], w_gate.shape[1]
 
@@ -1160,7 +1225,7 @@
             match = slot_match(ranks[b, e], slots)
             weight = slot_gates(match, gates[b, e])
             taken[0, b * slots : (b + 1) * slots, :] = (
-                dot_nn(match.astype(jnp.bfloat16), blocks[b][...]) * weight
+                take_rows(match.astype(jnp.bfloat16), blocks[b]) * weight
             ).astype(jnp.bfloat16)
 
     @pl.when(f < tiles)
@@ -1185,8 +1250,8 @@
 def experts_stage(
     forward, ranks, gates, blocks, weights, slopes, held, place, slots, all_slots, light=False
 ):
-    count = len(blocks)
-    rows, width = blocks[0].shape
+    count, pieces = ranks.shape[0], len(blocks)
+    rows, width = ranks.shape[3], blocks[0].shape[1]
     experts, _, hidden_units = weights[0].shape
     tile, wide_tile = min(512, hidden_units), min(1024, width)
     tiles, wide_tiles = hidden_units // tile, width // wide_tile
@@ -1199,7 +1264,7 @@
         return jnp.maximum(f - tiles, 0)
 
     info = pl.BlockSpec((count, experts, 1, rows), lambda e, f: (0, 0, 0, 0))
-    block = pl.BlockSpec((rows, width), lambda e, f: (0, 0))
+    block = pl.BlockSpec(blocks[0].shape, lambda e, f: (0, 0))
     wide = pl.BlockSpec((1, part, width), lambda e, f: (e, place, 0))
     narrow = pl.BlockSpec((1, part, hidden_units), lambda e, f: (e, place, 0))
     slope = pl.BlockSpec((1, part, tile), lambda e, f: (e, 0, first(f)))
@@ -1215,22 +1280,24 @@
         back = pl.BlockSpec((1, tile, width), lambda e, f: (e, first(f), 0))
         narrow_outs, own_outs, scratch = 2, 0, []
     held = () if held is None else tuple(held)
-    before = 2 + count + 3 + len(slopes)
+    before = 2 + pieces + 3 + len(slopes)
     scale = 0 if light else 1
     flops = 2 * experts * part * width * (3 * hidden_units + 2 * rows)
     return pl.pallas_call(
-        partial(kernel, count=count, slots=slots, aliased=len(held), tiles=tiles),
+        partial(
+            kernel, count=count, pieces=pieces, slots=slots, aliased=len(held), tiles=tiles
+        ),
         grid=(experts, tiles + wide_tiles),
         in_specs=[info, info]
-        + [block] * count
+        + [block] * pieces
         + [into, into, back]
         + [slope] * len(slopes)
         + [pl.BlockSpec(memory_space=pl.ANY)] * len(held),
-        out_specs=[wide] + [narrow] * narrow_outs + [own] * own_outs + [block] * count,
+        out_specs=[wide] + [narrow] * narrow_outs + [own] * own_outs + [block] * pieces,
         out_shape=[jax.ShapeDtypeStruct((experts, all_slots, width), jnp.bfloat16)]
         + [jax.ShapeDtypeStruct((experts, all_slots, hidden_units), jnp.bfloat16)] * narrow_outs
         + [jax.ShapeDtypeStruct((experts, part, hidden_units), jnp.bfloat16)] * own_outs
-        + [jax.ShapeDtypeStruct((rows, width), jnp.bfloat16)] * count,
+        + [jax.ShapeDtypeStruct(blocks[0].shape, jnp.bfloat16)] * pieces,
         scratch_shapes=[pltpu.VMEM((experts, part, width), jnp.bfloat16)] + scratch,
         input_output_aliases={before + k: k for k in range(len(held))},
         compiler_params=pltpu.CompilerParams(vmem_limit_bytes=VMEM_BYTES),
@@ -1275,7 +1342,7 @@
         cut = before.shape[0] // 2
         first = lax.ppermute(before[:cut], "ctx", self.up)
         second = lax.ppermute(past[cut:], "ctx", self.down)
-        self.blocks[self.half] = jnp.concatenate([first, second], axis=0)
+        self.blocks[self.half] = (first, second)
         return (self.half,)
 
 
@@ -1291,9 +1358,9 @@
 
     def prepare(self, terms, *earlier):
         if self.step == self.half:
-            far = after(terms[self.half], *earlier)
-            cut = far.shape[0] // 2
-            before, past = far[:cut], far[cut:]
+            before, past = terms[self.half]
+            if earlier:
+                before, past = lax.optimization_barrier((before, past) + earlier)[:2]
         else:
             before, past = terms[-self.step], terms[self.step]
             got_before, got_past = self.to_before, self.to_after
@@ -1452,7 +1519,8 @@
     made = project_all([0] + others[: 2 * (half - 2)], None)
     token_ring.advance(made[-1], up_all, gate_all)
     made = project_all(others[2 * (half - 2) : -1], made)
-    token_ring.blocks[half] = after(token_ring.blocks[half], made[-1])
+    far_tokens = jnp.concatenate(token_ring.blocks[half], axis=0)
+    token_ring.blocks[half] = after(far_tokens, made[-1])
     made = project_all(others[-1:], made)
     hidden_all, query_pre, key_pre, value_t, squares = made
     w_out_rows = place_rows(
@@ -1496,23 +1564,31 @@
     result_terms, second_terms, slopes = {}, {}, {}
     kept = kept_grads = None
 
+    def blocks_of(ring_of_blocks, step):
+        if step == half:
+            return list(ring_of_blocks.blocks[half])
+        return [ring_of_blocks.blocks[k] for k in stages[step]]
+
+    def terms_of(step, terms):
+        return {half: tuple(terms)} if step == half else dict(zip(stages[step], terms))
+
     def forward(step, *earlier):
         nonlocal kept
         ranks, stage_gates, at = infos[step]
         ranks = after(ranks, *earlier) if earlier else ranks
-        blocks = [second_ring.blocks[k] for k in stages[step]]
+        blocks = blocks_of(second_ring, step)
         made = experts_stage(
             True, ranks, stage_gates, blocks, weights, (), kept, at, slots, all_slots
         )
         kept, slopes[step], terms = made[:2], made[2:4], made[4:]
-        result_terms.update(zip(stages[step], terms))
+        result_terms.update(terms_of(step, terms))
         return terms[0]
 
     def backward(step, *earlier, light=False):
         nonlocal kept_grads
         ranks, stage_gates, at = infos[step]
         ranks = after(ranks, *earlier) if earlier else ranks
-        blocks = [grad_ring.blocks[k] for k in stages[step]]
+        blocks = blocks_of(grad_ring, step)
         made = experts_stage(
             False,
             ranks,
@@ -1527,7 +1603,7 @@
             light,
         )
         kept_grads, terms = made[:3], made[3:]
-        second_terms.update(zip(stages[step], terms))
+        second_terms.update(terms_of(step, terms))
         return terms[0]
 
     def weight_grad(left, right):
@@ -1566,20 +1642,20 @@
     sent = second_sum.advance(second_terms, gate_product)
     result_sum.prepare(result_terms, *sent)
     up_product = weight_grad(after(rows_taken, *result_sum.payload), up_grad)
-    second_grad = second_sum.finish(after(second_terms[0], up_product))
+    mixed_grad, branch, ffn_gain_grad = mixed_grad_of(
+        second_terms[0],
+        second_sum.to_before,
+        second_sum.to_after,
+        mixed,
+        cotangent[0],
+        after(gain_ffn[None], up_product),
+    )
+    ffn_gain_grad = ffn_gain_grad[0]
 
     def fsdp_sum_low(product):
         return lax.psum_scatter(product, "fsdp", scatter_dimension=1, tiled=True)
 
 
-    upstream = cotangent[0].astype(jnp.float32)
-    mixed_normed = mixed * mixed_inv
-    ffn_gain_grad = jnp.sum(second_grad * mixed_normed, axis=0)
-    scaled = second_grad * gain_ffn
-    mixed_grad = upstream + mixed_inv * (
-        scaled - mixed_normed * jnp.mean(scaled * mixed_normed, axis=-1, keepdims=True)
-    )
-    branch = mixed_grad.astype(jnp.bfloat16)
     out_grad = out_grad_of(branch, out_all, contexts)
     w_out_grad = lax.dot_general(
         own_attended, after(branch, out_grad), (((0,), (0,)), ((), ())), preferred_element_type=jnp.float32

time: 1390 us -> 1380 us (level)
  other arithmetic: 99.6 us -> 82.7 us
    pallas_call x10 -> x11, Pallas kernels: 313 us -> 321 us  [the longest x10 312 us: experts_stage(): pl.pallas_call(partial(kernel, count=count, pieces=pieces, slots=slots, a...]
  transfers between devices with their start and end apart: 74 -> 74, of which waited for: 36 -> 37; matrix products, arithmetic and copies ran while one was open for 16% -> 15% of each run, Pallas kernels for 41% -> 41%
where the time goes in v5:
time: 1380 us; the launch traced here: 1370 us
  Pallas kernels  592 us (43%)
  waiting for transfers between devices  432 us (31%)
  matrix products  101 us (7%)
  starting transfers between devices  95.4 us (7%)
  other arithmetic  82.7 us (6%)
  local copies, waits for them, and re-layouts  55.8 us (4%)
  between operations  15.8 us (1%)
    pallas_call x10, Pallas kernels, experts_stage(): pl.pallas_call(partial(kernel, count=count, pieces=pieces, slots=slots, a...  312 us
    ppermute x9, waiting for transfers between devices, advance(): self.from_before = lax.ppermute(before, 'ctx', self.up)  163 us
    ppermute x12, waiting for transfers between devices, send(): self.to_before = lax.ppermute(before, 'ctx', self.down)  104 us
    pallas_call x2, Pallas kernels, attend_backward(): pl.pallas_call(partial(attend_backward_kernel, size=size, prompt_rows=pro...  89.6 us
    dot_general x3, matrix products, weight_grad(): jnp.einsum('emd,emf->edf', left, right, preferred_element_type=jnp.float32)  82.5 us
    ppermute x12, waiting for transfers between devices, send(): self.to_after = lax.ppermute(past, 'ctx', self.up)  63.4 us
    pallas_call x1, Pallas kernels, attend_forward(): pl.pallas_call(partial(attend_forward_kernel, size=size, prompt_rows=prom...  49.7 us
    pallas_call x7, Pallas kernels, hidden_term(): pl.pallas_call(partial(hidden_term_kernel, start=start, halves=halves), g...  41.4 us
  transfers between devices with their start and end apart: 74, of which 37 were waited for; matrix products, arithmetic and copies ran while one was open for 15% of the time, Pallas kernels for 41%

profile of v5, /device:TPU:14, one launch (start us, length us, event | category | flops | bytes accessed | tf_op | source)
XLA Modules:
  0.0 1374.8 jit_solution(1433255638773359164)
XLA Ops:
  46.8 51.1 %collective-permute-done.1.refs_1_.refs_7_ = bf16[576,2048]{1,0:T(8,128)(2,1)S(1)} collective-permute-done((bf16[576,2048]{1,0:T(8,128)(2,1)S(1)}, bf16[576,2048]{1,0:T(8,128)(2,1)S(1)}, u32[]{:S(2)}, u32[]{:S(2)}) %collective-permute-start.1) | collective-permute-done | bytes 2359328 | tf_op jit(solution)/shard_map/ppermute | solution.py:1337
  100.0 50.5 %collective-permute-done.2.refs_3_.refs_6_ = bf16[576,2048]{1,0:T(8,128)(2,1)} collective-permute-done((bf16[576,2048]{1,0:T(8,128)(2,1)S(1)}, bf16[576,2048]{1,0:T(8,128)(2,1)}, u32[]{:S(2)}, u32[]{:S(2)}) %collective-permute-start.2) | collective-permute-done | bytes 2359328 | tf_op jit(solution)/shard_map/ppermute | solution.py:1337
  163.5 21.4 %project.3 = (bf16[4096,2048]{1,0:T(8,128)(2,1)}, f32[256,4096]{1,0:T(8,128)}, f32[256,4096]{1,0:T(8,128)}, bf16[256,4096]{1,0:T(8,128)(2,1)}, f32[2,4096]{1,0:T(2,128)}) custom-call(s32[5]{0:T(128)} %compare_select_fusion.12.places, bf16[576,2048]{1,0:T(8,128)(2,1)} %copy-done.3, bf16[576,2048]{1,0:T(8,128)(2,1)} %copy-done.8, bf16[576,2048]{1,0:T(8,128)(2,1)} %copy-done.9, ...), custom_call_target="tpu_custom_call" | custom-call | flops 8053063680 | bytes 30670848 | tf_op jit(solution)/shard_map/project/pallas_call | solution.py:818
  184.9 17.2 %collective-permute-done.3.refs_0_.refs_5_ = bf16[576,2048]{1,0:T(8,128)(2,1)S(1)} collective-permute-done((bf16[576,2048]{1,0:T(8,128)(2,1)}, bf16[576,2048]{1,0:T(8,128)(2,1)S(1)}, u32[]{:S(2)}, u32[]{:S(2)}) %collective-permute-start.3) | collective-permute-done | bytes 2359328 | tf_op jit(solution)/shard_map/ppermute | solution.py:1337
  209.4 10.3 project.4
  219.6 10.4 collective-permute-done.14
  237.1 6.0 project.5
  265.2 49.7 %attend_forward.1 = (bf16[4096,256]{1,0:T(8,128)(2,1)}, bf16[4096,256]{1,0:T(8,128)(2,1)}, bf16[4096,256]{1,0:T(8,128)(2,1)}, bf16[256,4096]{1,0:T(8,128)(2,1)}, f32[2,4096]{1,0:T(2,128)}) custom-call(s32[3]{0:T(128)} %bitcast_subtract_fusion.starts, f32[256,4096]{1,0:T(8,128)} %get-tuple-element.188.query_pre, f32[256,4096]{1,0:T(8,128)} %get-tuple-element.189.key_pre, ...), custom_call_target="tpu_custom_call" | custom-call | flops 25769803776 | bytes 20971520 | tf_op jit(solution)/shard_map/attend_forward/pallas_call | solution.py:597
  315.0 6.6 all-to-all-start
  325.6 37.6 %all-to-all-done = bf16[8,512,256]{2,1,0:T(8,128)(2,1)} async-done(((bf16[8,512,256]{2,1,0:T(8,128)(2,1)}), bf16[8,512,256]{2,1,0:T(8,128)(2,1)}, u32[]{:S(2)}, u32[]{:S(2)}) %all-to-all-start) | async-done | bytes 2097184 | tf_op jit(solution)/shard_map/all_to_all | solution.py:1542
  363.2 7.8 multiply_reduce_fusion
  382.3 24.4 %experts_forward.5 = (bf16[2,2560,2048]{2,1,0:T(8,128)(2,1)}, bf16[2,2560,1024]{2,1,0:T(8,128)(2,1)}, bf16[2,320,1024]{2,1,0:T(8,128)(2,1)}, bf16[2,320,1024]{2,1,0:T(8,128)(2,1)}, bf16[512,2048]{1,0:T(8,128)(2,1)}) custom-call(s32[1,2,1,512]{3,2,1,0:T(1,128)} %get-tuple-element.200.refs_0_, f32[1,2,1,512]{3,2,1,0:T(1,128)} %get-tuple-element.358.refs_1_, ...), custom_call_target="tpu_custom_call" | custom-call | flops 10737418240 | bytes 33554432 | tf_op jit(solution)/shard_map/experts_forward/pallas_call | solution.py:1286
  412.1 22.7 %experts_backward.5 = (bf16[2,2560,2048]{2,1,0:T(8,128)(2,1)}, bf16[2,2560,1024]{2,1,0:T(8,128)(2,1)}, bf16[2,2560,1024]{2,1,0:T(8,128)(2,1)}, bf16[512,2048]{1,0:T(8,128)(2,1)}) custom-call(s32[1,2,1,512]{3,2,1,0:T(1,128)} %get-tuple-element.200.refs_0_, f32[1,2,1,512]{3,2,1,0:T(1,128)} %get-tuple-element.358.refs_1_, bf16[512,2048]{1,0:T(8,128)(2,1)} %bitcast.156, ...), custom_call_target="tpu_custom_call" | custom-call | tf_op jit(solution)/shard_map/experts_backward/pallas_call | solution.py:1286
  434.8 20.2 %collective-permute-done.22.refs_2_ = bf16[512,2048]{1,0:T(8,128)(2,1)} collective-permute-done((bf16[512,2048]{1,0:T(8,128)(2,1)S(1)}, bf16[512,2048]{1,0:T(8,128)(2,1)}, u32[]{:S(2)}, u32[]{:S(2)}) %collective-permute-start.22) | collective-permute-done | bytes 2097184 | tf_op jit(solution)/shard_map/ppermute | solution.py:1337
  459.9 36.9 %experts_forward.6 = (bf16[2,2560,2048]{2,1,0:T(8,128)(2,1)}, bf16[2,2560,1024]{2,1,0:T(8,128)(2,1)}, bf16[2,640,1024]{2,1,0:T(8,128)(2,1)}, bf16[2,640,1024]{2,...) custom-call(s32[2,2,1,512]{3,2,1,0:T(1,128)} %pad_add_fusion.2.refs_, ...), custom_call_target="tpu_custom_call", output_to_operand_aliasing={{0}: (7, {}), {1}: (8, {})} | custom-call | flops 21474836480 | bytes 41943040 | tf_op jit(solution)/shard_map/experts_forward/pallas_call | solution.py:1286
  496.8 35.9 %experts_backward.6 = (bf16[2,2560,2048]{2,1,0:T(8,128)(2,1)}, bf16[2,2560,1024]{2,1,0:T(8,128)(2,1)}, bf16[2,2560,1024]{2,1,0:T(8,128)(2,1)}, bf16[512,2048]{1,0:T(8,128)(2,1)}, bf16[512,2048]{1,0:T(8,128)(2,1)}) custom-call(s32[2,2,1,512]{3,2,1,0:T(1,128)} %pad_add_fusion.2.refs_0_, ...), custom_call_target="tpu_custom_call", output_to_operand_aliasing={{0}: (9, {}), {1}: (10, {}), {2}: (11, {})} | custom-call | tf_op jit(solution)/shard_map/experts_backward/pallas_call | solution.py:1286
  535.3 13.4 collective-permute-done.24.refs_2_
  548.8 37.6 %experts_forward.7 = (bf16[2,2560,2048]{2,1,0:T(8,128)(2,1)}, bf16[2,2560,1024]{2,1,0:T(8,128)(2,1)}, bf16[2,640,1024]{2,1,0:T(8,128)(2,1)}, bf16[2,640,1024]{2,...) custom-call(s32[2,2,1,512]{3,2,1,0:T(1,128)} %pad_add_fusion.1.refs_, ...), custom_call_target="tpu_custom_call", output_to_operand_aliasing={{0}: (7, {}), {1}: (8, {})} | custom-call | flops 21474836480 | bytes 41943040 | tf_op jit(solution)/shard_map/experts_forward/pallas_call | solution.py:1286
  598.1 36.9 %experts_forward.8 = (bf16[2,2560,2048]{2,1,0:T(8,128)(2,1)}, bf16[2,2560,1024]{2,1,0:T(8,128)(2,1)}, bf16[2,640,1024]{2,1,0:T(8,128)(2,1)}, bf16[2,640,1024]{2,...) custom-call(s32[2,2,1,512]{3,2,1,0:T(1,128)} %pad_add_fusion.refs_0_, ...), custom_call_target="tpu_custom_call", output_to_operand_aliasing={{0}: (7, {}), {1}: (8, {})} | custom-call | flops 21474836480 | bytes 41943040 | tf_op jit(solution)/shard_map/experts_forward/pallas_call | solution.py:1286
  641.5 24.3 %experts_forward.9 = (bf16[2,2560,2048]{2,1,0:T(8,128)(2,1)}, bf16[2,2560,1024]{2,1,0:T(8,128)(2,1)}, bf16[2,320,1024]{2,1,0:T(8,128)(2,1)}, bf16[2,320,1024]{2,...) custom-call(s32[1,2,1,512]{3,2,1,0:T(1,128)} %get-tuple-element.236., ...), custom_call_target="tpu_custom_call", output_to_operand_aliasing={{0}: (7, {}), {1}: (8, {})} | custom-call | flops 10737418240 | bytes 33554432 | tf_op jit(solution)/shard_map/experts_forward/pallas_call | solution.py:1286
  669.5 22.6 %experts_backward.7 = (bf16[2,2560,2048]{2,1,0:T(8,128)(2,1)}, bf16[2,2560,1024]{2,1,0:T(8,128)(2,1)}, bf16[2,2560,1024]{2,1,0:T(8,128)(2,1)}, bf16[256,2048]{1,0:T(8,128)(2,1)}, bf16[256,2048]{1,0:T(8,128)(2,1)}) custom-call(s32[1,2,1,512]{3,2,1,0:T(1,128)} %get-tuple-element.236.refs_0_, ...), custom_call_target="tpu_custom_call", output_to_operand_aliasing={{0}: (9, {}), {1}: (10, {}), {2}: (11, {})} | custom-call | flops 10737418240 | bytes 33554432 | tf_op jit(solution)/shard_map/experts_backward/pallas_call | solution.py:1286
  694.6 35.4 %experts_backward.8 = (bf16[2,2560,2048]{2,1,0:T(8,128)(2,1)}, bf16[2,2560,1024]{2,1,0:T(8,128)(2,1)}, bf16[2,2560,1024]{2,1,0:T(8,128)(2,1)}, bf16[512,2048]{1,0:T(8,128)(2,1)}, bf16[512,2048]{1,0:T(8,128)(2,1)}) custom-call(s32[2,2,1,512]{3,2,1,0:T(1,128)} %pad_add_fusion.refs_0_, ...), custom_call_target="tpu_custom_call", output_to_operand_aliasing={{0}: (9, {}), {1}: (10, {}), {2}: (11, {})} | custom-call | flops 21474836480 | bytes 41943040 | tf_op jit(solution)/shard_map/experts_backward/pallas_call | solution.py:1286
  740.0 35.3 %experts_backward.9 = (bf16[2,2560,2048]{2,1,0:T(8,128)(2,1)}, bf16[2,2560,1024]{2,1,0:T(8,128)(2,1)}, bf16[2,2560,1024]{2,1,0:T(8,128)(2,1)}, bf16[512,2048]{1,0:T(8,128)(2,1)}, bf16[512,2048]{1,0:T(8,128)(2,1)}) custom-call(s32[2,2,1,512]{3,2,1,0:T(1,128)} %pad_add_fusion.1.refs_0_, ...), custom_call_target="tpu_custom_call", output_to_operand_aliasing={{0}: (9, {}), {1}: (10, {}), {2}: (11, {})} | custom-call | flops 21474836480 | bytes 41943040 | tf_op jit(solution)/shard_map/experts_backward/pallas_call | solution.py:1286
  789.9 26.6 %convolution_convert_fusion.3 = bf16[2,2048,1024]{2,1,0:T(8,128)(2,1)} fusion(bf16[2,2560,2048]{2,1,0:T(8,128)(2,1)} %get-tuple-element.273, bf16[2,2560,1024]{2,1,0:T(8,128)(2,1)S(1)} %copy-done), kind=kOutput, calls=%fused_computation.4 | convolution fusion | flops 21479030784 | bytes 39845888 | tf_op jit(solution)/shard_map/emd,emf->edf/dot_general | solution.py:1610
  816.5 10.7 collective-permute-done.39
  843.0 26.5 %convolution_convert_fusion.2 = bf16[2,2048,1024]{2,1,0:T(8,128)(2,1)} fusion(bf16[2,2560,2048]{2,1,0:T(8,128)(2,1)} %get-tuple-element.273, bf16[2,2560,1024]{2,1,0:T(8,128)(2,1)S(1)} %bitcast.152), kind=kOutput, calls=%fused_computation.3 | convolution fusion | flops 21479030784 | bytes 39845888 | tf_op jit(solution)/shard_map/emd,emf->edf/dot_general | solution.py:1610
  878.7 9.4 mixed_grad.1
  888.1 8.8 out_grad.1
  906.5 10.1 convolution_convert_fusion
  916.5 24.7 %all-to-all-done.1 = bf16[8,512,256]{2,1,0:T(8,128)(2,1)S(1)} async-done(((bf16[8,512,256]{2,1,0:T(8,128)(2,1)}), bf16[8,512,256]{2,1,0:T(8,128)(2,1)S(1)}, u32[]{:S(2)}, u32[]{:S(2)}) %all-to-all-start.1) | async-done | bytes 2097184 | tf_op jit(solution)/shard_map/all_to_all | solution.py:1663
  948.6 45.9 %attend_backward.2 = (f32[256,4096]{1,0:T(8,128)}, f32[256,4096]{1,0:T(8,128)}, bf16[256,4096]{1,0:T(8,128)(2,1)}, f32[256,1]{1,0:T(8,128)}, f32[256,1]{1,0:T(8,128)}, /*index=5*/f32[2,4096]{1,0:T(2,128)}) custom-call(s32[3]{0:T(128)} %bitcast_subtract_fusion.starts, bf16[4096,256]{1,0:T(8,128)(2,1)} %get-tuple-element.280.query, ...), custom_call_target="tpu_custom_call" | custom-call | flops 25769803776 | bytes 20971520 | tf_op jit(solution)/shard_map/attend_backward/pallas_call | solution.py:753
  1005.0 43.7 %attend_backward.3 = (f32[256,4096]{1,0:T(8,128)}, f32[256,4096]{1,0:T(8,128)}, bf16[256,4096]{1,0:T(8,128)(2,1)}, f32[256,1]{1,0:T(8,128)}, f32[256,1]{1,0:T(8,128)}, /*index=5*/f32[2,4096]{1,0:T(2,128)}) custom-call(s32[3]{0:T(128)} %bitcast_subtract_fusion.starts, ...), custom_call_target="tpu_custom_call", output_to_operand_aliasing={{0}: (16, {}), {1}: (17, {}), {2}: (18, {}), {3}: (19, {}),... | custom-call | flops 25769803776 | bytes 20971520 | tf_op jit(solution)/shard_map/attend_backward/pallas_call | solution.py:753
  1066.0 9.5 heads_grad.1
  1082.9 19.3 %heads_product.1 = bf16[8,256,896]{2,1,0:T(8,128)(2,1)} custom-call(bf16[768,4096]{1,0:T(8,128)(2,1)} %heads_grad.1, bf16[4096,2048]{1,0:T(8,128)(2,1)} %get-tuple-element.307.hidden, f32[2048,128]{1,0:T(8,128)} %maximum_maximum_fusion.others), custom_call_target="tpu_custom_call" | custom-call | flops 12884901888 | bytes 23068672 | tf_op jit(solution)/shard_map/heads_product/pallas_call | solution.py:1089
  1109.9 41.5 %collective-permute-done.52 = bf16[512,2048]{1,0:T(8,128)(2,1)S(1)} collective-permute-done((bf16[512,2048]{1,0:T(8,128)(2,1)}, bf16[512,2048]{1,0:T(8,128)(2,1)S(1)}, u32[]{:S(2)}, u32[]{:S(2)}) %collective-permute-start.52) | collective-permute-done | bytes 2097184 | tf_op jit(solution)/shard_map/ppermute | solution.py:1383
  1166.4 29.4 %convolution_convert_fusion.1 = bf16[2,1024,2048]{2,1,0:T(8,128)(2,1)} fusion(bf16[2,2560,1024]{2,1,0:T(8,128)(2,1)} %get-tuple-element.323, bf16[2,2560,2048]{2,1,0:T(8,128)(2,1)} %get-tuple-element.324), kind=kOutput, calls=%fused_computation.2 | convolution fusion | flops 21479030784 | bytes 39845888 | tf_op jit(solution)/shard_map/emd,emf->edf/dot_general | solution.py:1610
  1195.8 11.8 collective-permute-done.55.refs_0_
  1207.5 5.9 collective-permute-done.58.refs_0_
  1213.5 6.0 hidden_term.10
  1219.8 6.5 hidden_term.12
  1228.7 38.8 %collective-permute-done.56.refs_0_ = bf16[576,2048]{1,0:T(8,128)(2,1)S(1)} collective-permute-done((bf16[576,2048]{1,0:T(8,128)(2,1)}, bf16[576,2048]{1,0:T(8,128)(2,1)S(1)}, u32[]{:S(2)}, u32[]{:S(2)}) %collective-permute-start.56) | collective-permute-done | bytes 2359328 | tf_op jit(solution)/shard_map/ppermute | solution.py:1382
  1269.0 6.0 hidden_term.11
  1274.9 6.1 hidden_term.13
  1283.1 7.0 all-to-all-start.2
  1290.1 7.7 add_bitcast_fusion
  1302.8 29.6 %collective-permute-done.57.before = bf16[576,2048]{1,0:T(8,128)(2,1)S(1)} collective-permute-done((bf16[576,2048]{1,0:T(8,128)(2,1)}, bf16[576,2048]{1,0:T(8,128)(2,1)S(1)}, u32[]{:S(2)}, u32[]{:S(2)}) %collective-permute-start.57) | collective-permute-done | bytes 2359328 | tf_op jit(solution)/shard_map/ppermute | solution.py:1382
  1332.4 8.3 collective-permute-done.60.past
  1353.2 9.2 input_grad.1
  (394 shorter events, 296.0 us)
Async XLA Ops:
  7.2 145.8 %all-gather.6.cloned.1.call-start = ((), (), s32[]{:S(2)}) async-start(), calls=%async_computation.8 | async-start | bytes 4587520 | tf_op jit(solution)/shard_map/all_gather | solution.py:1490
  42.9 159.6 %all-gather.8.cloned.1.call-start = ((), (), s32[]{:S(2)}) async-start(), calls=%async_computation.9 | async-start | bytes 10485760 | tf_op jit(solution)/shard_map/all_gather | solution.py:1491
  43.7 158.8 %all-gather.10.cloned.1.call-start = ((), (), s32[]{:S(2)}) async-start(), calls=%async_computation.10 | async-start | bytes 10485760 | tf_op jit(solution)/shard_map/all_gather | solution.py:1489
  44.4 318.8 %all-gather.12.cloned.1.call-start = ((), (), s32[]{:S(2)}) async-start(), calls=%async_computation.11 | async-start | bytes 10485760 | tf_op jit(solution)/shard_map/all_gather | solution.py:1529
  44.7 53.2 %collective-permute-start.1 = (bf16[576,2048]{1,0:T(8,128)(2,1)S(1)}, bf16[576,2048]{1,0:T(8,128)(2,1)S(1)}, u32[]{:S(2)}, u32[]{:S(2)}) collective-permute-start(bf16[576,2048]{1,0:T(8,128)(2,1)S(1)} %pad_maximum_fusion.refs_0_), channel_id=1, source_target_pairs={{0,8},{8,16},{16,24},{24,28},{28,20},{20,12},{12,4},{4,0},{1,9},{9... | collective-permute-start | bytes 7077896 | tf_op jit(solution)/shard_map/ppermute | solution.py:1337
  45.7 52.5 %collective-permute-start.4 = (bf16[576,2048]{1,0:T(8,128)(2,1)S(1)}, bf16[576,2048]{1,0:T(8,128)(2,1)S(1)}, u32[]{:S(2)}, u32[]{:S(2)}) collective-permute-start(bf16[576,2048]{1,0:T(8,128)(2,1)S(1)} %pad_maximum_fusion.refs_0_), channel_id=1, source_target_pairs={{8,0},{16,8},{24,16},{28,24},{20,28},{12,20},{4,12},{0,4},{9,1},{1... | collective-permute-start | bytes 7077896 | tf_op jit(solution)/shard_map/ppermute | solution.py:1338
  97.9 52.5 %collective-permute-start.2 = (bf16[576,2048]{1,0:T(8,128)(2,1)S(1)}, bf16[576,2048]{1,0:T(8,128)(2,1)}, u32[]{:S(2)}, u32[]{:S(2)}) collective-permute-start(bf16[576,2048]{1,0:T(8,128)(2,1)S(1)} %collective-permute-done.1.refs_1_.refs_7_), channel_id=1, source_target_pairs={{0,8},{8,16},{16,24},{24,28},{28,20},{20,12},{12,4},{4,0},{1,9},{9... | collective-permute-start | bytes 7077896 | tf_op jit(solution)/shard_map/ppermute | solution.py:1337
  98.2 52.5 %collective-permute-start.5 = (bf16[576,2048]{1,0:T(8,128)(2,1)S(1)}, bf16[576,2048]{1,0:T(8,128)(2,1)}, u32[]{:S(2)}, u32[]{:S(2)}) collective-permute-start(bf16[576,2048]{1,0:T(8,128)(2,1)S(1)} %collective-permute-done.4.refs_2_.refs_1_), channel_id=1, source_target_pairs={{8,0},{16,8},{24,16},{28,24},{20,28},{12,20},{4,12},{0,4},{9,1},{1... | collective-permute-start | bytes 7077896 | tf_op jit(solution)/shard_map/ppermute | solution.py:1338
  150.5 51.7 %collective-permute-start.3 = (bf16[576,2048]{1,0:T(8,128)(2,1)}, bf16[576,2048]{1,0:T(8,128)(2,1)S(1)}, u32[]{:S(2)}, u32[]{:S(2)}) collective-permute-start(bf16[576,2048]{1,0:T(8,128)(2,1)} %collective-permute-done.2.refs_3_.refs_6_), channel_id=1, source_target_pairs={{0,8},{8,16},{16,24},{24,28},{28,20},{20,12},{12,4},{4,0},{1,9},{9... | collective-permute-start | bytes 7077896 | tf_op jit(solution)/shard_map/ppermute | solution.py:1337
  150.7 51.8 %collective-permute-start.6 = (bf16[576,2048]{1,0:T(8,128)(2,1)}, bf16[576,2048]{1,0:T(8,128)(2,1)}, u32[]{:S(2)}, u32[]{:S(2)}) collective-permute-start(bf16[576,2048]{1,0:T(8,128)(2,1)} %collective-permute-done.5.refs_4_.refs_2_), channel_id=1, source_target_pairs={{8,0},{16,8},{24,16},{28,24},{20,28},{12,20},{4,12},{0,4},{9,1},{1... | collective-permute-start | bytes 7077896 | tf_op jit(solution)/shard_map/ppermute | solution.py:1338
  246.8 135.5 %all-gather.14.cloned.1.call-start = ((), (), s32[]{:S(2)}) async-start(), calls=%async_computation.12 | async-start | bytes 10485760 | tf_op jit(solution)/shard_map/all_gather | solution.py:1530
  262.5 52.5 %collective-permute-start.18 = (bf16[512,2048]{1,0:T(8,128)(2,1)S(1)}, bf16[512,2048]{1,0:T(8,128)(2,1)}, u32[]{:S(2)}, u32[]{:S(2)}) collective-permute-start(bf16[512,2048]{1,0:T(8,128)(2,1)S(1)} %bitcast.158), channel_id=1, source_target_pairs={{0,8},{8,16},{16,24},{24,28},{28,20},{20,12},{12,4},{4,0},{1,9},{9... | collective-permute-start | bytes 6291464 | tf_op jit(solution)/shard_map/ppermute | solution.py:1337
  263.0 51.9 %collective-permute-start.19 = (bf16[512,2048]{1,0:T(8,128)(2,1)S(1)}, bf16[512,2048]{1,0:T(8,128)(2,1)}, u32[]{:S(2)}, u32[]{:S(2)}) collective-permute-start(bf16[512,2048]{1,0:T(8,128)(2,1)S(1)} %bitcast.159), channel_id=1, source_target_pairs={{8,0},{16,8},{24,16},{28,24},{20,28},{12,20},{4,12},{0,4},{9,1},{1... | collective-permute-start | bytes 6291464 | tf_op jit(solution)/shard_map/ppermute | solution.py:1338
  315.0 48.2 %all-to-all-start = ((bf16[8,512,256]{2,1,0:T(8,128)(2,1)}), bf16[8,512,256]{2,1,0:T(8,128)(2,1)}, u32[]{:S(2)}, u32[]{:S(2)}) async-start(bf16[8,512,256]{2,1,0:T(8,128)(2,1)} %bitcast.170), calls=%async_computation | async-start | bytes 4194304 | tf_op jit(solution)/shard_map/all_to_all | solution.py:1542
  323.6 88.5 %collective-permute-start.20 = (bf16[512,2048]{1,0:T(8,128)(2,1)}, bf16[512,2048]{1,0:T(8,128)(2,1)}, u32[]{:S(2)}, u32[]{:S(2)}) collective-permute-start(bf16[512,2048]{1,0:T(8,128)(2,1)} %collective-permute-done.18.refs_2_), channel_id=1, source_target_pairs={{0,8},{8,16},{16,24},{24,28},{28,20},{20,12},{12,4},{4,0},{1,9},{9... | collective-permute-start | bytes 6291464 | tf_op jit(solution)/shard_map/ppermute | solution.py:1337
  324.2 87.9 %collective-permute-start.21 = (bf16[512,2048]{1,0:T(8,128)(2,1)}, bf16[512,2048]{1,0:T(8,128)(2,1)}, u32[]{:S(2)}, u32[]{:S(2)}) collective-permute-start(bf16[512,2048]{1,0:T(8,128)(2,1)} %collective-permute-done.19.refs_3_), channel_id=1, source_target_pairs={{8,0},{16,8},{24,16},{28,24},{20,28},{12,20},{4,12},{0,4},{9,1},{1... | collective-permute-start | bytes 6291464 | tf_op jit(solution)/shard_map/ppermute | solution.py:1338
  373.0 81.9 %collective-permute-start.22 = (bf16[512,2048]{1,0:T(8,128)(2,1)S(1)}, bf16[512,2048]{1,0:T(8,128)(2,1)}, u32[]{:S(2)}, u32[]{:S(2)}) collective-permute-start(bf16[512,2048]{1,0:T(8,128)(2,1)S(1)} %multiply_convert_fusion.refs_2_), channel_id=1, source_target_pairs={{0,8},{8,16},{16,24},{24,28},{28,20},{20,12},{12,4},{4,0},{1,9},{9... | collective-permute-start | bytes 6291464 | tf_op jit(solution)/shard_map/ppermute | solution.py:1337
  378.4 76.6 %collective-permute-start.23 = (bf16[512,2048]{1,0:T(8,128)(2,1)S(1)}, bf16[512,2048]{1,0:T(8,128)(2,1)}, u32[]{:S(2)}, u32[]{:S(2)}) collective-permute-start(bf16[512,2048]{1,0:T(8,128)(2,1)S(1)} %multiply_convert_fusion.refs_2_), channel_id=1, source_target_pairs={{8,0},{16,8},{24,16},{28,24},{20,28},{12,20},{4,12},{0,4},{9,1},{1... | collective-permute-start | bytes 6291464 | tf_op jit(solution)/shard_map/ppermute | solution.py:1338
  455.0 77.6 %collective-permute-start.26 = (bf16[512,2048]{1,0:T(8,128)(2,1)}, bf16[512,2048]{1,0:T(8,128)(2,1)}, u32[]{:S(2)}, u32[]{:S(2)}) collective-permute-start(bf16[512,2048]{1,0:T(8,128)(2,1)} %collective-permute-done.22.refs_2_), channel_id=1, source_target_pairs={{0,8},{8,16},{16,24},{24,28},{28,20},{20,12},{12,4},{4,0},{1,9},{9... | collective-permute-start | bytes 6291464 | tf_op jit(solution)/shard_map/ppermute | solution.py:1337
  455.0 77.7 %collective-permute-start.27 = (bf16[512,2048]{1,0:T(8,128)(2,1)}, bf16[512,2048]{1,0:T(8,128)(2,1)}, u32[]{:S(2)}, u32[]{:S(2)}) collective-permute-start(bf16[512,2048]{1,0:T(8,128)(2,1)} %collective-permute-done.23.refs_3_), channel_id=1, source_target_pairs={{8,0},{16,8},{24,16},{28,24},{20,28},{12,20},{4,12},{0,4},{9,1},{1... | collective-permute-start | bytes 6291464 | tf_op jit(solution)/shard_map/ppermute | solution.py:1338
  457.6 91.1 %collective-permute-start.24 = (bf16[512,2048]{1,0:T(8,128)(2,1)}, bf16[512,2048]{1,0:T(8,128)(2,1)S(1)}, u32[]{:S(2)}, u32[]{:S(2)}) collective-permute-start(bf16[512,2048]{1,0:T(8,128)(2,1)} %collective-permute-done.20.refs_2_), channel_id=1, source_target_pairs={{0,8},{8,16},{16,24},{24,28},{28,20},{20,12},{12,4},{4,0},{1,9},{9... | collective-permute-start | bytes 6291464 | tf_op jit(solution)/shard_map/ppermute | solution.py:1337
  457.6 91.2 %collective-permute-start.25 = (bf16[512,2048]{1,0:T(8,128)(2,1)}, bf16[512,2048]{1,0:T(8,128)(2,1)}, u32[]{:S(2)}, u32[]{:S(2)}) collective-permute-start(bf16[512,2048]{1,0:T(8,128)(2,1)} %collective-permute-done.21.refs_3_), channel_id=1, source_target_pairs={{8,0},{16,8},{24,16},{28,24},{20,28},{12,20},{4,12},{0,4},{9,1},{1... | collective-permute-start | bytes 6291464 | tf_op jit(solution)/shard_map/ppermute | solution.py:1338
  532.7 58.8 %collective-permute-start.28 = (bf16[512,2048]{1,0:T(8,128)(2,1)}, bf16[512,2048]{1,0:T(8,128)(2,1)}, u32[]{:S(2)}, u32[]{:S(2)}) collective-permute-start(bf16[512,2048]{1,0:T(8,128)(2,1)} %collective-permute-done.26.refs_2_), channel_id=1, source_target_pairs={{0,8},{8,16},{16,24},{24,28},{28,20},{20,12},{12,4},{4,0},{1,9},{9... | collective-permute-start | bytes 6291464 | tf_op jit(solution)/shard_map/ppermute | solution.py:1337
  532.7 58.8 %collective-permute-start.29 = (bf16[512,2048]{1,0:T(8,128)(2,1)}, bf16[512,2048]{1,0:T(8,128)(2,1)}, u32[]{:S(2)}, u32[]{:S(2)}) collective-permute-start(bf16[512,2048]{1,0:T(8,128)(2,1)} %collective-permute-done.27.refs_3_), channel_id=1, source_target_pairs={{8,0},{16,8},{24,16},{28,24},{20,28},{12,20},{4,12},{0,4},{9,1},{1... | collective-permute-start | bytes 6291464 | tf_op jit(solution)/shard_map/ppermute | solution.py:1338
  593.8 46.7 %collective-permute-start.30 = (bf16[256,2048]{1,0:T(8,128)(2,1)}, bf16[256,2048]{1,0:T(8,128)(2,1)S(1)}, u32[]{:S(2)}, u32[]{:S(2)}) collective-permute-start(bf16[256,2048]{1,0:T(8,128)(2,1)} %slice.260), channel_id=1, source_target_pairs={{0,8},{8,16},{16,24},{24,28},{28,20},{20,12},{12,4},{4,0},{1,9},{9... | collective-permute-start | bytes 3145736 | tf_op jit(solution)/shard_map/ppermute | solution.py:1343
  596.1 44.4 %collective-permute-start.31 = (bf16[256,2048]{1,0:T(8,128)(2,1)}, bf16[256,2048]{1,0:T(8,128)(2,1)}, u32[]{:S(2)}, u32[]{:S(2)}) collective-permute-start(bf16[256,2048]{1,0:T(8,128)(2,1)} %slice.261), channel_id=1, source_target_pairs={{8,0},{16,8},{24,16},{28,24},{20,28},{12,20},{4,12},{0,4},{9,1},{1... | collective-permute-start | bytes 3145736 | tf_op jit(solution)/shard_map/ppermute | solution.py:1344
  734.6 44.7 %collective-permute-start.37 = (bf16[512,2048]{1,0:T(8,128)(2,1)}, bf16[512,2048]{1,0:T(8,128)(2,1)S(1)}, u32[]{:S(2)}, u32[]{:S(2)}) collective-permute-start(bf16[512,2048]{1,0:T(8,128)(2,1)} %pad_maximum_fusion.2), channel_id=1, source_target_pairs={{8,0},{16,8},{24,16},{28,24},{20,28},{12,20},{4,12},{0,4},{9,1},{1... | collective-permute-start | bytes 6291464 | tf_op jit(solution)/shard_map/ppermute | solution.py:1382
  739.5 45.5 %collective-permute-start.40 = (bf16[512,2048]{1,0:T(8,128)(2,1)}, bf16[512,2048]{1,0:T(8,128)(2,1)}, u32[]{:S(2)}, u32[]{:S(2)}) collective-permute-start(bf16[512,2048]{1,0:T(8,128)(2,1)} %pad_maximum_fusion.3), channel_id=1, source_target_pairs={{0,8},{8,16},{16,24},{24,28},{28,20},{20,12},{12,4},{4,0},{1,9},{9... | collective-permute-start | bytes 6291464 | tf_op jit(solution)/shard_map/ppermute | solution.py:1383
  783.3 44.0 %collective-permute-start.39 = (bf16[512,2048]{1,0:T(8,128)(2,1)}, bf16[512,2048]{1,0:T(8,128)(2,1)}, u32[]{:S(2)}, u32[]{:S(2)}) collective-permute-start(bf16[512,2048]{1,0:T(8,128)(2,1)} %add_convert_fusion.7), channel_id=1, source_target_pairs={{8,0},{16,8},{24,16},{28,24},{20,28},{12,20},{4,12},{0,4},{9,1},{1... | collective-permute-start | bytes 6291464 | tf_op jit(solution)/shard_map/ppermute | solution.py:1382
  789.4 43.9 %collective-permute-start.41 = (bf16[512,2048]{1,0:T(8,128)(2,1)}, bf16[512,2048]{1,0:T(8,128)(2,1)}, u32[]{:S(2)}, u32[]{:S(2)}) collective-permute-start(bf16[512,2048]{1,0:T(8,128)(2,1)} %add_convert_fusion.6), channel_id=1, source_target_pairs={{0,8},{8,16},{16,24},{24,28},{28,20},{20,12},{12,4},{4,0},{1,9},{9... | collective-permute-start | bytes 6291464 | tf_op jit(solution)/shard_map/ppermute | solution.py:1383
  896.9 44.3 %all-to-all-start.1 = ((bf16[8,512,256]{2,1,0:T(8,128)(2,1)}), bf16[8,512,256]{2,1,0:T(8,128)(2,1)S(1)}, u32[]{:S(2)}, u32[]{:S(2)}) async-start(bf16[8,512,256]{2,1,0:T(8,128)(2,1)} %out_grad.1), calls=%async_computation.1 | async-start | bytes 4194304 | tf_op jit(solution)/shard_map/all_to_all | solution.py:1663
  902.0 173.4 %reduce-scatter.6.cloned.1.call-start = ((), (), s32[]{:S(2)}) async-start(), calls=%async_computation.13 | async-start | bytes 10485760 | tf_op jit(solution)/shard_map/reduce_scatter | solution.py:1656
  942.5 271.0 %reduce-scatter.12.cloned.1.call-start = ((), (), s32[]{:S(2)}) async-start(), calls=%async_computation.16 | async-start | bytes 10485760 | tf_op jit(solution)/shard_map/reduce_scatter | solution.py:1656
  943.3 285.5 %reduce-scatter.10.cloned.1.call-start = ((), (), s32[]{:S(2)}) async-start(), calls=%async_computation.15 | async-start | bytes 10485760 | tf_op jit(solution)/shard_map/reduce_scatter | solution.py:1656
  944.0 339.1 %reduce-scatter.8.cloned.1.call-start = ((), (), s32[]{:S(2)}) async-start(), calls=%async_computation.14 | async-start | bytes 4587520 | tf_op jit(solution)/shard_map/reduce_scatter | solution.py:1656
  945.2 49.3 %collective-permute-start.44 = (bf16[512,2048]{1,0:T(8,128)(2,1)}, bf16[512,2048]{1,0:T(8,128)(2,1)}, u32[]{:S(2)}, u32[]{:S(2)}) collective-permute-start(bf16[512,2048]{1,0:T(8,128)(2,1)} %pad_maximum_fusion.4), channel_id=1, source_target_pairs={{8,0},{16,8},{24,16},{28,24},{20,28},{12,20},{4,12},{0,4},{9,1},{1... | collective-permute-start | bytes 6291464 | tf_op jit(solution)/shard_map/ppermute | solution.py:1382
  946.7 51.7 %collective-permute-start.45 = (bf16[512,2048]{1,0:T(8,128)(2,1)}, bf16[512,2048]{1,0:T(8,128)(2,1)}, u32[]{:S(2)}, u32[]{:S(2)}) collective-permute-start(bf16[512,2048]{1,0:T(8,128)(2,1)} %pad_maximum_fusion.5), channel_id=1, source_target_pairs={{0,8},{8,16},{16,24},{24,28},{28,20},{20,12},{12,4},{4,0},{1,9},{9... | collective-permute-start | bytes 6291464 | tf_op jit(solution)/shard_map/ppermute | solution.py:1383
  1002.2 48.4 %collective-permute-start.46 = (bf16[512,2048]{1,0:T(8,128)(2,1)}, bf16[512,2048]{1,0:T(8,128)(2,1)}, u32[]{:S(2)}, u32[]{:S(2)}) collective-permute-start(bf16[512,2048]{1,0:T(8,128)(2,1)} %add_convert_fusion.3), channel_id=1, source_target_pairs={{8,0},{16,8},{24,16},{28,24},{20,28},{12,20},{4,12},{0,4},{9,1},{1... | collective-permute-start | bytes 6291464 | tf_op jit(solution)/shard_map/ppermute | solution.py:1382
  1002.7 47.9 %collective-permute-start.47 = (bf16[512,2048]{1,0:T(8,128)(2,1)}, bf16[512,2048]{1,0:T(8,128)(2,1)S(1)}, u32[]{:S(2)}, u32[]{:S(2)}) collective-permute-start(bf16[512,2048]{1,0:T(8,128)(2,1)} %add_convert_fusion.2), channel_id=1, source_target_pairs={{0,8},{8,16},{16,24},{24,28},{28,20},{20,12},{12,4},{4,0},{1,9},{9... | collective-permute-start | bytes 6291464 | tf_op jit(solution)/shard_map/ppermute | solution.py:1383
  1107.7 255.8 %reduce-scatter.14.cloned.1.call-start = ((), (), s32[]{:S(2)}) async-start(), calls=%async_computation.17 | async-start | bytes 10485760 | tf_op jit(solution)/shard_map/reduce_scatter | solution.py:1656
  1108.1 44.4 %collective-permute-start.51 = (bf16[512,2048]{1,0:T(8,128)(2,1)}, bf16[512,2048]{1,0:T(8,128)(2,1)}, u32[]{:S(2)}, u32[]{:S(2)}) collective-permute-start(bf16[512,2048]{1,0:T(8,128)(2,1)} %add_convert_fusion.1), channel_id=1, source_target_pairs={{8,0},{16,8},{24,16},{28,24},{20,28},{12,20},{4,12},{0,4},{9,1},{1... | collective-permute-start | bytes 6291464 | tf_op jit(solution)/shard_map/ppermute | solution.py:1382
  1158.4 49.1 %collective-permute-start.55 = (bf16[576,2048]{1,0:T(8,128)(2,1)}, bf16[576,2048]{1,0:T(8,128)(2,1)S(1)}, u32[]{:S(2)}, u32[]{:S(2)}) collective-permute-start(bf16[576,2048]{1,0:T(8,128)(2,1)} %hidden_term.8), channel_id=1, source_target_pairs={{8,0},{16,8},{24,16},{28,24},{20,28},{12,20},{4,12},{0,4},{9,1},{1... | collective-permute-start | bytes 7077896 | tf_op jit(solution)/shard_map/ppermute | solution.py:1382
  1164.6 48.8 %collective-permute-start.58 = (bf16[576,2048]{1,0:T(8,128)(2,1)}, bf16[576,2048]{1,0:T(8,128)(2,1)}, u32[]{:S(2)}, u32[]{:S(2)}) collective-permute-start(bf16[576,2048]{1,0:T(8,128)(2,1)} %hidden_term.9), channel_id=1, source_target_pairs={{0,8},{8,16},{16,24},{24,28},{28,20},{20,12},{12,4},{4,0},{1,9},{9... | collective-permute-start | bytes 7077896 | tf_op jit(solution)/shard_map/ppermute | solution.py:1383
  1219.5 48.1 %collective-permute-start.56 = (bf16[576,2048]{1,0:T(8,128)(2,1)}, bf16[576,2048]{1,0:T(8,128)(2,1)S(1)}, u32[]{:S(2)}, u32[]{:S(2)}) collective-permute-start(bf16[576,2048]{1,0:T(8,128)(2,1)} %hidden_term.10), channel_id=1, source_target_pairs={{8,0},{16,8},{24,16},{28,24},{20,28},{12,20},{4,12},{0,4},{9,1},{1... | collective-permute-start | bytes 7077896 | tf_op jit(solution)/shard_map/ppermute | solution.py:1382
  1226.3 48.7 %collective-permute-start.59 = (bf16[576,2048]{1,0:T(8,128)(2,1)}, bf16[576,2048]{1,0:T(8,128)(2,1)}, u32[]{:S(2)}, u32[]{:S(2)}) collective-permute-start(bf16[576,2048]{1,0:T(8,128)(2,1)} %hidden_term.12), channel_id=1, source_target_pairs={{0,8},{8,16},{16,24},{24,28},{28,20},{20,12},{12,4},{4,0},{1,9},{9... | collective-permute-start | bytes 7077896 | tf_op jit(solution)/shard_map/ppermute | solution.py:1383
  1274.9 57.4 %collective-permute-start.57 = (bf16[576,2048]{1,0:T(8,128)(2,1)}, bf16[576,2048]{1,0:T(8,128)(2,1)S(1)}, u32[]{:S(2)}, u32[]{:S(2)}) collective-permute-start(bf16[576,2048]{1,0:T(8,128)(2,1)} %hidden_term.11), channel_id=1, source_target_pairs={{8,0},{16,8},{24,16},{28,24},{20,28},{12,20},{4,12},{0,4},{9,1},{1... | collective-permute-start | bytes 7077896 | tf_op jit(solution)/shard_map/ppermute | solution.py:1382
  1281.0 59.6 %collective-permute-start.60 = (bf16[576,2048]{1,0:T(8,128)(2,1)}, bf16[576,2048]{1,0:T(8,128)(2,1)}, u32[]{:S(2)}, u32[]{:S(2)}) collective-permute-start(bf16[576,2048]{1,0:T(8,128)(2,1)} %hidden_term.13), channel_id=1, source_target_pairs={{0,8},{8,16},{16,24},{24,28},{28,20},{20,12},{12,4},{4,0},{1,9},{9... | collective-permute-start | bytes 7077896 | tf_op jit(solution)/shard_map/ppermute | solution.py:1383
  1283.1 62.3 %all-to-all-start.2 = ((bf16[8,64,896]{2,1,0:T(8,128)(2,1)}), bf16[8,64,896]{2,1,0:T(8,128)(2,1)S(1)}, u32[]{:S(2)}, u32[]{:S(2)}) async-start(bf16[8,64,896]{2,1,0:T(8,128)(2,1)} %reduce-scatter.8.cloned.1.call-done), calls=%async_computation.4 | async-start | bytes 1835008 | tf_op jit(solution)/shard_map/all_to_all | solution.py:1735
  (88 other events, 1605.9 us)
Sparse Core Ops, SparseCore 0:
  43.1 31.5 all-gather.5
  76.2 58.2 all-gather.7
  136.1 58.2 all-gather.9
  246.9 57.9 all-gather.11
  306.3 58.2 all-gather.13
  941.3 72.5 reduce-scatter.5
  1016.7 71.7 reduce-scatter.11
  1091.1 71.7 reduce-scatter.9
  1166.1 41.2 reduce-scatter.7
  1213.5 70.8 reduce-scatter.13
